TPU v7x, 512 devices: a whole 4x8x8 slice. The times are simulated.
512 devices in a mesh: leaf: 8 (over x, core), col: 64 (over z, y).
Axes of the slice: x: 4, y: 8, z: 8, core: 2. Of those that a mesh axis runs over, the one named last changes fastest.
Arguments:
- child_panels: bfloat16 [8, 8192, 2048], P('leaf', 'col'), may hold values from -6 to 6
- child_links: bfloat16 [8, 512, 2048], P('leaf', 'col'), may hold values from -6 to 6
- child_pivots: bfloat16 [8, 1024, 1024], P('leaf', 'col'), may hold values from -6 to 6
- child_inverse: bfloat16 [8, 2, 1024, 1024], P('leaf', None, 'col'), as said below
- block_mask: int32 [8, 64, 2], P('leaf', 'col'), may hold values from 0 to 1, as said below
- row_map: int32 [8, 8192], P('leaf', 'col'), may hold values from 0 to 255, as said below
- parent_panels: bfloat16 [8, 8192, 2048], P('leaf', 'col'), may hold values from -6 to 6
- parent_pivots: bfloat16 [4, 1024, 1024], P(None, 'col'), may hold values from -6 to 6
- parent_inverse: bfloat16 [4, 2, 1024, 1024], P(None, None, 'col'), as said below
Outputs:
- child_factor: bfloat16 [8, 8192, 2048], P('leaf', 'col')
- parent_factor: bfloat16 [8, 8192, 2048], P('leaf', 'col')
Inputs may be any that keep to these rules, and one draw needn't show every extreme that they name: block_mask[f, b, 1] >= block_mask[f, b, 0]: a row block present in a front's first panel is present in its second. `row_map`: within each block of 128 consecutive rows of one front the values are distinct. Each child_inverse[f, k] is lower triangular. Each parent_inverse[p, k] is lower triangular.
All inputs are finite; a program needn't handle non-finite values.
Results may differ from a plain program's by a relative error of at most 0.011.
Values may be sent and summed in bfloat16 or wider, within the bound.
No kernel may reach another device: no remote copies, remote signals or barrier semaphores. Data moves between devices by JAX's collectives and lax.ppermute only.
A program may use at most 64 MiB of HBM per device.

v0:
```python
import jax
import jax.numpy as jnp
from jax import lax
from jax.sharding import PartitionSpec as P


def partner(value, axis, stride):
    return lax.ppermute(value, axis, [(i, i ^ 1 << stride) for i in range(lax.axis_size(axis))])


def times_rows(left_rows, segment):
    return lax.dot_general(
        left_rows, segment, (((1,), (1,)), ((), ())), preferred_element_type=jnp.float32
    )


def masked_products(body_rows, segment):
    return times_rows(body_rows, segment)


def all_products(body_rows, extra_rows, segment):
    main_part = masked_products(body_rows, segment)
    if extra_rows is None:
        return main_part
    return jnp.concatenate([main_part, times_rows(extra_rows, segment)], 0)


def apply_inverse(body_rows, extra_rows, inverse_shard):

    def apply_segment(segment, offset):
        return all_products(body_rows, extra_rows, segment)

    return apply_segment(lax.all_gather(inverse_shard, "col", axis=0, tiled=True), jnp.int32(0))


def apply_factor(body_rows, extra_rows, factor_shard):

    def apply_segment(segment, offset):
        return all_products(body_rows, extra_rows, segment)

    return apply_segment(lax.all_gather(factor_shard, "col", axis=0, tiled=True), jnp.int32(0))


def local(
    child_panels,
    child_links,
    child_pivots,
    child_inverse,
    block_mask,
    row_map,
    parent_panels,
    parent_pivots,
    parent_inverse,
):
    panel_width = child_pivots.shape[2]
    local_rows = child_panels.shape[1]
    row_flags = block_mask[0]
    first_flags = row_flags[:, 0]
    second_flags = row_flags[:, 1]
    keep_first = jnp.repeat(first_flags, 128)[:, None].astype(jnp.bfloat16)
    keep_second = jnp.repeat(second_flags, 128)[:, None].astype(jnp.bfloat16)
    first_input = child_panels[0, :, :panel_width] * keep_first
    second_input = child_panels[0, :, panel_width:] * keep_second
    link_rows = child_links[0]
    pivot_rows = child_pivots[0]
    link_count = link_rows.shape[0]
    extra_first = jnp.concatenate([link_rows[:, :panel_width], pivot_rows], 0)
    first_all = apply_inverse(first_input, extra_first, child_inverse[0, 0]).astype(jnp.bfloat16)
    child_first = first_all[:local_rows]
    link_first = first_all[local_rows : local_rows + link_count]
    pivot_first = first_all[local_rows + link_count :]
    update_terms = apply_factor(child_first, link_first, pivot_first)
    second_source = jnp.concatenate([second_input, link_rows[:, panel_width:]], 0)
    second_rhs = (second_source.astype(jnp.float32) - update_terms).astype(jnp.bfloat16)
    second_all = apply_inverse(
        second_rhs[:local_rows], second_rhs[local_rows:], child_inverse[0, 1]
    ).astype(jnp.bfloat16)
    child_second = second_all[:local_rows]
    link_second = second_all[local_rows:]
    child_factor = jnp.concatenate([child_first, child_second], 1)
    link_factor = jnp.concatenate([link_first, link_second], 1)
    contribution = -apply_factor(child_factor, None, link_factor)
    sibling_bit = lax.axis_index("leaf") % 2
    target_rows = row_map[0]
    placed = (
        jnp.zeros((2 * local_rows, contribution.shape[1]), jnp.float32)
        .at[target_rows]
        .add(contribution)
    )
    own_part = lax.dynamic_slice_in_dim(placed, sibling_bit * local_rows, local_rows, 0)
    sent_part = lax.dynamic_slice_in_dim(placed, (1 - sibling_bit) * local_rows, local_rows, 0)
    received = partner(sent_part, "leaf", 0)
    extension = jnp.where(
        sibling_bit == 0,
        jnp.concatenate([own_part, received], 1),
        jnp.concatenate([received, own_part], 1),
    )
    parent_index = lax.axis_index("leaf") // 2
    parent_pivot_rows = lax.dynamic_index_in_dim(parent_pivots, parent_index, 0, keepdims=False)
    parent_inverses = lax.dynamic_index_in_dim(parent_inverse, parent_index, 0, keepdims=False)
    parent_input = (parent_panels[0, :, :panel_width].astype(jnp.float32) + extension).astype(
        jnp.bfloat16
    )
    parent_all = apply_inverse(parent_input, parent_pivot_rows, parent_inverses[0]).astype(
        jnp.bfloat16
    )
    parent_first = parent_all[:local_rows]
    parent_pivot_first = parent_all[local_rows:]
    parent_update = apply_factor(parent_first, None, parent_pivot_first)
    parent_rhs = (parent_panels[0, :, panel_width:].astype(jnp.float32) - parent_update).astype(
        jnp.bfloat16
    )
    parent_second = apply_inverse(parent_rhs, None, parent_inverses[1]).astype(jnp.bfloat16)
    parent_factor = jnp.concatenate([parent_first, parent_second], 1)
    return (child_factor[None], parent_factor[None])


def solution(mesh):
    return jax.shard_map(
        local,
        mesh=mesh,
        in_specs=(
            P("leaf", "col", None),
            P("leaf", "col", None),
            P("leaf", "col", None),
            P("leaf", None, "col", None),
            P("leaf", "col", None),
            P("leaf", "col"),
            P("leaf", "col", None),
            P(None, "col", None),
            P(None, None, "col", None),
        ),
        out_specs=(P("leaf", "col", None), P("leaf", "col", None)),
        check_vma=False,
    )
```

profile of v0, /device:TPU:1, one launch (start us, length us, event | category | flops | bytes accessed | tf_op | source)
XLA Modules:
  0.0 610.9 jit_solution(18251603384100737075)
XLA Ops:
  7.2 0.0 copy-start
  7.2 0.0 copy-start.7
  7.2 0.0 copy-start.4
  7.2 0.0 all-gather.18.cloned.1.call-start
  7.2 1.5 fusion.71
  8.7 0.0 all-gather.18.cloned.1.call-update
  8.7 0.0 all-gather.12.cloned.1.call-start
  8.8 0.7 fusion.72
  9.5 87.5 %all-gather.18.cloned.1.call-done = bf16[1,1,1024,1024]{3,2,1,0:T(8,128)(2,1)} async-done(((bf16[1,1,16,1024]{3,2,1,0:T(8,128)(2,1)}), bf16[1,1,1024,1024]{3,2,1,0:T(8,128)(2,1)}) %all-gather.18.cloned.1.call-update) | async-done | bytes 2097168 | tf_op jit(solution)/shard_map/all_gather | solution.py:33
  97.0 0.0 copy-start.2
  97.0 2.4 fusion.27
  99.4 0.0 copy-start.5
  99.4 0.6 slice.92
  100.0 0.0 all-gather.12.cloned.1.call-update
  100.1 0.0 all-gather.20.cloned.1.call-start
  100.1 0.7 all-gather.20.cloned.1.call-update
  100.8 0.0 all-gather.22.cloned.1.call-start
  100.9 1.4 constant_dynamic-slice_fusion
  102.3 0.0 all-gather.22.cloned.1.call-update
  102.3 0.0 all-gather.14.cloned.1.call-start
  102.4 0.0 copy-done.7
  102.4 0.6 fusion.73
  103.0 0.0 copy-done.4
  103.0 0.7 multiply_bitcast_fusion
  103.6 0.0 copy-done.2
  103.7 1.4 fusion.14
  105.0 75.7 %all-gather.12.cloned.1.call-done = bf16[1024,1024]{1,0:T(8,128)(2,1)} async-done(((bf16[16,1024]{1,0:T(8,128)(2,1)}), bf16[1024,1024]{1,0:T(8,128)(2,1)}) %all-gather.12.cloned.1.call-update) | async-done | bytes 2097168 | tf_op jit(solution)/shard_map/all_gather | solution.py:41
  180.7 0.0 copy-start.3
  180.7 2.4 fusion.69
  183.1 0.0 copy-done.5
  183.1 0.0 copy-done.3
  183.1 0.9 fusion.74
  184.0 0.0 slice-start
  184.0 80.9 %all-gather.20.cloned.1.call-done = bf16[1,1,1024,1024]{3,2,1,0:T(8,128)(2,1)} async-done(((bf16[1,1,16,1024]{3,2,1,0:T(8,128)(2,1)}), bf16[1,1,1024,1024]{3,2,1,0:T(8,128)(2,1)}) %all-gather.20.cloned.1.call-update) | async-done | bytes 2097168 | tf_op jit(solution)/shard_map/all_gather | solution.py:33
  264.9 0.0 copy-start.8
  264.9 2.2 fusion.33
  267.2 0.0 slice-done
  267.2 0.0 copy-start.1
  267.2 0.6 pad_maximum_fusion.2
  267.8 0.0 all-gather.14.cloned.1.call-update
  267.8 0.0 all-gather.24.cloned.1.call-start
  267.9 0.5 all-gather.24.cloned.1.call-update
  268.4 0.0 all-gather.16.cloned.1.call-start
  268.4 79.9 %all-gather.22.cloned.1.call-done = bf16[1,1,1024,1024]{3,2,1,0:T(8,128)(2,1)} async-done(((bf16[1,1,16,1024]{3,2,1,0:T(8,128)(2,1)}), bf16[1,1,1024,1024]{3,2,1,0:T(8,128)(2,1)}) %all-gather.22.cloned.1.call-update) | async-done | bytes 2097168 | tf_op jit(solution)/shard_map/all_gather | solution.py:33
  348.4 0.0 copy-done
  348.4 2.9 fusion.30
  351.2 0.0 all-gather.16.cloned.1.call-update
  351.3 0.0 copy-done.8
  351.3 0.1 fusion.36
  351.4 0.0 copy-done.1
  351.4 0.8 fusion.17
  352.2 0.0 copy-start.6
  352.2 80.2 %all-gather.14.cloned.1.call-done = bf16[512,2048]{1,0:T(8,128)(2,1)} async-done(((bf16[8,2048]{1,0:T(8,128)(2,1)}), bf16[512,2048]{1,0:T(8,128)(2,1)}) %all-gather.14.cloned.1.call-update) | async-done | bytes 2097168 | tf_op jit(solution)/shard_map/all_gather | solution.py:41
  432.4 2.4 convolution_negate_fusion
  434.8 1.5 scatter_custom_fusion
  436.4 6.5 %collective-permute-start = (f32[128,512]{1,0:T(8,128)S(1)}, f32[128,512]{1,0:T(8,128)S(1)}, u32[]{:S(2)}, u32[]{:S(2)}) collective-permute-start(f32[128,512]{1,0:T(8,128)S(1)} %get-tuple-element.3), channel_id=1, source_target_pairs={{0,64},{64,0},{128,192},{192,128},{256,320},{320,256},{384,448},{4... | collective-permute-start | bytes 786440 | tf_op jit(solution)/shard_map/ppermute | solution.py:8
  442.9 0.8 fusion.40
  443.7 0.3 collective-permute-done
  444.0 0.0 copy-done.6
  444.0 2.4 fusion.20
  446.5 69.4 %all-gather.24.cloned.1.call-done = bf16[1,1,1024,1024]{3,2,1,0:T(8,128)(2,1)} async-done(((bf16[1,1,16,1024]{3,2,1,0:T(8,128)(2,1)}), bf16[1,1,1024,1024]{3,2,1,0:T(8,128)(2,1)}) %all-gather.24.cloned.1.call-update) | async-done | bytes 2097168 | tf_op jit(solution)/shard_map/all_gather | solution.py:33
  515.9 83.6 %all-gather.16.cloned.1.call-done = bf16[1024,1024]{1,0:T(8,128)(2,1)} async-done(((bf16[16,1024]{1,0:T(8,128)(2,1)}), bf16[1024,1024]{1,0:T(8,128)(2,1)}) %all-gather.16.cloned.1.call-update) | async-done | bytes 2097168 | tf_op jit(solution)/shard_map/all_gather | solution.py:41
  599.5 3.7 fusion.23
  603.2 0.8 maximum_bitcast_fusion
  (3 shorter events, 0.1 us)
Async XLA Ops:
  7.2 341.2 %copy-start = (bf16[4,16,1024]{2,1,0:T(8,128)(2,1)S(1)}, bf16[4,16,1024]{2,1,0:T(8,128)(2,1)}, u32[]{:S(2)}) copy-start(bf16[4,16,1024]{2,1,0:T(8,128)(2,1)} %param.16) | copy-start | bytes 393220
  7.2 95.2 %copy-start.7 = (s32[1,1,2]{2,1,0:T(1,128)S(1)}, s32[1,1,2]{2,1,0:T(1,128)}, u32[]{:S(2)}) copy-start(s32[1,1,2]{2,1,0:T(1,128)} %param.13) | copy-start | bytes 28
  7.2 95.8 %copy-start.4 = (bf16[1,128,2048]{2,1,0:T(8,128)(2,1)S(1)}, bf16[1,128,2048]{2,1,0:T(8,128)(2,1)}, u32[]{:S(2)}) copy-start(bf16[1,128,2048]{2,1,0:T(8,128)(2,1)} %param.9) | copy-start | bytes 1572868
  7.2 89.8 %all-gather.18.cloned.1.call-start = ((), (), s32[]{:S(2)}) async-start(), calls=%async_computation.3 | async-start | bytes 2129920 | tf_op jit(solution)/shard_map/all_gather | solution.py:33
  8.7 172.0 %all-gather.12.cloned.1.call-start = ((), (), s32[]{:S(2)}) async-start(), calls=%async_computation | async-start | bytes 2129920 | tf_op jit(solution)/shard_map/all_gather | solution.py:41
  97.0 6.7 %copy-start.2 = (bf16[1,1,1024,1024]{3,2,1,0:T(8,128)(2,1)S(1)}, bf16[1,1,1024,1024]{3,2,1,0:T(8,128)(2,1)}, u32[]{:S(2)}) copy-start(bf16[1,1,1024,1024]{3,2,1,0:T(8,128)(2,1)} %all-gather.18.cloned.1.call-done) | copy-start | bytes 6291460
  99.4 83.7 %copy-start.5 = (bf16[24,1024]{1,0:T(8,128)(2,1)}, bf16[24,1024]{1,0:T(8,128)(2,1)S(1)}, u32[]{:S(2)}) copy-start(bf16[24,1024]{1,0:T(8,128)(2,1)S(1)} %fusion.27) | copy-start | bytes 147460
  100.1 164.8 %all-gather.20.cloned.1.call-start = ((), (), s32[]{:S(2)}) async-start(), calls=%async_computation.4 | async-start | bytes 2129920 | tf_op jit(solution)/shard_map/all_gather | solution.py:33
  100.8 247.6 %all-gather.22.cloned.1.call-start = ((), (), s32[]{:S(2)}) async-start(), calls=%async_computation.5 | async-start | bytes 2129920 | tf_op jit(solution)/shard_map/all_gather | solution.py:33
  102.3 330.1 %all-gather.14.cloned.1.call-start = ((), (), s32[]{:S(2)}) async-start(), calls=%async_computation.1 | async-start | bytes 2129920 | tf_op jit(solution)/shard_map/all_gather | solution.py:41
  180.7 2.4 copy-start.3
  184.0 83.2 %slice-start = ((bf16[24,1024]{1,0:T(8,128)(2,1)}), bf16[8,1024]{1,0:T(8,128)(2,1)S(1)}, s32[]{:S(2)}) async-start(bf16[24,1024]{1,0:T(8,128)(2,1)} %copy-done.5), calls=%async_computation.7 | async-start | bytes 32768 | tf_op jit(solution)/shard_map/slice | solution.py:70
  264.9 86.4 %copy-start.8 = (s32[1,128]{1,0:T(1,128)S(1)}, s32[1,128]{1,0:T(1,128)}, u32[]{:S(2)}) copy-start(s32[1,128]{1,0:T(1,128)} %param.14) | copy-start | bytes 1540
  267.2 84.2 %copy-start.1 = (bf16[1,1,1024,1024]{3,2,1,0:T(8,128)(2,1)S(1)}, bf16[1,1,1024,1024]{3,2,1,0:T(8,128)(2,1)}, u32[]{:S(2)}) copy-start(bf16[1,1,1024,1024]{3,2,1,0:T(8,128)(2,1)} %all-gather.20.cloned.1.call-done) | copy-start | bytes 6291460
  267.8 248.0 %all-gather.24.cloned.1.call-start = ((), (), s32[]{:S(2)}) async-start(), calls=%async_computation.6 | async-start | bytes 2129920 | tf_op jit(solution)/shard_map/all_gather | solution.py:33
  268.4 331.1 %all-gather.16.cloned.1.call-start = ((), (), s32[]{:S(2)}) async-start(), calls=%async_computation.2 | async-start | bytes 2129920 | tf_op jit(solution)/shard_map/all_gather | solution.py:41
  352.2 91.8 %copy-start.6 = (bf16[1,128,2048]{2,1,0:T(8,128)(2,1)S(1)}, bf16[1,128,2048]{2,1,0:T(8,128)(2,1)}, u32[]{:S(2)}) copy-start(bf16[1,128,2048]{2,1,0:T(8,128)(2,1)} %param.15) | copy-start | bytes 1572868
  436.4 7.7 %collective-permute-start = (f32[128,512]{1,0:T(8,128)S(1)}, f32[128,512]{1,0:T(8,128)S(1)}, u32[]{:S(2)}, u32[]{:S(2)}) collective-permute-start(f32[128,512]{1,0:T(8,128)S(1)} %get-tuple-element.3), channel_id=1, source_target_pairs={{0,64},{64,0},{128,192},{192,128},{256,320},{320,256},{384,448},{4... | collective-permute-start | bytes 786440 | tf_op jit(solution)/shard_map/ppermute | solution.py:8
Sparse Core Ops, SparseCore 0:
  11.7 85.2 all-gather.17
  100.2 80.4 all-gather.11
  184.4 80.4 all-gather.19
  267.8 80.4 all-gather.21
  351.9 80.4 all-gather.13
  435.3 80.4 all-gather.23
  518.9 80.4 all-gather.15
where the time goes:
time: 614 us; the launch traced here: 611 us
  waiting for transfers between devices  559 us (91%)
  matrix products  21.5 us (4%)
  between operations  14.4 us (2%)
  starting transfers between devices  6.81 us (1%)
    all_gather x4, waiting for transfers between devices, apply_inverse(): lax.all_gather(inverse_shard, 'col', axis=0, tiled=True)  318 us
    all_gather x3, waiting for transfers between devices, apply_factor(): lax.all_gather(factor_shard, 'col', axis=0, tiled=True)  239 us
    dot_general x10, matrix products, times_rows(): lax.dot_general(left_rows, segment, (((1,), (1,)), ((), ())), preferred_e...  21.5 us
  transfers between devices with their start and end apart: 8, of which 8 were waited for; matrix products, arithmetic and copies ran while one was open for 4% of the time, Pallas kernels for 0%

commit v1 on v0

v1 whole, which is shorter than its diff:
```python
import jax
import jax.numpy as jnp
from jax import lax
from jax.sharding import PartitionSpec as P


def partner(value, axis, stride):
    return lax.ppermute(value, axis, [(i, i ^ 1 << stride) for i in range(lax.axis_size(axis))])


def times_rows(left_rows, segment):
    return lax.dot_general(
        left_rows, segment, (((1,), (1,)), ((), ())), preferred_element_type=jnp.float32
    )


def local(
    child_panels,
    child_links,
    child_pivots,
    child_inverse,
    block_mask,
    row_map,
    parent_panels,
    parent_pivots,
    parent_inverse,
):
    bf16 = jnp.bfloat16
    width = child_pivots.shape[2]
    rows = child_panels.shape[1]
    shard = child_pivots.shape[1]
    link_shard = child_links.shape[1]
    leaf = lax.axis_index("leaf")
    sibling_bit = leaf % 2
    parent_index = leaf // 2

    half = shard // 2
    mine_inverse = lax.dynamic_slice(
        parent_inverse, (parent_index, sibling_bit, 0, 0), (1, 1, shard, width)
    )[0, 0]
    mine_pivots = lax.dynamic_slice(
        parent_pivots, (parent_index, sibling_bit * half, 0), (1, half, width)
    )[0]
    packed = jnp.concatenate(
        [
            child_inverse[0, 0],
            child_pivots[0],
            child_links[0, :, :width],
            child_links[0, :, width:],
            child_inverse[0, 1],
            mine_inverse,
            mine_pivots,
        ],
        0,
    )
    gathered = lax.all_gather(packed, "col", axis=0, tiled=False)

    def part(start, count):
        return gathered[:, start : start + count].reshape(-1, width)

    inverse_0 = part(0, shard)
    pivots = part(shard, shard)
    links_0 = part(2 * shard, link_shard)
    links_1 = part(2 * shard + link_shard, link_shard)
    inverse_1 = part(2 * shard + 2 * link_shard, shard)
    at = 3 * shard + 2 * link_shard
    mine = gathered[:, at:]
    theirs = partner(mine, "leaf", 0)

    flags = block_mask[0, 0].astype(bf16)
    first_input = child_panels[0, :, :width] * flags[0]
    second_input = child_panels[0, :, width:] * flags[1]
    link_count = links_0.shape[0]
    first_all = times_rows(
        jnp.concatenate([first_input, links_0, pivots], 0), inverse_0
    ).astype(bf16)
    child_first = first_all[:rows]
    pivot_first = first_all[rows + link_count :]
    update = times_rows(first_all[: rows + link_count], pivot_first)
    second_source = jnp.concatenate([second_input, links_1], 0)
    second_rhs = (second_source.astype(jnp.float32) - update).astype(bf16)
    second_all = times_rows(second_rhs, inverse_1).astype(bf16)
    child_second = second_all[:rows]
    child_factor = jnp.concatenate([child_first, child_second], 1)
    contribution = -(
        times_rows(child_first, first_all[rows : rows + link_count])
        + times_rows(child_second, second_all[rows:])
    )
    placed = (
        jnp.zeros((2 * rows, contribution.shape[1]), jnp.float32)
        .at[row_map[0]]
        .add(contribution)
    )
    own_part = lax.dynamic_slice_in_dim(placed, sibling_bit * rows, rows, 0)
    sent_part = lax.dynamic_slice_in_dim(placed, (1 - sibling_bit) * rows, rows, 0)
    received = partner(sent_part, "leaf", 0)
    even = sibling_bit == 0
    extension = jnp.where(
        even,
        jnp.concatenate([own_part, received], 1),
        jnp.concatenate([received, own_part], 1),
    )
    parent_input = (parent_panels[0, :, :width].astype(jnp.float32) + extension).astype(bf16)

    low = jnp.where(even, mine, theirs)
    high = jnp.where(even, theirs, mine)
    parent_inverse_0 = low[:, :shard].reshape(-1, width)
    parent_inverse_1 = high[:, :shard].reshape(-1, width)
    parent_pivot_rows = jnp.concatenate([low[:, shard:], high[:, shard:]], 1).reshape(-1, width)
    parent_pivot_first = times_rows(parent_pivot_rows, parent_inverse_0).astype(bf16)
    parent_first = times_rows(parent_input, parent_inverse_0).astype(bf16)
    parent_update = times_rows(parent_first, parent_pivot_first)
    parent_rhs = (parent_panels[0, :, width:].astype(jnp.float32) - parent_update).astype(bf16)
    parent_second = times_rows(parent_rhs, parent_inverse_1).astype(bf16)
    parent_factor = jnp.concatenate([parent_first, parent_second], 1)
    return (child_factor[None], parent_factor[None])


def solution(mesh):
    return jax.shard_map(
        local,
        mesh=mesh,
        in_specs=(
            P("leaf", "col", None),
            P("leaf", "col", None),
            P("leaf", "col", None),
            P("leaf", None, "col", None),
            P("leaf", "col", None),
            P("leaf", "col"),
            P("leaf", "col", None),
            P(None, "col", None),
            P(None, None, "col", None),
        ),
        out_specs=(P("leaf", "col", None), P("leaf", "col", None)),
        check_vma=False,
    )
```

time: 614 us -> 193 us (0.31)
  waiting for transfers between devices: 559 us -> 116 us
  local copies, waits for them, and re-layouts: 4.96 us -> 23.5 us
  other arithmetic: 4.48 us -> 12.2 us
    all_gather x7 -> x1, waiting for transfers between devices: 557 us -> 116 us  [local(): gathered = lax.all_gather(packed, 'col', axis=0, tiled=False)]
    unnamed x18 -> x17, local copies, waits for them, and re-layouts: 0.05 us -> 9.06 us
    dot_general x10 -> x7, matrix products: 21.5 us -> 21.7 us  [times_rows(): lax.dot_general(left_rows, segment, (((1,), (1,)), ((), ())), preferred_e...]
  transfers between devices with their start and end apart: 8 -> 3, of which waited for: 8 -> 1; matrix products, arithmetic and copies ran while one was open for 4% -> 21% of each run, Pallas kernels for 0% -> 0%
where the time goes in v1:
time: 193 us; the launch traced here: 192 us
  waiting for transfers between devices  116 us (60%)
  local copies, waits for them, and re-layouts  23.5 us (12%)
  matrix products  21.7 us (11%)
  between operations  14.2 us (7%)
  other arithmetic  12.2 us (6%)
  starting transfers between devices  4.72 us (2%)
    all_gather x1, waiting for transfers between devices, local(): gathered = lax.all_gather(packed, 'col', axis=0, tiled=False)  116 us
    dot_general x7, matrix products, times_rows(): lax.dot_general(left_rows, segment, (((1,), (1,)), ((), ())), preferred_e...  21.7 us
    unnamed x17, local copies, waits for them, and re-layouts  9.06 us
    slice x1, local copies, waits for them, and re-layouts, part(): return gathered[:, start:start + count].reshape(-1, width)  5.57 us
    ppermute x2, starting transfers between devices, partner(): lax.ppermute(value, axis, [(i, i ^ 1 << stride) for i in range(lax.axis_s...  4.69 us
  transfers between devices with their start and end apart: 3, of which 1 were waited for; matrix products, arithmetic and copies ran while one was open for 21% of the time, Pallas kernels for 0%

profile of v1, /device:TPU:1, one launch (start us, length us, event | category | flops | bytes accessed | tf_op | source)
XLA Modules:
  0.0 192.3 jit_solution(10525875611768439943)
XLA Ops:
  7.2 0.0 all-gather.3.cloned.1.call-start
  7.2 0.8 bitcast_dynamic-update-slice_fusion.3
  8.0 0.8 bitcast_dynamic-update-slice_fusion.2
  8.8 0.7 constant_dynamic-update-slice_fusion.2
  9.5 0.7 constant_dynamic-update-slice_fusion.1
  10.2 0.8 bitcast_dynamic-update-slice_fusion.1
  11.0 0.8 bitcast_dynamic-update-slice_fusion
  11.7 0.7 constant_dynamic-update-slice_fusion
  12.4 0.0 copy-start.2
  12.4 0.7 copy-done.2
  13.1 0.0 all-gather.3.cloned.1.call-update
  13.1 0.7 convert_element_type.44
  13.8 0.6 fusion.43
  14.4 3.0 %multiply_bitcast_fusion = (bf16[128,1024]{1,0:T(8,128)(2,1)}, bf16[128,1024]{1,0:T(8,128)(2,1)S(1)}) fusion(bf16[1,128,2048]{2,1,0:T(8,128)(2,1)} %param.9, bf16[]{:T(256)} %bitcast.13, bf16[]{:T(256)} %bitcast), kind=kLoop, calls=%fused_computation.39 | loop fusion | flops 262144 | bytes 1048580 | tf_op jit(solution)/shard_map/mul | solution.py:72
  17.5 115.8 %all-gather.3.cloned.1.call-done = bf16[5632,1024]{1,0:T(8,128)(2,1)} async-done(((bf16[88,1024]{1,0:T(8,128)(2,1)}), bf16[5632,1024]{1,0:T(8,128)(2,1)}) %all-gather.3.cloned.1.call-update) | async-done | bytes 11534352 | tf_op jit(solution)/shard_map/all_gather | solution.py:56
  133.3 0.0 copy-start.4
  133.3 2.2 %slice.117 = bf16[64,24,1024]{2,1,0:T(8,128)(2,1)S(1)} slice(bf16[64,88,1024]{2,1,0:T(8,128)(2,1)} %bitcast.56), slice={[0:64], [64:88], [0:1024]} | slice | bytes 6291456 | tf_op jit(solution)/shard_map/slice | solution.py:67
  135.5 2.6 %collective-permute-start.1 = (bf16[64,24,1024]{2,1,0:T(8,128)(2,1)S(1)}, bf16[64,24,1024]{2,1,0:T(8,128)(2,1)}, u32[]{:S(2)}, u32[]{:S(2)}) collective-permute-start(bf16[64,24,1024]{2,1,0:T(8,128)(2,1)S(1)} %slice.117), channel_id=1, source_target_pairs={{0,64},{64,0},{128,192},{192,128},{256,320},{320,256},{384,448},{4... | collective-permute-start | bytes 9437192 | tf_op jit(solution)/shard_map/ppermute | solution.py:8
  138.1 0.0 copy-done.4
  138.1 2.7 %slice_bitcast_fusion = (bf16[512,1024]{1,0:T(8,128)(2,1)}, bf16[512,1024]{1,0:T(8,128)(2,1)S(1)}) fusion(bf16[64,88,1024]{2,1,0:T(8,128)(2,1)} %bitcast.57), kind=kLoop, calls=%fused_computation.27 | loop fusion | bytes 4194304 | tf_op jit(solution)/shard_map/reshape | solution.py:59
  140.8 5.6 %fusion.42 = (bf16[64,16,1024]{2,1,0:T(8,128)(2,1)S(1)}, bf16[64,16,1024]{2,1,0:T(8,128)(2,1)}, bf16[64,16,1024]{2,1,0:T(8,128)(2,1)S(1)}) fusion(bf16[64,88,1024]{2,1,0:T(8,128)(2,1)} %bitcast.58), kind=kLoop, calls=%fused_computation.57 | loop fusion | bytes 12582912 | tf_op jit(solution)/shard_map/slice | solution.py:59
  146.4 4.2 %convolution_convert_fusion = bf16[1664,1024]{0,1:T(8,128)(2,1)S(1)} fusion(bf16[1024,1024]{1,0:T(8,128)(2,1)S(1)} %bitcast.66, bf16[1024,1024]{1,0:T(8,128)(2,1)S(1)} %bitcast.65, bf16[512,1024]{1,0:T(8,128)(2,1)S(1)} %get-tuple-element.7, bf16[128,1024]{1,0:T(8,128)(2,1)S(1)} %get-tuple-element.14), kind=kOutput, calls=%fused_computation.1 | convolution fusion | flops 3501588480 | bytes 8912896 | tf_op jit(solution)/shard_map/dot_general | solution.py:12
  150.6 0.0 copy-start.1
  150.6 1.8 copy-done.1
  152.4 0.0 slice-start
  152.4 7.3 %convolution_convert_fusion.1 = bf16[640,1024]{0,1:T(8,128)(2,1)} fusion(bf16[1024,1024]{1,0:T(8,128)(2,1)} %bitcast.64, bf16[1664,1024]{0,1:T(8,128)(2,1)} %copy-done.1, bf16[512,1024]{1,0:T(8,128)(2,1)} %get-tuple-element.6, bf16[128,1024]{1,0:T(8,128)(2,1)} %get-tuple-element.13), kind=kOutput, calls=%fused_computation.15 | convolution fusion | flops 2688942080 | bytes 8126464 | tf_op jit(solution)/shard_map/dot_general | solution.py:12
  159.8 1.0 slice.114
  160.7 0.0 slice-done
  160.8 0.8 maximum_bitcast_fusion
  161.6 2.0 %copy.12 = bf16[1,128,2048]{2,1,0:T(8,128)(2,1)} copy(bf16[1,128,2048]{1,2,0:T(8,128)(2,1)} %maximum_bitcast_fusion) | data formatting | bytes 1048576
  163.6 1.6 fusion.22
  165.3 1.7 fusion.20
  166.9 2.1 %scatter_custom_fusion = f32[256,512]{1,0:T(8,128)} fusion(s32[128]{0:T(128)S(1)} %fusion.36, f32[128,512]{1,0:T(8,128)S(1)} %fusion.20, f32[]{:T(128)} %constant.43.clone.1), kind=kCustom, calls=%fused_computation.36 | custom fusion | flops 65536 | bytes 524292 | tf_op jit(solution)/shard_map/scatter-add | solution.py:92
  169.0 1.1 constant_dynamic-slice_fusion
  170.1 2.1 %collective-permute-start = (f32[128,512]{1,0:T(8,128)S(1)}, f32[128,512]{1,0:T(8,128)S(1)}, u32[]{:S(2)}, u32[]{:S(2)}) collective-permute-start(f32[128,512]{1,0:T(8,128)S(1)} %get-tuple-element.11), channel_id=1, source_target_pairs={{0,64},{64,0},{128,192},{192,128},{256,320},{320,256},{384,448},{4... | collective-permute-start | bytes 786440 | tf_op jit(solution)/shard_map/ppermute | solution.py:8
  172.2 0.0 collective-permute-done.1
  172.2 3.3 %broadcast_select_fusion = (bf16[64,24,1024]{2,1,0:T(8,128)(2,1)S(1)}, bf16[64,24,1024]{2,1,0:T(8,128)(2,1)S(1)}) fusion(bf16[64,24,1024]{2,1,0:T(8,128)(2,1)} %collective-permute-done.1, pred[]{:T(512)S(6)} %eq.5, bf16[64,88,1024]{2,1,0:T(8,128)(2,1)} %bitcast.59), kind=kLoop, calls=%fused_computation.7 | loop fusion | flops 3145728 | bytes 12582913 | tf_op jit(solution)/shard_map/jit(_where)/select_n | solution.py:106
  175.5 0.2 slice.118
  175.7 0.0 copy-start
  175.7 0.1 slice.119
  175.8 0.1 slice.120
  175.8 0.2 slice.121
  176.1 0.0 copy-start.3
  176.1 1.5 pad_maximum_fusion
  177.6 0.0 collective-permute-done
  177.6 0.1 copy-done
  177.7 0.0 copy-done.3
  177.7 0.9 convolution_convert_fusion.3
  178.6 5.2 %fusion.17 = bf16[128,1024]{1,0:T(8,128)(2,1)S(1)} fusion(bf16[128,1024]{1,0:T(8,128)(2,1)S(1)} %convolution_convert_fusion.3, bf16[1024,1024]{1,0:T(8,128)(2,1)} %bitcast.63, bf16[1024,1024]{1,0:T(8,128)(2,1)} %bitcast.62, bf16[1,128,2048]{2,1,0:T(8,128)(2,1)S(1)} %copy-done.3), kind=kOutput, calls=%fused_computation.19 | convolution fusion | flops 2417360896 | bytes 4980736 | tf_op jit(solution)/shard_map/dot_general | solution.py:12
  183.8 0.8 convolution_convert_fusion.2
  184.6 0.8 maximum_bitcast_fusion.1
  (1 shorter events, 0.0 us)
Async XLA Ops:
  7.2 126.1 %all-gather.3.cloned.1.call-start = ((), (), s32[]{:S(2)}) async-start(), calls=%async_computation | async-start | bytes 11714560 | tf_op jit(solution)/shard_map/all_gather | solution.py:56
  12.4 0.7 copy-start.2
  133.3 4.8 %copy-start.4 = (s32[1,128]{1,0:T(1,128)S(1)}, s32[1,128]{1,0:T(1,128)}, u32[]{:S(2)}) copy-start(s32[1,128]{1,0:T(1,128)} %param.14) | copy-start | bytes 1540
  135.5 36.7 %collective-permute-start.1 = (bf16[64,24,1024]{2,1,0:T(8,128)(2,1)S(1)}, bf16[64,24,1024]{2,1,0:T(8,128)(2,1)}, u32[]{:S(2)}, u32[]{:S(2)}) collective-permute-start(bf16[64,24,1024]{2,1,0:T(8,128)(2,1)S(1)} %slice.117), channel_id=1, source_target_pairs={{0,64},{64,0},{128,192},{192,128},{256,320},{320,256},{384,448},{4... | collective-permute-start | bytes 9437192 | tf_op jit(solution)/shard_map/ppermute | solution.py:8
  150.6 1.8 copy-start.1
  152.4 8.3 %slice-start = ((bf16[1664,1024]{0,1:T(8,128)(2,1)}), bf16[128,1024]{0,1:T(8,128)(2,1)S(1)}, s32[]{:S(2)}) async-start(bf16[1664,1024]{0,1:T(8,128)(2,1)} %copy-done.1), calls=%async_computation.1 | async-start | bytes 524288 | tf_op jit(solution)/shard_map/slice | solution.py:77
  170.1 7.5 %collective-permute-start = (f32[128,512]{1,0:T(8,128)S(1)}, f32[128,512]{1,0:T(8,128)S(1)}, u32[]{:S(2)}, u32[]{:S(2)}) collective-permute-start(f32[128,512]{1,0:T(8,128)S(1)} %get-tuple-element.11), channel_id=1, source_target_pairs={{0,64},{64,0},{128,192},{192,128},{256,320},{320,256},{384,448},{4... | collective-permute-start | bytes 786440 | tf_op jit(solution)/shard_map/ppermute | solution.py:8
  175.7 2.0 %copy-start = (bf16[64,16,1024]{2,1,0:T(8,128)(2,1)}, bf16[64,16,1024]{2,1,0:T(8,128)(2,1)S(1)}, u32[]{:S(2)}) copy-start(bf16[64,16,1024]{2,1,0:T(8,128)(2,1)S(1)} %slice.118) | copy-start | bytes 6291460
  176.1 1.6 copy-start.3
Sparse Core Ops, SparseCore 0:
  13.2 119.9 all-gather.2

commit v2 on v0

v2 whole, which is shorter than its diff:
```python
import functools

import jax
import jax.numpy as jnp
from jax import lax
from jax.experimental import pallas as pl
from jax.experimental.pallas import tpu as pltpu
from jax.sharding import PartitionSpec as P

BF16, F32 = jnp.bfloat16, jnp.float32
SIDE = 8
ROWS = 128
WIDTH = 1024
LINK = 512
TILE = 256
AXES = ("leaf", "col")
VMEM = pl.BlockSpec(memory_space=pltpu.VMEM)
SMEM = pl.BlockSpec(memory_space=pltpu.SMEM)
ANY = pl.BlockSpec(memory_space=pl.ANY)


def lines():
    even = [[(leaf * SIDE + z) * SIDE + y for y in range(SIDE)] for leaf in range(0, 8, 2) for z in range(SIDE)]
    odd = [[(leaf * SIDE + z) * SIDE + y for z in range(SIDE)] for leaf in range(1, 8, 2) for y in range(SIDE)]
    return even + odd


def ring(step):
    pairs = []
    for leaf in range(8):
        for z in range(SIDE):
            for y in range(SIDE):
                dz, dy = (step, 0) if leaf % 2 == 0 else (0, step)
                target = (leaf * SIDE + (z + dz) % SIDE) * SIDE + (y + dy) % SIDE
                pairs.append(((leaf * SIDE + z) * SIDE + y, target))
    return pairs


def swap_cores(value):
    return lax.ppermute(value, "leaf", [(i, i ^ 1) for i in range(8)])


def times_rows(left, right):
    return lax.dot_general(left, right, (((1,), (1,)), ((), ())), preferred_element_type=F32)


def times_lower(left, inverse, out):
    for j in range(WIDTH // TILE):
        depth = TILE * (j + 1)
        rows = inverse[2 * j : 2 * j + 2, :, :, :depth].reshape(TILE, depth)
        out[:, TILE * j : depth] = times_rows(left(depth), rows).astype(BF16)


def child_kernel(row_map, mask, panels, *refs):
    blocks, refs = refs[:9], refs[9:]
    factor, own, sent, inv0, piv, lnk, inv1, p1, x1, x2, f1, r2, f2, placed, contrib, sems = refs
    leaf, col = lax.axis_index("leaf"), lax.axis_index("col")
    core = lax.rem(leaf, 2)
    place = jnp.where(core == 0, col // SIDE, lax.rem(col, SIDE))
    half = SIDE // 2
    sources = [(0, 0, SIDE)] + [(-k, 0, SIDE) for k in (1, 2, 3)] + [(k, 0, SIDE) for k in (1, 2, 3)]
    sources += [(half, 0, half), (half, half, half)]
    copies = [[], [], [], []]
    for i, (block, (offset, first, count)) in enumerate(zip(blocks, sources, strict=True)):
        at = lax.rem(place + offset + SIDE, SIDE)
        for m, target in enumerate((inv0, piv, lnk, inv1)):
            sem = sems.at[i, m]
            by_z = pltpu.make_async_copy(block.at[:, m], target.at[at, pl.ds(first, count)], sem)
            by_y = pltpu.make_async_copy(block.at[:, m], target.at[pl.ds(first, count), at], sem)

            @pl.when(core == 0)
            def _():
                by_z.start()

            @pl.when(core != 0)
            def _():
                by_y.start()

            copies[m].append(by_z)

    zero = jnp.zeros((), BF16)
    x1[:ROWS] = jnp.where(mask[0, 0, 0] != 0, panels[:, :WIDTH], zero)
    x2[:ROWS] = jnp.where(mask[0, 0, 1] != 0, panels[:, WIDTH:], zero)
    placed[...] = jnp.zeros_like(placed)
    for m in (2, 0, 1):
        for copy in copies[m]:
            copy.wait()
    for j in range(LINK // 16):
        one = lnk[j // 4, 2 * j % 8].astype(F32)
        two = lnk[j // 4, 2 * j % 8 + 1].astype(F32)
        x1[ROWS + 16 * j : ROWS + 16 * j + 16] = jnp.concatenate([one[:8], two[:8]], 0).astype(BF16)
        x2[ROWS + 16 * j : ROWS + 16 * j + 16] = jnp.concatenate([one[8:], two[8:]], 0).astype(BF16)
    times_lower(lambda depth: piv[:, :, :, :depth].reshape(WIDTH, depth), inv0, p1)
    times_lower(lambda depth: x1[:, :depth], inv0, f1)
    for j in range(WIDTH // TILE):
        at = slice(TILE * j, TILE * j + TILE)
        r2[:, at] = (x2[:, at].astype(F32) - times_rows(f1[...], p1[at, :])).astype(BF16)
    for copy in copies[3]:
        copy.wait()
    times_lower(lambda depth: r2[:, :depth], inv1, f2)
    contrib[...] = -(times_rows(f1[:ROWS], f1[ROWS:]) + times_rows(f2[:ROWS], f2[ROWS:]))
    factor[:, :WIDTH] = f1[:ROWS]
    factor[:, WIDTH:] = f2[:ROWS]
    flip = core * ROWS

    def put(r, carry):
        t = row_map[0, r]
        t = jnp.where(t >= ROWS, t - ROWS + (ROWS - flip), t + flip)
        placed[pl.ds(t, 1), :] = contrib[pl.ds(r, 1), :]
        return carry

    lax.fori_loop(0, ROWS, put, 0)
    own[...] = placed[:ROWS]
    sent[...] = placed[ROWS:]


def start_from(core, low, high, pairs):
    copies = []
    for from_low, lanes, target, sem in pairs:
        mine, theirs = (low, high) if from_low else (high, low)
        here = pltpu.make_async_copy(mine.at[:, :, :, lanes], target, sem)
        there = pltpu.make_async_copy(theirs.at[:, :, :, lanes], target, sem)

        @pl.when(core == 0)
        def _():
            here.start()

        @pl.when(core != 0)
        def _():
            there.start()

        copies.append(here)
    return copies


def pivot_kernel(mine, theirs, p1, inv0, piv, sems):
    core = lax.rem(lax.axis_index("leaf"), 2)
    half = WIDTH // 2
    tail = pl.ds(WIDTH, half)
    copies = start_from(
        core,
        mine,
        theirs,
        [
            (True, pl.ds(0, WIDTH), inv0, sems.at[0]),
            (True, tail, piv.at[:, :, :, pl.ds(0, half)], sems.at[1]),
            (False, tail, piv.at[:, :, :, pl.ds(half, half)], sems.at[2]),
        ],
    )
    for copy in copies:
        copy.wait()
    times_lower(lambda depth: piv[:, :, :, :depth].reshape(WIDTH, depth), inv0, p1)


def parent_kernel(panels, own, received, p1, mine, theirs, factor, inv0, inv1, x1, f1, r2, f2, sems):
    core = lax.rem(lax.axis_index("leaf"), 2)
    whole = pl.ds(0, WIDTH)
    copies = start_from(
        core, mine, theirs, [(True, whole, inv0, sems.at[0]), (False, whole, inv1, sems.at[1])]
    )
    even = core == 0
    left = jnp.where(even, own[...], received[...])
    right = jnp.where(even, received[...], own[...])
    x1[:, :LINK] = (panels[:, :LINK].astype(F32) + left).astype(BF16)
    x1[:, LINK:] = (panels[:, LINK:WIDTH].astype(F32) + right).astype(BF16)
    copies[0].wait()
    times_lower(lambda depth: x1[:, :depth], inv0, f1)
    for j in range(WIDTH // TILE):
        at = slice(TILE * j, TILE * j + TILE)
        source = panels[:, WIDTH + TILE * j : WIDTH + TILE * j + TILE].astype(F32)
        r2[:, at] = (source - times_rows(f1[...], p1[at, :])).astype(BF16)
    copies[1].wait()
    times_lower(lambda depth: r2[:, :depth], inv1, f2)
    factor[:, :WIDTH] = f1[...]
    factor[:, WIDTH:] = f2[...]


def matrix(*shape, dtype=BF16):
    return pltpu.VMEM(shape, dtype)


def call(kernel, in_specs, outs, scratch, flops):
    return pl.pallas_call(
        kernel,
        in_specs=in_specs,
        out_specs=tuple(VMEM for _ in outs),
        out_shape=tuple(jax.ShapeDtypeStruct(shape, dtype) for shape, dtype in outs),
        scratch_shapes=scratch,
        compiler_params=pltpu.CompilerParams(vmem_limit_bytes=24 << 20),
        cost_estimate=pl.CostEstimate(flops=flops, bytes_accessed=8 << 20, transcendentals=0),
    )


def local(
    child_panels,
    child_links,
    child_pivots,
    child_inverse,
    block_mask,
    row_map,
    parent_panels,
    parent_pivots,
    parent_inverse,
):
    leaf = lax.axis_index("leaf")
    core, parent = leaf % 2, leaf // 2
    half = WIDTH // 2
    my_inverse = lax.dynamic_slice(parent_inverse, (parent, core, 0, 0), (1, 1, 16, WIDTH))[0, 0]
    my_pivots = lax.dynamic_slice(parent_pivots, (parent, 0, core * half), (1, 16, half))[0]
    packed = jnp.concatenate([my_inverse, my_pivots], 1)
    links = jnp.concatenate([child_links[0, :, :WIDTH], child_links[0, :, WIDTH:]], 0)
    message = jnp.stack([child_inverse[0, 0], child_pivots[0], links, child_inverse[0, 1]], 0)
    packed, message = lax.optimization_barrier((packed, message))

    gathered = lax.all_gather(packed, "col", axis=0, tiled=False)
    block = lax.all_to_all(
        jnp.broadcast_to(message[None], (SIDE, *message.shape)), AXES, 0, 0, axis_index_groups=lines()
    )
    up = functools.partial(lax.ppermute, axis_name=AXES, perm=ring(1))
    down = functools.partial(lax.ppermute, axis_name=AXES, perm=ring(-1))
    ups, downs = [block], [block]
    for _ in range(3):
        ups.append(up(ups[-1]))
        downs.append(down(downs[-1]))
    last_up, last_down = up(ups[-1][: SIDE // 2]), down(downs[-1][SIDE // 2 :])

    weight = (SIDE, SIDE, 16, WIDTH)
    stack = ROWS + LINK
    child_factor, own, sent = call(
        child_kernel,
        [SMEM, SMEM, VMEM] + [ANY] * 9,
        [((ROWS, 2 * WIDTH), BF16), ((ROWS, LINK), F32), ((ROWS, LINK), F32)],
        [matrix(*weight)] * 4
        + [matrix(WIDTH, WIDTH)]
        + [matrix(stack, WIDTH)] * 5
        + [matrix(2 * ROWS, LINK, dtype=F32), matrix(ROWS, LINK, dtype=F32), pltpu.SemaphoreType.DMA((9, 4))],
        7_000_000_000,
    )(row_map, block_mask, child_panels[0], *ups, *downs[1:], last_up, last_down)
    gathered, sent = lax.optimization_barrier((gathered, sent))
    received = swap_cores(sent)

    mine = gathered.reshape(SIDE, SIDE, 16, WIDTH + half)
    theirs = swap_cores(mine)
    (parent_p1,) = call(
        pivot_kernel,
        [ANY, ANY],
        [((WIDTH, WIDTH), BF16)],
        [matrix(*weight)] * 2 + [pltpu.SemaphoreType.DMA((3,))],
        1_400_000_000,
    )(mine, theirs)
    (parent_factor,) = call(
        parent_kernel,
        [VMEM] * 4 + [ANY, ANY],
        [((ROWS, 2 * WIDTH), BF16)],
        [matrix(*weight)] * 2 + [matrix(ROWS, WIDTH)] * 4 + [pltpu.SemaphoreType.DMA((2,))],
        800_000_000,
    )(parent_panels[0], own, received, parent_p1, mine, theirs)
    return (child_factor[None], parent_factor[None])


def solution(mesh):
    return jax.shard_map(
        local,
        mesh=mesh,
        in_specs=(
            P("leaf", "col", None),
            P("leaf", "col", None),
            P("leaf", "col", None),
            P("leaf", None, "col", None),
            P("leaf", "col", None),
            P("leaf", "col"),
            P("leaf", "col", None),
            P(None, "col", None),
            P(None, None, "col", None),
        ),
        out_specs=(P("leaf", "col", None), P("leaf", "col", None)),
        check_vma=False,
    )
```

time: 614 us -> 157 us (0.26)
  waiting for transfers between devices: 559 us -> 54.2 us
  starting transfers between devices: 6.81 us -> 37.9 us
  blocking collectives: 0 us -> 28.5 us
  matrix products: 21.5 us -> 0 us
  Pallas kernels: 0 us -> 16 us
    all_gather x7 -> x1, waiting for transfers between devices: 557 us -> 0.02 us  [local(): gathered = lax.all_gather(packed, 'col', axis=0, tiled=False)]
    ppermute x1 -> x10, waiting for transfers between devices: 0.3 us -> 54.2 us  [the longest x3 43.1 us: local(): ups.append(up(ups[-1]))]
    ppermute x1 -> x10, starting transfers between devices: 6.53 us -> 37.8 us  [the longest x3 13.6 us: local(): downs.append(down(downs[-1]))]
    all_to_all x0 -> x1, blocking collectives: none -> 28.5 us  [local(): lax.all_to_all(jnp.broadcast_to(message[None], (SIDE, *message.shape)), A...]
    dot_general x10 -> x0, matrix products: 21.5 us -> none  [times_rows(): lax.dot_general(left_rows, segment, (((1,), (1,)), ((), ())), preferred_e...]
    pallas_call x0 -> x3, Pallas kernels: none -> 16 us  [the longest x1 10.2 us: local(): call(child_kernel, [SMEM, SMEM, VMEM] + [ANY] * 9, [((ROWS, 2 * WIDTH), B...]
  transfers between devices with their start and end apart: 8 -> 11, of which waited for: 8 -> 7; matrix products, arithmetic and copies ran while one was open for 4% -> 0% of each run, Pallas kernels for 0% -> 8%
where the time goes in v2:
time: 157 us
  waiting for transfers between devices  54.2 us (35%)
  starting transfers between devices  37.9 us (24%)
  blocking collectives  28.5 us (18%)
  Pallas kernels  16 us (10%)
  between operations  14.3 us (9%)
  local copies, waits for them, and re-layouts  4.45 us (3%)
    ppermute x3, waiting for transfers between devices, local(): ups.append(up(ups[-1]))  43.1 us
    all_to_all x1, blocking collectives, local(): lax.all_to_all(jnp.broadcast_to(message[None], (SIDE, *message.shape)), A...  28.5 us
    ppermute x3, starting transfers between devices, local(): downs.append(down(downs[-1]))  13.6 us
    ppermute x2, starting transfers between devices, swap_cores(): return lax.ppermute(value, 'leaf', [(i, i ^ 1) for i in range(8)])  10.7 us
    pallas_call x1, Pallas kernels, local(): call(child_kernel, [SMEM, SMEM, VMEM] + [ANY] * 9, [((ROWS, 2 * WIDTH), B...  10.2 us
    ppermute x3, starting transfers between devices, local(): ups.append(up(ups[-1]))  7.02 us
    ppermute x2, starting transfers between devices, local(): last_up, last_down = (up(ups[-1][:SIDE // 2]), down(downs[-1][SIDE // 2:]))  6.49 us
    ppermute x2, waiting for transfers between devices, local(): last_up, last_down = (up(ups[-1][:SIDE // 2]), down(downs[-1][SIDE // 2:]))  6.1 us
  transfers between devices with their start and end apart: 11, of which 7 were waited for; matrix products, arithmetic and copies ran while one was open for 0% of the time, Pallas kernels for 8%

profile of v2, /device:TPU:1, one launch (start us, length us, event | category | flops | bytes accessed | tf_op | source)
XLA Modules:
  0.0 156.8 jit_solution(11125823270636557288)
XLA Ops:
  7.2 0.0 copy-start
  7.2 0.0 copy-start.5
  7.2 0.0 copy-start.6
  7.2 0.0 copy-start.4
  7.2 0.0 all-gather.3.cloned.1.call-start
  7.3 0.9 slice_bitcast_fusion.1
  8.2 0.7 slice_bitcast_fusion.3
  8.9 0.7 dynamic-slice_bitcast_fusion.1
  9.6 0.0 copy-done
  9.6 0.6 pad_maximum_fusion.1
  10.3 0.8 pad_maximum_fusion
  11.0 0.0 all-gather.3.cloned.1.call-update
  11.1 0.1 broadcast_in_dim.12
  11.2 28.5 %all_to_all.5.refs_0_ = bf16[8,4,16,1024]{3,2,1,0:T(8,128)(2,1)S(1)} all-to-all(bf16[8,4,16,1024]{3,2,1,0:T(8,128)(2,1)S(1)} %broadcast_in_dim.12), channel_id=1, replica_groups={{0,1,2,3,4,5,6,7},{8,9,10,11,12,13,14,15},{16,17,18,19,20,21,22,23},{24..., dimensions={0} | all-to-all | bytes 2097152 | tf_op jit(solution)/shard_map/all_to_all | solution.py:216
  39.7 3.2 %collective-permute-start = (bf16[8,4,16,1024]{3,2,1,0:T(8,128)(2,1)S(1)}, bf16[8,4,16,1024]{3,2,1,0:T(8,128)(2,1)S(1)}, u32[]{:S(2)}, u32[]{:S(2)}) collective-permute-start(bf16[8,4,16,1024]{3,2,1,0:T(8,128)(2,1)S(1)} %all_to_all.5.refs_0_), channel_id=1, source_target_pairs={{0,8},{1,9},{2,10},{3,11},{4,12},{5,13},{6,14},{7,15},{8,16},{9,17... | collective-permute-start | bytes 3145736 | tf_op jit(solution)/shard_map/ppermute | solution.py:223
  42.9 4.0 %collective-permute-start.3 = (bf16[8,4,16,1024]{3,2,1,0:T(8,128)(2,1)S(1)}, bf16[8,4,16,1024]{3,2,1,0:T(8,128)(2,1)S(1)}, u32[]{:S(2)}, u32[]{:S(2)}) collective-permute-start(bf16[8,4,16,1024]{3,2,1,0:T(8,128)(2,1)S(1)} %all_to_all.5.refs_0_), channel_id=1, source_target_pairs={{0,56},{1,57},{2,58},{3,59},{4,60},{5,61},{6,62},{7,63},{8,0},{9,1... | collective-permute-start | bytes 3145736 | tf_op jit(solution)/shard_map/ppermute | solution.py:224
  46.9 11.5 %collective-permute-done.refs_1_ = bf16[8,4,16,1024]{3,2,1,0:T(8,128)(2,1)S(1)} collective-permute-done((bf16[8,4,16,1024]{3,2,1,0:T(8,128)(2,1)S(1)}, bf16[8,4,16,1024]{3,2,1,0:T(8,128)(2,1)S(1)}, u32[]{:S(2)}, u32[]{:S(2)}) %collective-permute-start) | collective-permute-done | bytes 1048608 | tf_op jit(solution)/shard_map/ppermute | solution.py:223
  58.4 1.9 %collective-permute-start.1 = (bf16[8,4,16,1024]{3,2,1,0:T(8,128)(2,1)S(1)}, bf16[8,4,16,1024]{3,2,1,0:T(8,128)(2,1)S(1)}, u32[]{:S(2)}, u32[]{:S(2)}) collective-permute-start(bf16[8,4,16,1024]{3,2,1,0:T(8,128)(2,1)S(1)} %collective-permute-done.refs_1_), channel_id=1, source_target_pairs={{0,8},{1,9},{2,10},{3,11},{4,12},{5,13},{6,14},{7,15},{8,16},{9,17... | collective-permute-start | bytes 3145736 | tf_op jit(solution)/shard_map/ppermute | solution.py:223
  60.3 0.0 collective-permute-done.3.refs_4_
  60.4 4.6 %collective-permute-start.4 = (bf16[8,4,16,1024]{3,2,1,0:T(8,128)(2,1)S(1)}, bf16[8,4,16,1024]{3,2,1,0:T(8,128)(2,1)S(1)}, u32[]{:S(2)}, u32[]{:S(2)}) collective-permute-start(bf16[8,4,16,1024]{3,2,1,0:T(8,128)(2,1)S(1)} %collective-permute-done.3.refs_4_), channel_id=1, source_target_pairs={{0,56},{1,57},{2,58},{3,59},{4,60},{5,61},{6,62},{7,63},{8,0},{9,1... | collective-permute-start | bytes 3145736 | tf_op jit(solution)/shard_map/ppermute | solution.py:224
  64.9 10.5 %collective-permute-done.1.refs_2_ = bf16[8,4,16,1024]{3,2,1,0:T(8,128)(2,1)S(1)} collective-permute-done((bf16[8,4,16,1024]{3,2,1,0:T(8,128)(2,1)S(1)}, bf16[8,4,16,1024]{3,2,1,0:T(8,128)(2,1)S(1)}, u32[]{:S(2)}, u32[]{:S(2)}) %collective-permute-start.1) | collective-permute-done | bytes 1048608 | tf_op jit(solution)/shard_map/ppermute | solution.py:223
  75.5 1.9 %collective-permute-start.2 = (bf16[8,4,16,1024]{3,2,1,0:T(8,128)(2,1)S(1)}, bf16[8,4,16,1024]{3,2,1,0:T(8,128)(2,1)S(1)}, u32[]{:S(2)}, u32[]{:S(2)}) collective-permute-start(bf16[8,4,16,1024]{3,2,1,0:T(8,128)(2,1)S(1)} %collective-permute-done.1.refs_2_), channel_id=1, source_target_pairs={{0,8},{1,9},{2,10},{3,11},{4,12},{5,13},{6,14},{7,15},{8,16},{9,17... | collective-permute-start | bytes 3145736 | tf_op jit(solution)/shard_map/ppermute | solution.py:223
  77.4 1.4 collective-permute-done.4.refs_5_
  78.8 5.0 %collective-permute-start.5 = (bf16[8,4,16,1024]{3,2,1,0:T(8,128)(2,1)S(1)}, bf16[8,4,16,1024]{3,2,1,0:T(8,128)(2,1)S(1)}, u32[]{:S(2)}, u32[]{:S(2)}) collective-permute-start(bf16[8,4,16,1024]{3,2,1,0:T(8,128)(2,1)S(1)} %collective-permute-done.4.refs_5_), channel_id=1, source_target_pairs={{0,56},{1,57},{2,58},{3,59},{4,60},{5,61},{6,62},{7,63},{8,0},{9,1... | collective-permute-start | bytes 3145736 | tf_op jit(solution)/shard_map/ppermute | solution.py:224
  83.8 21.1 %collective-permute-done.2.refs_3_ = bf16[8,4,16,1024]{3,2,1,0:T(8,128)(2,1)S(1)} collective-permute-done((bf16[8,4,16,1024]{3,2,1,0:T(8,128)(2,1)S(1)}, bf16[8,4,16,1024]{3,2,1,0:T(8,128)(2,1)S(1)}, u32[]{:S(2)}, u32[]{:S(2)}) %collective-permute-start.2) | collective-permute-done | bytes 1048608 | tf_op jit(solution)/shard_map/ppermute | solution.py:223
  104.9 1.9 %collective-permute-start.6 = (bf16[4,4,16,1024]{3,2,1,0:T(8,128)(2,1)S(1)}, bf16[4,4,16,1024]{3,2,1,0:T(8,128)(2,1)S(1)}, u32[]{:S(2)}, u32[]{:S(2)}) collective-permute-start(bf16[4,4,16,1024]{3,2,1,0:T(8,128)(2,1)S(1)} %slice.24), channel_id=1, source_target_pairs={{0,8},{1,9},{2,10},{3,11},{4,12},{5,13},{6,14},{7,15},{8,16},{9,17... | collective-permute-start | bytes 1572872 | tf_op jit(solution)/shard_map/ppermute | solution.py:225
  106.9 0.0 collective-permute-done.5.refs_6_
  106.9 4.6 %collective-permute-start.7 = (bf16[4,4,16,1024]{3,2,1,0:T(8,128)(2,1)S(1)}, bf16[4,4,16,1024]{3,2,1,0:T(8,128)(2,1)S(1)}, u32[]{:S(2)}, u32[]{:S(2)}) collective-permute-start(bf16[4,4,16,1024]{3,2,1,0:T(8,128)(2,1)S(1)} %slice.25), channel_id=1, source_target_pairs={{0,56},{1,57},{2,58},{3,59},{4,60},{5,61},{6,62},{7,63},{8,0},{9,1... | collective-permute-start | bytes 1572872 | tf_op jit(solution)/shard_map/ppermute | solution.py:225
  111.5 4.6 %collective-permute-done.6.refs_7_ = bf16[4,4,16,1024]{3,2,1,0:T(8,128)(2,1)S(1)} collective-permute-done((bf16[4,4,16,1024]{3,2,1,0:T(8,128)(2,1)S(1)}, bf16[4,4,16,1024]{3,2,1,0:T(8,128)(2,1)S(1)}, u32[]{:S(2)}, u32[]{:S(2)}) %collective-permute-start.6) | collective-permute-done | bytes 524320 | tf_op jit(solution)/shard_map/ppermute | solution.py:225
  116.1 1.5 collective-permute-done.7.refs_8_
  117.6 0.0 copy-done.5
  117.6 0.0 copy-done.6
  117.6 0.0 copy-done.4
  117.6 10.2 %shard_map.104 = (bf16[128,2048]{1,0:T(8,128)(2,1)}, f32[128,512]{1,0:T(8,128)S(1)}, f32[128,512]{1,0:T(8,128)S(1)}) custom-call(s32[1,128]{1,0:T(1,128)S(1)} %copy-done.5, s32[1,1,2]{2,1,0:T(1,128)S(1)} %copy-done.6, bf16[128,2048]{1,0:T(8,128)(2,1)S(1)} %bitcast.24, bf16[8,4,16,1024]{3,2,1,0:T(8,128)(2,1)S(1)} %all_to_all.5.refs_0_, ...), custom_call_target="tpu_custom_call" | custom-call | flops 7000000000 | bytes 8388608 | tf_op jit(solution)/shard_map/pallas_call | solution.py:229
  127.8 0.0 all-gather.3.cloned.1.call-done
  127.9 8.8 %collective-permute-start.9 = (bf16[8,8,16,1536]{3,2,1,0:T(8,128)(2,1)}, bf16[8,8,16,1536]{3,2,1,0:T(8,128)(2,1)S(1)}, u32[]{:S(2)}, u32[]{:S(2)}) collective-permute-start(bf16[8,8,16,1536]{3,2,1,0:T(8,128)(2,1)} %bitcast.20), channel_id=1, source_target_pairs={{0,64},{64,0},{128,192},{192,128},{256,320},{320,256},{384,448},{4... | collective-permute-start | bytes 9437192 | tf_op jit(solution)/shard_map/ppermute | solution.py:40
  136.7 1.9 %collective-permute-start.8 = (f32[128,512]{1,0:T(8,128)S(1)}, f32[128,512]{1,0:T(8,128)S(1)}, u32[]{:S(2)}, u32[]{:S(2)}) collective-permute-start(f32[128,512]{1,0:T(8,128)S(1)} %get-tuple-element.14), channel_id=1, source_target_pairs={{0,64},{64,0},{128,192},{192,128},{256,320},{320,256},{384,448},{4... | collective-permute-start | bytes 786440 | tf_op jit(solution)/shard_map/ppermute | solution.py:40
  138.6 3.5 %collective-permute-done.9.theirs = bf16[8,8,16,1536]{3,2,1,0:T(8,128)(2,1)S(1)} collective-permute-done((bf16[8,8,16,1536]{3,2,1,0:T(8,128)(2,1)}, bf16[8,8,16,1536]{3,2,1,0:T(8,128)(2,1)S(1)}, u32[]{:S(2)}, u32[]{:S(2)}) %collective-permute-start.9) | collective-permute-done | bytes 3145760 | tf_op jit(solution)/shard_map/ppermute | solution.py:40
  142.2 0.0 copy-start.1
  142.2 1.9 %copy-done.1 = bf16[1024,1536]{1,0:T(8,128)(2,1)S(1)} copy-done((bf16[1024,1536]{1,0:T(8,128)(2,1)S(1)}, bf16[1024,1536]{1,0:T(8,128)(2,1)}, u32[]{:S(2)}) %copy-start.1) | copy-done | bytes 3145752
  144.1 0.0 copy-start.2
  144.1 0.0 copy-start.3
  144.1 2.2 %shard_map.105.p1 = bf16[1024,1024]{1,0:T(8,128)(2,1)S(1)} custom-call(bf16[8,8,16,1536]{3,2,1,0:T(8,128)(2,1)S(1)} %bitcast.21, bf16[8,8,16,1536]{3,2,1,0:T(8,128)(2,1)S(1)} %collective-permute-done.9.theirs), custom_call_target="tpu_custom_call" | custom-call | flops 1400000000 | bytes 8388608 | tf_op jit(solution)/shard_map/pallas_call | solution.py:244
  146.3 0.0 collective-permute-done.8.received
  146.3 0.0 copy-done.2
  146.3 0.0 copy-done.3
  146.3 3.6 %shard_map.106 = bf16[128,2048]{1,0:T(8,128)(2,1)} custom-call(bf16[128,2048]{1,0:T(8,128)(2,1)S(1)} %bitcast.23, f32[128,512]{1,0:T(8,128)S(1)} %get-tuple-element.11.own, f32[128,512]{1,0:T(8,128)S(1)} %collective-permute-done.8.received, bf16[1024,1024]{1,0:T(8,128)(2,1)S(1)} %shard_map.105.p1, bf16[8,8,16,1536]{3,2,1,0:T(8,128)(2,1)S(1)} %bitcast.22, ...), custom_call_target="tpu_custom_call" | custom-call | flops 800000000 | bytes 8388608 | tf_op jit(solution)/shard_map/pallas_call | solution.py:251
  (4 shorter events, 0.1 us)
Async XLA Ops:
  7.2 2.5 %copy-start = (bf16[4,2,16,1024]{3,2,1,0:T(8,128)(2,1)S(1)}, bf16[4,2,16,1024]{3,2,1,0:T(8,128)(2,1)}, u32[]{:S(2)}) copy-start(bf16[4,2,16,1024]{3,2,1,0:T(8,128)(2,1)} %param.17) | copy-start | bytes 786436
  7.2 110.4 %copy-start.5 = (s32[1,128]{1,0:T(1,128)S(1)}, s32[1,128]{1,0:T(1,128)}, u32[]{:S(2)}) copy-start(s32[1,128]{1,0:T(1,128)} %row_map.1) | copy-start | bytes 1540
  7.2 110.4 %copy-start.6 = (s32[1,1,2]{2,1,0:T(1,128)S(1)}, s32[1,1,2]{2,1,0:T(1,128)}, u32[]{:S(2)}) copy-start(s32[1,1,2]{2,1,0:T(1,128)} %mask.1) | copy-start | bytes 28
  7.2 110.4 %copy-start.4 = (bf16[1,128,2048]{2,1,0:T(8,128)(2,1)S(1)}, bf16[1,128,2048]{2,1,0:T(8,128)(2,1)}, u32[]{:S(2)}) copy-start(bf16[1,128,2048]{2,1,0:T(8,128)(2,1)} %param.9) | copy-start | bytes 1572868
  7.2 120.7 %all-gather.3.cloned.1.call-start = ((), (), s32[]{:S(2)}) async-start(), calls=%async_computation.1 | async-start | bytes 3194880 | tf_op jit(solution)/shard_map/all_gather | solution.py:215
  39.7 18.7 %collective-permute-start = (bf16[8,4,16,1024]{3,2,1,0:T(8,128)(2,1)S(1)}, bf16[8,4,16,1024]{3,2,1,0:T(8,128)(2,1)S(1)}, u32[]{:S(2)}, u32[]{:S(2)}) collective-permute-start(bf16[8,4,16,1024]{3,2,1,0:T(8,128)(2,1)S(1)} %all_to_all.5.refs_0_), channel_id=1, source_target_pairs={{0,8},{1,9},{2,10},{3,11},{4,12},{5,13},{6,14},{7,15},{8,16},{9,17... | collective-permute-start | bytes 3145736 | tf_op jit(solution)/shard_map/ppermute | solution.py:223
  42.9 17.4 %collective-permute-start.3 = (bf16[8,4,16,1024]{3,2,1,0:T(8,128)(2,1)S(1)}, bf16[8,4,16,1024]{3,2,1,0:T(8,128)(2,1)S(1)}, u32[]{:S(2)}, u32[]{:S(2)}) collective-permute-start(bf16[8,4,16,1024]{3,2,1,0:T(8,128)(2,1)S(1)} %all_to_all.5.refs_0_), channel_id=1, source_target_pairs={{0,56},{1,57},{2,58},{3,59},{4,60},{5,61},{6,62},{7,63},{8,0},{9,1... | collective-permute-start | bytes 3145736 | tf_op jit(solution)/shard_map/ppermute | solution.py:224
  58.4 17.0 %collective-permute-start.1 = (bf16[8,4,16,1024]{3,2,1,0:T(8,128)(2,1)S(1)}, bf16[8,4,16,1024]{3,2,1,0:T(8,128)(2,1)S(1)}, u32[]{:S(2)}, u32[]{:S(2)}) collective-permute-start(bf16[8,4,16,1024]{3,2,1,0:T(8,128)(2,1)S(1)} %collective-permute-done.refs_1_), channel_id=1, source_target_pairs={{0,8},{1,9},{2,10},{3,11},{4,12},{5,13},{6,14},{7,15},{8,16},{9,17... | collective-permute-start | bytes 3145736 | tf_op jit(solution)/shard_map/ppermute | solution.py:223
  60.4 18.4 %collective-permute-start.4 = (bf16[8,4,16,1024]{3,2,1,0:T(8,128)(2,1)S(1)}, bf16[8,4,16,1024]{3,2,1,0:T(8,128)(2,1)S(1)}, u32[]{:S(2)}, u32[]{:S(2)}) collective-permute-start(bf16[8,4,16,1024]{3,2,1,0:T(8,128)(2,1)S(1)} %collective-permute-done.3.refs_4_), channel_id=1, source_target_pairs={{0,56},{1,57},{2,58},{3,59},{4,60},{5,61},{6,62},{7,63},{8,0},{9,1... | collective-permute-start | bytes 3145736 | tf_op jit(solution)/shard_map/ppermute | solution.py:224
  75.5 29.4 %collective-permute-start.2 = (bf16[8,4,16,1024]{3,2,1,0:T(8,128)(2,1)S(1)}, bf16[8,4,16,1024]{3,2,1,0:T(8,128)(2,1)S(1)}, u32[]{:S(2)}, u32[]{:S(2)}) collective-permute-start(bf16[8,4,16,1024]{3,2,1,0:T(8,128)(2,1)S(1)} %collective-permute-done.1.refs_2_), channel_id=1, source_target_pairs={{0,8},{1,9},{2,10},{3,11},{4,12},{5,13},{6,14},{7,15},{8,16},{9,17... | collective-permute-start | bytes 3145736 | tf_op jit(solution)/shard_map/ppermute | solution.py:223
  78.8 28.1 %collective-permute-start.5 = (bf16[8,4,16,1024]{3,2,1,0:T(8,128)(2,1)S(1)}, bf16[8,4,16,1024]{3,2,1,0:T(8,128)(2,1)S(1)}, u32[]{:S(2)}, u32[]{:S(2)}) collective-permute-start(bf16[8,4,16,1024]{3,2,1,0:T(8,128)(2,1)S(1)} %collective-permute-done.4.refs_5_), channel_id=1, source_target_pairs={{0,56},{1,57},{2,58},{3,59},{4,60},{5,61},{6,62},{7,63},{8,0},{9,1... | collective-permute-start | bytes 3145736 | tf_op jit(solution)/shard_map/ppermute | solution.py:224
  104.9 11.1 %collective-permute-start.6 = (bf16[4,4,16,1024]{3,2,1,0:T(8,128)(2,1)S(1)}, bf16[4,4,16,1024]{3,2,1,0:T(8,128)(2,1)S(1)}, u32[]{:S(2)}, u32[]{:S(2)}) collective-permute-start(bf16[4,4,16,1024]{3,2,1,0:T(8,128)(2,1)S(1)} %slice.24), channel_id=1, source_target_pairs={{0,8},{1,9},{2,10},{3,11},{4,12},{5,13},{6,14},{7,15},{8,16},{9,17... | collective-permute-start | bytes 1572872 | tf_op jit(solution)/shard_map/ppermute | solution.py:225
  106.9 10.7 %collective-permute-start.7 = (bf16[4,4,16,1024]{3,2,1,0:T(8,128)(2,1)S(1)}, bf16[4,4,16,1024]{3,2,1,0:T(8,128)(2,1)S(1)}, u32[]{:S(2)}, u32[]{:S(2)}) collective-permute-start(bf16[4,4,16,1024]{3,2,1,0:T(8,128)(2,1)S(1)} %slice.25), channel_id=1, source_target_pairs={{0,56},{1,57},{2,58},{3,59},{4,60},{5,61},{6,62},{7,63},{8,0},{9,1... | collective-permute-start | bytes 1572872 | tf_op jit(solution)/shard_map/ppermute | solution.py:225
  127.9 14.3 %collective-permute-start.9 = (bf16[8,8,16,1536]{3,2,1,0:T(8,128)(2,1)}, bf16[8,8,16,1536]{3,2,1,0:T(8,128)(2,1)S(1)}, u32[]{:S(2)}, u32[]{:S(2)}) collective-permute-start(bf16[8,8,16,1536]{3,2,1,0:T(8,128)(2,1)} %bitcast.20), channel_id=1, source_target_pairs={{0,64},{64,0},{128,192},{192,128},{256,320},{320,256},{384,448},{4... | collective-permute-start | bytes 9437192 | tf_op jit(solution)/shard_map/ppermute | solution.py:40
  136.7 9.6 %collective-permute-start.8 = (f32[128,512]{1,0:T(8,128)S(1)}, f32[128,512]{1,0:T(8,128)S(1)}, u32[]{:S(2)}, u32[]{:S(2)}) collective-permute-start(f32[128,512]{1,0:T(8,128)S(1)} %get-tuple-element.14), channel_id=1, source_target_pairs={{0,64},{64,0},{128,192},{192,128},{256,320},{320,256},{384,448},{4... | collective-permute-start | bytes 786440 | tf_op jit(solution)/shard_map/ppermute | solution.py:40
  142.2 1.9 %copy-start.1 = (bf16[1024,1536]{1,0:T(8,128)(2,1)S(1)}, bf16[1024,1536]{1,0:T(8,128)(2,1)}, u32[]{:S(2)}) copy-start(bf16[1024,1536]{1,0:T(8,128)(2,1)} %all-gather.3.cloned.1.call-done) | copy-start | bytes 9437188
  144.1 2.3 %copy-start.2 = (bf16[1024,1536]{1,0:T(8,128)(2,1)S(1)}, bf16[1024,1536]{1,0:T(8,128)(2,1)}, u32[]{:S(2)}) copy-start(bf16[1024,1536]{1,0:T(8,128)(2,1)} %all-gather.3.cloned.1.call-done) | copy-start | bytes 9437188
  144.1 2.3 %copy-start.3 = (bf16[1,128,2048]{2,1,0:T(8,128)(2,1)S(1)}, bf16[1,128,2048]{2,1,0:T(8,128)(2,1)}, u32[]{:S(2)}) copy-start(bf16[1,128,2048]{2,1,0:T(8,128)(2,1)} %param.15) | copy-start | bytes 1572868
Sparse Core Ops, SparseCore 0:
  11.6 90.9 all-gather.2

commit v3 on v2

--- a/solution.py
+++ b/solution.py
@@ -17,6 +17,7 @@
 VMEM = pl.BlockSpec(memory_space=pltpu.VMEM)
 SMEM = pl.BlockSpec(memory_space=pltpu.SMEM)
 ANY = pl.BlockSpec(memory_space=pl.ANY)
+HBM = pl.BlockSpec(memory_space=pltpu.HBM)
 
 
 def lines():
@@ -51,19 +52,19 @@
         out[:, TILE * j : depth] = times_rows(left(depth), rows).astype(BF16)
 
 
-def child_kernel(row_map, mask, panels, *refs):
+def first_kernel(mask, panels, *refs):
     blocks, refs = refs[:9], refs[9:]
-    factor, own, sent, inv0, piv, lnk, inv1, p1, x1, x2, f1, r2, f2, placed, contrib, sems = refs
+    f1, r2, inv0, piv, lnk, p1, x1, x2, sems = refs
     leaf, col = lax.axis_index("leaf"), lax.axis_index("col")
     core = lax.rem(leaf, 2)
     place = jnp.where(core == 0, col // SIDE, lax.rem(col, SIDE))
     half = SIDE // 2
     sources = [(0, 0, SIDE)] + [(-k, 0, SIDE) for k in (1, 2, 3)] + [(k, 0, SIDE) for k in (1, 2, 3)]
     sources += [(half, 0, half), (half, half, half)]
-    copies = [[], [], [], []]
+    copies = [[], [], []]
     for i, (block, (offset, first, count)) in enumerate(zip(blocks, sources, strict=True)):
         at = lax.rem(place + offset + SIDE, SIDE)
-        for m, target in enumerate((inv0, piv, lnk, inv1)):
+        for m, target in enumerate((inv0, piv, lnk)):
             sem = sems.at[i, m]
             by_z = pltpu.make_async_copy(block.at[:, m], target.at[at, pl.ds(first, count)], sem)
             by_y = pltpu.make_async_copy(block.at[:, m], target.at[pl.ds(first, count), at], sem)
@@ -81,7 +82,6 @@
     zero = jnp.zeros((), BF16)
     x1[:ROWS] = jnp.where(mask[0, 0, 0] != 0, panels[:, :WIDTH], zero)
     x2[:ROWS] = jnp.where(mask[0, 0, 1] != 0, panels[:, WIDTH:], zero)
-    placed[...] = jnp.zeros_like(placed)
     for m in (2, 0, 1):
         for copy in copies[m]:
             copy.wait()
@@ -95,21 +95,28 @@
     for j in range(WIDTH // TILE):
         at = slice(TILE * j, TILE * j + TILE)
         r2[:, at] = (x2[:, at].astype(F32) - times_rows(f1[...], p1[at, :])).astype(BF16)
-    for copy in copies[3]:
-        copy.wait()
+
+
+def second_kernel(row_map, f1, r2, gathered, factor, own, sent, inv1, f2, placed, contrib, sem):
+    copy = pltpu.make_async_copy(gathered.at[:, :, :, pl.ds(0, WIDTH)], inv1, sem)
+    copy.start()
+    core = lax.rem(lax.axis_index("leaf"), 2)
+    placed[...] = jnp.zeros_like(placed)
+    factor[:, :WIDTH] = f1[:ROWS]
+    contrib[...] = times_rows(f1[:ROWS], f1[ROWS:])
+    copy.wait()
     times_lower(lambda depth: r2[:, :depth], inv1, f2)
-    contrib[...] = -(times_rows(f1[:ROWS], f1[ROWS:]) + times_rows(f2[:ROWS], f2[ROWS:]))
-    factor[:, :WIDTH] = f1[:ROWS]
+    contrib[...] = -(contrib[...] + times_rows(f2[:ROWS], f2[ROWS:]))
     factor[:, WIDTH:] = f2[:ROWS]
     flip = core * ROWS
 
     def put(r, carry):
         t = row_map[0, r]
-        t = jnp.where(t >= ROWS, t - ROWS + (ROWS - flip), t + flip)
+        t = jnp.where(t >= ROWS, t - flip, t + flip)
         placed[pl.ds(t, 1), :] = contrib[pl.ds(r, 1), :]
         return carry
 
-    lax.fori_loop(0, ROWS, put, 0)
+    lax.fori_loop(0, ROWS, put, 0, unroll=8)
     own[...] = placed[:ROWS]
     sent[...] = placed[ROWS:]
 
@@ -136,13 +143,13 @@
 def pivot_kernel(mine, theirs, p1, inv0, piv, sems):
     core = lax.rem(lax.axis_index("leaf"), 2)
     half = WIDTH // 2
-    tail = pl.ds(WIDTH, half)
+    tail = pl.ds(2 * WIDTH, half)
     copies = start_from(
         core,
         mine,
         theirs,
         [
-            (True, pl.ds(0, WIDTH), inv0, sems.at[0]),
+            (True, pl.ds(WIDTH, WIDTH), inv0, sems.at[0]),
             (True, tail, piv.at[:, :, :, pl.ds(0, half)], sems.at[1]),
             (False, tail, piv.at[:, :, :, pl.ds(half, half)], sems.at[2]),
         ],
@@ -154,7 +161,7 @@
 
 def parent_kernel(panels, own, received, p1, mine, theirs, factor, inv0, inv1, x1, f1, r2, f2, sems):
     core = lax.rem(lax.axis_index("leaf"), 2)
-    whole = pl.ds(0, WIDTH)
+    whole = pl.ds(WIDTH, WIDTH)
     copies = start_from(
         core, mine, theirs, [(True, whole, inv0, sems.at[0]), (False, whole, inv1, sems.at[1])]
     )
@@ -179,14 +186,14 @@
     return pltpu.VMEM(shape, dtype)
 
 
-def call(kernel, in_specs, outs, scratch, flops):
+def call(kernel, in_specs, outs, scratch, flops, vmem=24):
     return pl.pallas_call(
         kernel,
         in_specs=in_specs,
         out_specs=tuple(VMEM for _ in outs),
         out_shape=tuple(jax.ShapeDtypeStruct(shape, dtype) for shape, dtype in outs),
         scratch_shapes=scratch,
-        compiler_params=pltpu.CompilerParams(vmem_limit_bytes=24 << 20),
+        compiler_params=pltpu.CompilerParams(vmem_limit_bytes=vmem << 20),
         cost_estimate=pl.CostEstimate(flops=flops, bytes_accessed=8 << 20, transcendentals=0),
     )
 
@@ -207,9 +214,9 @@
     half = WIDTH // 2
     my_inverse = lax.dynamic_slice(parent_inverse, (parent, core, 0, 0), (1, 1, 16, WIDTH))[0, 0]
     my_pivots = lax.dynamic_slice(parent_pivots, (parent, 0, core * half), (1, 16, half))[0]
-    packed = jnp.concatenate([my_inverse, my_pivots], 1)
+    packed = jnp.concatenate([child_inverse[0, 1], my_inverse, my_pivots], 1)
     links = jnp.concatenate([child_links[0, :, :WIDTH], child_links[0, :, WIDTH:]], 0)
-    message = jnp.stack([child_inverse[0, 0], child_pivots[0], links, child_inverse[0, 1]], 0)
+    message = jnp.stack([child_inverse[0, 0], child_pivots[0], links], 0)
     packed, message = lax.optimization_barrier((packed, message))
 
     gathered = lax.all_gather(packed, "col", axis=0, tiled=False)
@@ -226,34 +233,41 @@
 
     weight = (SIDE, SIDE, 16, WIDTH)
     stack = ROWS + LINK
+    f1, r2 = call(
+        first_kernel,
+        [SMEM, VMEM] + [ANY] * 9,
+        [((stack, WIDTH), BF16)] * 2,
+        [matrix(*weight)] * 3 + [matrix(WIDTH, WIDTH)] + [matrix(stack, WIDTH)] * 2 + [pltpu.SemaphoreType.DMA((9, 3))],
+        5_000_000_000,
+    )(block_mask, child_panels[0], *ups, *downs[1:], last_up, last_down)
+    gathered, f1, r2 = lax.optimization_barrier((gathered, f1, r2))
+    mine = gathered.reshape(SIDE, SIDE, 16, 2 * WIDTH + half)
+    theirs = swap_cores(mine)
     child_factor, own, sent = call(
-        child_kernel,
-        [SMEM, SMEM, VMEM] + [ANY] * 9,
+        second_kernel,
+        [SMEM, VMEM, VMEM, HBM],
         [((ROWS, 2 * WIDTH), BF16), ((ROWS, LINK), F32), ((ROWS, LINK), F32)],
-        [matrix(*weight)] * 4
-        + [matrix(WIDTH, WIDTH)]
-        + [matrix(stack, WIDTH)] * 5
-        + [matrix(2 * ROWS, LINK, dtype=F32), matrix(ROWS, LINK, dtype=F32), pltpu.SemaphoreType.DMA((9, 4))],
-        7_000_000_000,
-    )(row_map, block_mask, child_panels[0], *ups, *downs[1:], last_up, last_down)
-    gathered, sent = lax.optimization_barrier((gathered, sent))
+        [matrix(*weight), matrix(stack, WIDTH), matrix(2 * ROWS, LINK, dtype=F32), matrix(ROWS, LINK, dtype=F32)]
+        + [pltpu.SemaphoreType.DMA(())],
+        1_500_000_000,
+        52,
+    )(row_map, f1, r2, mine)
     received = swap_cores(sent)
-
-    mine = gathered.reshape(SIDE, SIDE, 16, WIDTH + half)
-    theirs = swap_cores(mine)
     (parent_p1,) = call(
         pivot_kernel,
-        [ANY, ANY],
+        [HBM, ANY],
         [((WIDTH, WIDTH), BF16)],
         [matrix(*weight)] * 2 + [pltpu.SemaphoreType.DMA((3,))],
         1_400_000_000,
+        36,
     )(mine, theirs)
     (parent_factor,) = call(
         parent_kernel,
-        [VMEM] * 4 + [ANY, ANY],
+        [VMEM] * 4 + [HBM, ANY],
         [((ROWS, 2 * WIDTH), BF16)],
         [matrix(*weight)] * 2 + [matrix(ROWS, WIDTH)] * 4 + [pltpu.SemaphoreType.DMA((2,))],
         800_000_000,
+        36,
     )(parent_panels[0], own, received, parent_p1, mine, theirs)
     return (child_factor[None], parent_factor[None])
 

time: 157 us -> 157 us (level)
  waiting for transfers between devices: 54.2 us -> 48.8 us
  starting transfers between devices: 37.9 us -> 43.3 us
  Pallas kernels: 16 us -> 19 us
  blocking collectives: 28.5 us -> 25.7 us
    ppermute x3, waiting for transfers between devices: 43.1 us -> 0.13 us  [local(): ups.append(up(ups[-1]))]
    ppermute x3, waiting for transfers between devices: 1.39 us -> 35.3 us  [local(): downs.append(down(downs[-1]))]
    ppermute x2, waiting for transfers between devices: 6.1 us -> 12.6 us  [local(): last_up, last_down = (up(ups[-1][:SIDE // 2]), down(downs[-1][SIDE // 2:]))]
    ppermute x2, starting transfers between devices: 10.7 us -> 14.5 us  [swap_cores(): return lax.ppermute(value, 'leaf', [(i, i ^ 1) for i in range(8)])]
    pallas_call x3 -> x4, Pallas kernels: 16 us -> 19 us  [the longest x1 5.68 us: local(): call(second_kernel, [SMEM, VMEM, VMEM, HBM], [((ROWS, 2 * WIDTH), BF16),...]
    ppermute x2, waiting for transfers between devices: 3.55 us -> 0.71 us  [swap_cores(): return lax.ppermute(value, 'leaf', [(i, i ^ 1) for i in range(8)])]
    all_to_all x1, blocking collectives: 28.5 us -> 25.7 us  [local(): lax.all_to_all(jnp.broadcast_to(message[None], (SIDE, *message.shape)), A...]
    ppermute x3, starting transfers between devices: 13.6 us -> 15.7 us  [local(): downs.append(down(downs[-1]))]
  transfers between devices with their start and end apart: 11 -> 11, of which waited for: 7 -> 7; matrix products, arithmetic and copies ran while one was open for 0% -> 0% of each run, Pallas kernels for 8% -> 9%
where the time goes in v3:
time: 157 us; the launch traced here: 156 us
  waiting for transfers between devices  48.8 us (31%)
  starting transfers between devices  43.3 us (28%)
  blocking collectives  25.7 us (16%)
  Pallas kernels  19 us (12%)
  between operations  14.3 us (9%)
  local copies, waits for them, and re-layouts  3.45 us (2%)
    ppermute x3, waiting for transfers between devices, local(): downs.append(down(downs[-1]))  35.3 us
    all_to_all x1, blocking collectives, local(): lax.all_to_all(jnp.broadcast_to(message[None], (SIDE, *message.shape)), A...  25.7 us
    ppermute x3, starting transfers between devices, local(): downs.append(down(downs[-1]))  15.7 us
    ppermute x2, starting transfers between devices, swap_cores(): return lax.ppermute(value, 'leaf', [(i, i ^ 1) for i in range(8)])  14.5 us
    ppermute x2, waiting for transfers between devices, local(): last_up, last_down = (up(ups[-1][:SIDE // 2]), down(downs[-1][SIDE // 2:]))  12.6 us
    ppermute x2, starting transfers between devices, local(): last_up, last_down = (up(ups[-1][:SIDE // 2]), down(downs[-1][SIDE // 2:]))  7.35 us
    ppermute x3, starting transfers between devices, local(): ups.append(up(ups[-1]))  5.75 us
    pallas_call x1, Pallas kernels, local(): call(second_kernel, [SMEM, VMEM, VMEM, HBM], [((ROWS, 2 * WIDTH), BF16),...  5.68 us
  transfers between devices with their start and end apart: 11, of which 7 were waited for; matrix products, arithmetic and copies ran while one was open for 0% of the time, Pallas kernels for 9%

profile of v3, /device:TPU:1, one launch (start us, length us, event | category | flops | bytes accessed | tf_op | source)
XLA Modules:
  0.0 155.9 jit_solution(7043545656257233528)
XLA Ops:
  7.2 0.0 copy-start
  7.2 0.0 all-gather.3.cloned.1.call-start
  7.3 0.7 slice_bitcast_fusion.3
  8.0 0.8 slice_bitcast_fusion
  8.8 0.7 dynamic-slice_bitcast_fusion.1
  9.5 0.0 copy-done
  9.5 0.8 pad_maximum_fusion
  10.3 0.6 pad_maximum_fusion.1
  10.9 0.0 copy-start.5
  10.9 0.0 copy-start.6
  10.9 0.0 all-gather.3.cloned.1.call-update
  11.0 0.1 broadcast_in_dim.12
  11.0 25.7 %all_to_all.5.refs_0_ = bf16[8,3,16,1024]{3,2,1,0:T(8,128)(2,1)S(1)} all-to-all(bf16[8,3,16,1024]{3,2,1,0:T(8,128)(2,1)S(1)} %broadcast_in_dim.12), channel_id=1, replica_groups={{0,1,2,3,4,5,6,7},{8,9,10,11,12,13,14,15},{16,17,18,19,20,21,22,23},{24..., dimensions={0} | all-to-all | bytes 1572864 | tf_op jit(solution)/shard_map/all_to_all | solution.py:223
  36.8 5.1 %collective-permute-start.3 = (bf16[8,3,16,1024]{3,2,1,0:T(8,128)(2,1)S(1)}, bf16[8,3,16,1024]{3,2,1,0:T(8,128)(2,1)S(1)}, u32[]{:S(2)}, u32[]{:S(2)}) collective-permute-start(bf16[8,3,16,1024]{3,2,1,0:T(8,128)(2,1)S(1)} %all_to_all.5.refs_0_), channel_id=1, source_target_pairs={{0,56},{1,57},{2,58},{3,59},{4,60},{5,61},{6,62},{7,63},{8,0},{9,1... | collective-permute-start | bytes 2359304 | tf_op jit(solution)/shard_map/ppermute | solution.py:231
  41.9 1.9 %collective-permute-start = (bf16[8,3,16,1024]{3,2,1,0:T(8,128)(2,1)S(1)}, bf16[8,3,16,1024]{3,2,1,0:T(8,128)(2,1)S(1)}, u32[]{:S(2)}, u32[]{:S(2)}) collective-permute-start(bf16[8,3,16,1024]{3,2,1,0:T(8,128)(2,1)S(1)} %all_to_all.5.refs_0_), channel_id=1, source_target_pairs={{0,8},{1,9},{2,10},{3,11},{4,12},{5,13},{6,14},{7,15},{8,16},{9,17... | collective-permute-start | bytes 2359304 | tf_op jit(solution)/shard_map/ppermute | solution.py:230
  43.8 8.1 %collective-permute-done.3.refs_4_ = bf16[8,3,16,1024]{3,2,1,0:T(8,128)(2,1)S(1)} collective-permute-done((bf16[8,3,16,1024]{3,2,1,0:T(8,128)(2,1)S(1)}, bf16[8,3,16,1024]{3,2,1,0:T(8,128)(2,1)S(1)}, u32[]{:S(2)}, u32[]{:S(2)}) %collective-permute-start.3) | collective-permute-done | bytes 786464 | tf_op jit(solution)/shard_map/ppermute | solution.py:231
  51.9 5.3 %collective-permute-start.4 = (bf16[8,3,16,1024]{3,2,1,0:T(8,128)(2,1)S(1)}, bf16[8,3,16,1024]{3,2,1,0:T(8,128)(2,1)S(1)}, u32[]{:S(2)}, u32[]{:S(2)}) collective-permute-start(bf16[8,3,16,1024]{3,2,1,0:T(8,128)(2,1)S(1)} %collective-permute-done.3.refs_4_), channel_id=1, source_target_pairs={{0,56},{1,57},{2,58},{3,59},{4,60},{5,61},{6,62},{7,63},{8,0},{9,1... | collective-permute-start | bytes 2359304 | tf_op jit(solution)/shard_map/ppermute | solution.py:231
  57.2 0.1 collective-permute-done.refs_1_
  57.3 1.9 %collective-permute-start.1 = (bf16[8,3,16,1024]{3,2,1,0:T(8,128)(2,1)S(1)}, bf16[8,3,16,1024]{3,2,1,0:T(8,128)(2,1)S(1)}, u32[]{:S(2)}, u32[]{:S(2)}) collective-permute-start(bf16[8,3,16,1024]{3,2,1,0:T(8,128)(2,1)S(1)} %collective-permute-done.refs_1_), channel_id=1, source_target_pairs={{0,8},{1,9},{2,10},{3,11},{4,12},{5,13},{6,14},{7,15},{8,16},{9,17... | collective-permute-start | bytes 2359304 | tf_op jit(solution)/shard_map/ppermute | solution.py:230
  59.2 7.0 %collective-permute-done.4.refs_5_ = bf16[8,3,16,1024]{3,2,1,0:T(8,128)(2,1)S(1)} collective-permute-done((bf16[8,3,16,1024]{3,2,1,0:T(8,128)(2,1)S(1)}, bf16[8,3,16,1024]{3,2,1,0:T(8,128)(2,1)S(1)}, u32[]{:S(2)}, u32[]{:S(2)}) %collective-permute-start.4) | collective-permute-done | bytes 786464 | tf_op jit(solution)/shard_map/ppermute | solution.py:231
  66.3 5.3 %collective-permute-start.5 = (bf16[8,3,16,1024]{3,2,1,0:T(8,128)(2,1)S(1)}, bf16[8,3,16,1024]{3,2,1,0:T(8,128)(2,1)S(1)}, u32[]{:S(2)}, u32[]{:S(2)}) collective-permute-start(bf16[8,3,16,1024]{3,2,1,0:T(8,128)(2,1)S(1)} %collective-permute-done.4.refs_5_), channel_id=1, source_target_pairs={{0,56},{1,57},{2,58},{3,59},{4,60},{5,61},{6,62},{7,63},{8,0},{9,1... | collective-permute-start | bytes 2359304 | tf_op jit(solution)/shard_map/ppermute | solution.py:231
  71.6 0.0 collective-permute-done.1.refs_2_
  71.6 1.9 %collective-permute-start.2 = (bf16[8,3,16,1024]{3,2,1,0:T(8,128)(2,1)S(1)}, bf16[8,3,16,1024]{3,2,1,0:T(8,128)(2,1)S(1)}, u32[]{:S(2)}, u32[]{:S(2)}) collective-permute-start(bf16[8,3,16,1024]{3,2,1,0:T(8,128)(2,1)S(1)} %collective-permute-done.1.refs_2_), channel_id=1, source_target_pairs={{0,8},{1,9},{2,10},{3,11},{4,12},{5,13},{6,14},{7,15},{8,16},{9,17... | collective-permute-start | bytes 2359304 | tf_op jit(solution)/shard_map/ppermute | solution.py:230
  73.5 20.2 %collective-permute-done.5.refs_6_ = bf16[8,3,16,1024]{3,2,1,0:T(8,128)(2,1)S(1)} collective-permute-done((bf16[8,3,16,1024]{3,2,1,0:T(8,128)(2,1)S(1)}, bf16[8,3,16,1024]{3,2,1,0:T(8,128)(2,1)S(1)}, u32[]{:S(2)}, u32[]{:S(2)}) %collective-permute-start.5) | collective-permute-done | bytes 786464 | tf_op jit(solution)/shard_map/ppermute | solution.py:231
  93.7 5.4 %collective-permute-start.7 = (bf16[4,3,16,1024]{3,2,1,0:T(8,128)(2,1)S(1)}, bf16[4,3,16,1024]{3,2,1,0:T(8,128)(2,1)S(1)}, u32[]{:S(2)}, u32[]{:S(2)}) collective-permute-start(bf16[4,3,16,1024]{3,2,1,0:T(8,128)(2,1)S(1)} %slice.25), channel_id=1, source_target_pairs={{0,56},{1,57},{2,58},{3,59},{4,60},{5,61},{6,62},{7,63},{8,0},{9,1... | collective-permute-start | bytes 1179656 | tf_op jit(solution)/shard_map/ppermute | solution.py:232
  99.2 0.0 collective-permute-done.2.refs_3_
  99.2 1.9 %collective-permute-start.6 = (bf16[4,3,16,1024]{3,2,1,0:T(8,128)(2,1)S(1)}, bf16[4,3,16,1024]{3,2,1,0:T(8,128)(2,1)S(1)}, u32[]{:S(2)}, u32[]{:S(2)}) collective-permute-start(bf16[4,3,16,1024]{3,2,1,0:T(8,128)(2,1)S(1)} %slice.24), channel_id=1, source_target_pairs={{0,8},{1,9},{2,10},{3,11},{4,12},{5,13},{6,14},{7,15},{8,16},{9,17... | collective-permute-start | bytes 1179656 | tf_op jit(solution)/shard_map/ppermute | solution.py:232
  101.1 9.7 %collective-permute-done.7.refs_8_ = bf16[4,3,16,1024]{3,2,1,0:T(8,128)(2,1)S(1)} collective-permute-done((bf16[4,3,16,1024]{3,2,1,0:T(8,128)(2,1)S(1)}, bf16[4,3,16,1024]{3,2,1,0:T(8,128)(2,1)S(1)}, u32[]{:S(2)}, u32[]{:S(2)}) %collective-permute-start.7) | collective-permute-done | bytes 393248 | tf_op jit(solution)/shard_map/ppermute | solution.py:232
  110.8 3.0 %collective-permute-done.6.refs_7_ = bf16[4,3,16,1024]{3,2,1,0:T(8,128)(2,1)S(1)} collective-permute-done((bf16[4,3,16,1024]{3,2,1,0:T(8,128)(2,1)S(1)}, bf16[4,3,16,1024]{3,2,1,0:T(8,128)(2,1)S(1)}, u32[]{:S(2)}, u32[]{:S(2)}) %collective-permute-start.6) | collective-permute-done | bytes 393248 | tf_op jit(solution)/shard_map/ppermute | solution.py:232
  113.8 0.0 copy-done.5
  113.8 0.0 copy-done.6
  113.8 0.0 copy-start.4
  113.8 5.4 %shard_map.104 = (bf16[640,1024]{1,0:T(8,128)(2,1)S(1)}, bf16[640,1024]{1,0:T(8,128)(2,1)S(1)}) custom-call(s32[1,1,2]{2,1,0:T(1,128)S(1)} %copy-done.6, bf16[128,2048]{1,0:T(8,128)(2,1)S(1)} %bitcast.25, bf16[8,3,16,1024]{3,2,1,0:T(8,128)(2,1)S(1)} %all_to_all.5.refs_0_, bf16[8,3,16,1024]{3,2,1,0:T(8,128)(2,1)S(1)} %collective-permute-done.refs_1_, ...), custom_call_target="tpu_custom_call" | custom-call | flops 5000000000 | bytes 8388608 | tf_op jit(solution)/shard_map/pallas_call | solution.py:236
  119.2 0.0 copy-start.2
  119.2 1.0 copy-done.2
  120.3 0.0 all-gather.3.cloned.1.call-done
  120.3 0.0 copy-start.1
  120.3 12.3 %collective-permute-start.9 = (bf16[8,8,16,2560]{3,2,1,0:T(8,128)(2,1)}, bf16[8,8,16,2560]{3,2,1,0:T(8,128)(2,1)}, u32[]{:S(2)}, u32[]{:S(2)}) collective-permute-start(bf16[8,8,16,2560]{3,2,1,0:T(8,128)(2,1)} %bitcast.20), channel_id=1, source_target_pairs={{0,64},{64,0},{128,192},{192,128},{256,320},{320,256},{384,448},{4... | collective-permute-start | bytes 15728648 | tf_op jit(solution)/shard_map/ppermute | solution.py:41
  132.6 0.0 copy-done.4
  132.6 5.7 %shard_map.105 = (bf16[128,2048]{1,0:T(8,128)(2,1)}, f32[128,512]{1,0:T(8,128)S(1)}, f32[128,512]{1,0:T(8,128)S(1)}) custom-call(s32[1,128]{1,0:T(1,128)S(1)} %copy-done.4, bf16[640,1024]{1,0:T(8,128)(2,1)S(1)} %get-tuple-element.16.f1, bf16[640,1024]{1,0:T(8,128)(2,1)} %copy-done.2, bf16[8,8,16,2560]{3,2,1,0:T(8,128)(2,1)} %bitcast.21), custom_call_target="tpu_custom_call" | custom-call | flops 1500000000 | bytes 8388608 | tf_op jit(solution)/shard_map/pallas_call | solution.py:246
  138.3 0.0 copy-start.3
  138.3 2.2 %collective-permute-start.8 = (f32[128,512]{1,0:T(8,128)S(1)}, f32[128,512]{1,0:T(8,128)S(1)}, u32[]{:S(2)}, u32[]{:S(2)}) collective-permute-start(f32[128,512]{1,0:T(8,128)S(1)} %get-tuple-element.21), channel_id=1, source_target_pairs={{0,64},{64,0},{128,192},{192,128},{256,320},{320,256},{384,448},{4... | collective-permute-start | bytes 786440 | tf_op jit(solution)/shard_map/ppermute | solution.py:41
  140.5 0.7 collective-permute-done.9.theirs
  141.2 0.0 copy-done.1
  141.2 3.5 %shard_map.106.p1 = bf16[1024,1024]{1,0:T(8,128)(2,1)S(1)} custom-call(bf16[8,8,16,2560]{3,2,1,0:T(8,128)(2,1)S(1)} %bitcast.22, bf16[8,8,16,2560]{3,2,1,0:T(8,128)(2,1)} %collective-permute-done.9.theirs), custom_call_target="tpu_custom_call" | custom-call | flops 1400000000 | bytes 8388608 | tf_op jit(solution)/shard_map/pallas_call | solution.py:256
  144.7 0.0 collective-permute-done.8.received
  144.7 0.0 copy-done.3
  144.7 4.4 %shard_map.107 = bf16[128,2048]{1,0:T(8,128)(2,1)} custom-call(bf16[128,2048]{1,0:T(8,128)(2,1)S(1)} %bitcast.24, f32[128,512]{1,0:T(8,128)S(1)} %get-tuple-element.20.own, f32[128,512]{1,0:T(8,128)S(1)} %collective-permute-done.8.received, bf16[1024,1024]{1,0:T(8,128)(2,1)S(1)} %shard_map.106.p1, bf16[8,8,16,2560]{3,2,1,0:T(8,128)(2,1)S(1)} %bitcast.23, ...), custom_call_target="tpu_custom_call" | custom-call | flops 800000000 | bytes 8388608 | tf_op jit(solution)/shard_map/pallas_call | solution.py:264
  (4 shorter events, 0.1 us)
Async XLA Ops:
  7.2 2.3 %copy-start = (bf16[4,2,16,1024]{3,2,1,0:T(8,128)(2,1)S(1)}, bf16[4,2,16,1024]{3,2,1,0:T(8,128)(2,1)}, u32[]{:S(2)}) copy-start(bf16[4,2,16,1024]{3,2,1,0:T(8,128)(2,1)} %param.17) | copy-start | bytes 786436
  7.2 113.1 %all-gather.3.cloned.1.call-start = ((), (), s32[]{:S(2)}) async-start(), calls=%async_computation.1 | async-start | bytes 5324800 | tf_op jit(solution)/shard_map/all_gather | solution.py:222
  10.9 102.9 %copy-start.5 = (bf16[1,128,2048]{2,1,0:T(8,128)(2,1)S(1)}, bf16[1,128,2048]{2,1,0:T(8,128)(2,1)}, u32[]{:S(2)}) copy-start(bf16[1,128,2048]{2,1,0:T(8,128)(2,1)} %param.9) | copy-start | bytes 1572868
  10.9 102.9 %copy-start.6 = (s32[1,1,2]{2,1,0:T(1,128)S(1)}, s32[1,1,2]{2,1,0:T(1,128)}, u32[]{:S(2)}) copy-start(s32[1,1,2]{2,1,0:T(1,128)} %mask.1) | copy-start | bytes 28
  36.8 15.1 %collective-permute-start.3 = (bf16[8,3,16,1024]{3,2,1,0:T(8,128)(2,1)S(1)}, bf16[8,3,16,1024]{3,2,1,0:T(8,128)(2,1)S(1)}, u32[]{:S(2)}, u32[]{:S(2)}) collective-permute-start(bf16[8,3,16,1024]{3,2,1,0:T(8,128)(2,1)S(1)} %all_to_all.5.refs_0_), channel_id=1, source_target_pairs={{0,56},{1,57},{2,58},{3,59},{4,60},{5,61},{6,62},{7,63},{8,0},{9,1... | collective-permute-start | bytes 2359304 | tf_op jit(solution)/shard_map/ppermute | solution.py:231
  41.9 15.4 %collective-permute-start = (bf16[8,3,16,1024]{3,2,1,0:T(8,128)(2,1)S(1)}, bf16[8,3,16,1024]{3,2,1,0:T(8,128)(2,1)S(1)}, u32[]{:S(2)}, u32[]{:S(2)}) collective-permute-start(bf16[8,3,16,1024]{3,2,1,0:T(8,128)(2,1)S(1)} %all_to_all.5.refs_0_), channel_id=1, source_target_pairs={{0,8},{1,9},{2,10},{3,11},{4,12},{5,13},{6,14},{7,15},{8,16},{9,17... | collective-permute-start | bytes 2359304 | tf_op jit(solution)/shard_map/ppermute | solution.py:230
  51.9 14.4 %collective-permute-start.4 = (bf16[8,3,16,1024]{3,2,1,0:T(8,128)(2,1)S(1)}, bf16[8,3,16,1024]{3,2,1,0:T(8,128)(2,1)S(1)}, u32[]{:S(2)}, u32[]{:S(2)}) collective-permute-start(bf16[8,3,16,1024]{3,2,1,0:T(8,128)(2,1)S(1)} %collective-permute-done.3.refs_4_), channel_id=1, source_target_pairs={{0,56},{1,57},{2,58},{3,59},{4,60},{5,61},{6,62},{7,63},{8,0},{9,1... | collective-permute-start | bytes 2359304 | tf_op jit(solution)/shard_map/ppermute | solution.py:231
  57.3 14.3 %collective-permute-start.1 = (bf16[8,3,16,1024]{3,2,1,0:T(8,128)(2,1)S(1)}, bf16[8,3,16,1024]{3,2,1,0:T(8,128)(2,1)S(1)}, u32[]{:S(2)}, u32[]{:S(2)}) collective-permute-start(bf16[8,3,16,1024]{3,2,1,0:T(8,128)(2,1)S(1)} %collective-permute-done.refs_1_), channel_id=1, source_target_pairs={{0,8},{1,9},{2,10},{3,11},{4,12},{5,13},{6,14},{7,15},{8,16},{9,17... | collective-permute-start | bytes 2359304 | tf_op jit(solution)/shard_map/ppermute | solution.py:230
  66.3 27.4 %collective-permute-start.5 = (bf16[8,3,16,1024]{3,2,1,0:T(8,128)(2,1)S(1)}, bf16[8,3,16,1024]{3,2,1,0:T(8,128)(2,1)S(1)}, u32[]{:S(2)}, u32[]{:S(2)}) collective-permute-start(bf16[8,3,16,1024]{3,2,1,0:T(8,128)(2,1)S(1)} %collective-permute-done.4.refs_5_), channel_id=1, source_target_pairs={{0,56},{1,57},{2,58},{3,59},{4,60},{5,61},{6,62},{7,63},{8,0},{9,1... | collective-permute-start | bytes 2359304 | tf_op jit(solution)/shard_map/ppermute | solution.py:231
  71.6 27.6 %collective-permute-start.2 = (bf16[8,3,16,1024]{3,2,1,0:T(8,128)(2,1)S(1)}, bf16[8,3,16,1024]{3,2,1,0:T(8,128)(2,1)S(1)}, u32[]{:S(2)}, u32[]{:S(2)}) collective-permute-start(bf16[8,3,16,1024]{3,2,1,0:T(8,128)(2,1)S(1)} %collective-permute-done.1.refs_2_), channel_id=1, source_target_pairs={{0,8},{1,9},{2,10},{3,11},{4,12},{5,13},{6,14},{7,15},{8,16},{9,17... | collective-permute-start | bytes 2359304 | tf_op jit(solution)/shard_map/ppermute | solution.py:230
  93.7 17.1 %collective-permute-start.7 = (bf16[4,3,16,1024]{3,2,1,0:T(8,128)(2,1)S(1)}, bf16[4,3,16,1024]{3,2,1,0:T(8,128)(2,1)S(1)}, u32[]{:S(2)}, u32[]{:S(2)}) collective-permute-start(bf16[4,3,16,1024]{3,2,1,0:T(8,128)(2,1)S(1)} %slice.25), channel_id=1, source_target_pairs={{0,56},{1,57},{2,58},{3,59},{4,60},{5,61},{6,62},{7,63},{8,0},{9,1... | collective-permute-start | bytes 1179656 | tf_op jit(solution)/shard_map/ppermute | solution.py:232
  99.2 14.6 %collective-permute-start.6 = (bf16[4,3,16,1024]{3,2,1,0:T(8,128)(2,1)S(1)}, bf16[4,3,16,1024]{3,2,1,0:T(8,128)(2,1)S(1)}, u32[]{:S(2)}, u32[]{:S(2)}) collective-permute-start(bf16[4,3,16,1024]{3,2,1,0:T(8,128)(2,1)S(1)} %slice.24), channel_id=1, source_target_pairs={{0,8},{1,9},{2,10},{3,11},{4,12},{5,13},{6,14},{7,15},{8,16},{9,17... | collective-permute-start | bytes 1179656 | tf_op jit(solution)/shard_map/ppermute | solution.py:232
  113.8 18.8 %copy-start.4 = (s32[1,128]{1,0:T(1,128)S(1)}, s32[1,128]{1,0:T(1,128)}, u32[]{:S(2)}) copy-start(s32[1,128]{1,0:T(1,128)} %row_map.1) | copy-start | bytes 1540
  119.2 1.1 copy-start.2
  120.3 20.9 %copy-start.1 = (bf16[1024,2560]{1,0:T(8,128)(2,1)S(1)}, bf16[1024,2560]{1,0:T(8,128)(2,1)}, u32[]{:S(2)}) copy-start(bf16[1024,2560]{1,0:T(8,128)(2,1)} %all-gather.3.cloned.1.call-done) | copy-start | bytes 15728644
  120.3 20.9 %collective-permute-start.9 = (bf16[8,8,16,2560]{3,2,1,0:T(8,128)(2,1)}, bf16[8,8,16,2560]{3,2,1,0:T(8,128)(2,1)}, u32[]{:S(2)}, u32[]{:S(2)}) collective-permute-start(bf16[8,8,16,2560]{3,2,1,0:T(8,128)(2,1)} %bitcast.20), channel_id=1, source_target_pairs={{0,64},{64,0},{128,192},{192,128},{256,320},{320,256},{384,448},{4... | collective-permute-start | bytes 15728648 | tf_op jit(solution)/shard_map/ppermute | solution.py:41
  138.3 6.4 %copy-start.3 = (bf16[1,128,2048]{2,1,0:T(8,128)(2,1)S(1)}, bf16[1,128,2048]{2,1,0:T(8,128)(2,1)}, u32[]{:S(2)}) copy-start(bf16[1,128,2048]{2,1,0:T(8,128)(2,1)} %param.15) | copy-start | bytes 1572868
  138.3 6.4 %collective-permute-start.8 = (f32[128,512]{1,0:T(8,128)S(1)}, f32[128,512]{1,0:T(8,128)S(1)}, u32[]{:S(2)}, u32[]{:S(2)}) collective-permute-start(f32[128,512]{1,0:T(8,128)S(1)} %get-tuple-element.21), channel_id=1, source_target_pairs={{0,64},{64,0},{128,192},{192,128},{256,320},{320,256},{384,448},{4... | collective-permute-start | bytes 786440 | tf_op jit(solution)/shard_map/ppermute | solution.py:41
Sparse Core Ops, SparseCore 0:
  11.6 101.2 all-gather.2

commit v4 on v3

--- a/solution.py
+++ b/solution.py
@@ -17,7 +17,6 @@
 VMEM = pl.BlockSpec(memory_space=pltpu.VMEM)
 SMEM = pl.BlockSpec(memory_space=pltpu.SMEM)
 ANY = pl.BlockSpec(memory_space=pl.ANY)
-HBM = pl.BlockSpec(memory_space=pltpu.HBM)
 
 
 def lines():
@@ -52,22 +51,40 @@
         out[:, TILE * j : depth] = times_rows(left(depth), rows).astype(BF16)
 
 
-def first_kernel(mask, panels, *refs):
-    blocks, refs = refs[:9], refs[9:]
-    f1, r2, inv0, piv, lnk, p1, x1, x2, sems = refs
+def pack_kernel(links, pivots, inverse, upper_pivots, upper_inverse, out, low, sems):
+    leaf = lax.axis_index("leaf")
+    core, parent = lax.rem(leaf, 2), leaf // 2
+    half = WIDTH // 2
+    part = upper_pivots.at[parent, :, pl.ds(pl.multiple_of(core * half, half), half)]
+    pairs = [
+        (links.at[0], low),
+        (inverse.at[0, 0], out.at[:, pl.ds(0, WIDTH)]),
+        (pivots.at[0], out.at[:, pl.ds(WIDTH, WIDTH)]),
+        (inverse.at[0, 1], out.at[:, pl.ds(3 * WIDTH, WIDTH)]),
+        (upper_inverse.at[parent, core], out.at[:, pl.ds(4 * WIDTH, WIDTH)]),
+        (part, out.at[:, pl.ds(5 * WIDTH, half)]),
+    ]
+    copies = [pltpu.make_async_copy(source, target, sems.at[i]) for i, (source, target) in enumerate(pairs)]
+    for copy in copies:
+        copy.start()
+    copies[0].wait()
+    rows = low[...].astype(F32)
+    out[:, 2 * WIDTH : 3 * WIDTH] = jnp.concatenate([rows[:, :WIDTH], rows[:, WIDTH:]], 0).astype(BF16)
+    for copy in copies[1:]:
+        copy.wait()
+
+
+def arrivals(blocks, targets, sems):
     leaf, col = lax.axis_index("leaf"), lax.axis_index("col")
     core = lax.rem(leaf, 2)
     place = jnp.where(core == 0, col // SIDE, lax.rem(col, SIDE))
-    half = SIDE // 2
-    sources = [(0, 0, SIDE)] + [(-k, 0, SIDE) for k in (1, 2, 3)] + [(k, 0, SIDE) for k in (1, 2, 3)]
-    sources += [(half, 0, half), (half, half, half)]
-    copies = [[], [], []]
-    for i, (block, (offset, first, count)) in enumerate(zip(blocks, sources, strict=True)):
+    copies = [[] for _ in targets]
+    for i, (block, offset) in enumerate(zip(blocks, (0, -1, -2, -3, 1, 2, 3, 4), strict=True)):
         at = lax.rem(place + offset + SIDE, SIDE)
-        for m, target in enumerate((inv0, piv, lnk)):
-            sem = sems.at[i, m]
-            by_z = pltpu.make_async_copy(block.at[:, m], target.at[at, pl.ds(first, count)], sem)
-            by_y = pltpu.make_async_copy(block.at[:, m], target.at[pl.ds(first, count), at], sem)
+        for m, (target, lane) in enumerate(targets):
+            source, sem = block.at[:, :, pl.ds(lane, target.shape[3])], sems.at[i, m]
+            by_z = pltpu.make_async_copy(source, target.at[at], sem)
+            by_y = pltpu.make_async_copy(source, target.at[:, at], sem)
 
             @pl.when(core == 0)
             def _():
@@ -78,7 +95,20 @@
                 by_y.start()
 
             copies[m].append(by_z)
-
+    return copies
+
+
+def order_kernel(*refs):
+    blocks, (inv1, mine, sems) = refs[:8], refs[8:]
+    for copies in arrivals(blocks, [(inv1, 0), (mine, WIDTH)], sems):
+        for copy in copies:
+            copy.wait()
+
+
+def first_kernel(mask, panels, *refs):
+    blocks, refs = refs[:8], refs[8:]
+    f1, r2, inv0, piv, lnk, p1, x1, x2, sems = refs
+    copies = arrivals(blocks, [(inv0, 0), (piv, WIDTH), (lnk, 2 * WIDTH)], sems)
     zero = jnp.zeros((), BF16)
     x1[:ROWS] = jnp.where(mask[0, 0, 0] != 0, panels[:, :WIDTH], zero)
     x2[:ROWS] = jnp.where(mask[0, 0, 1] != 0, panels[:, WIDTH:], zero)
@@ -97,14 +127,11 @@
         r2[:, at] = (x2[:, at].astype(F32) - times_rows(f1[...], p1[at, :])).astype(BF16)
 
 
-def second_kernel(row_map, f1, r2, gathered, factor, own, sent, inv1, f2, placed, contrib, sem):
-    copy = pltpu.make_async_copy(gathered.at[:, :, :, pl.ds(0, WIDTH)], inv1, sem)
-    copy.start()
+def second_kernel(row_map, f1, r2, inv1, factor, own, sent, f2, placed, contrib):
     core = lax.rem(lax.axis_index("leaf"), 2)
     placed[...] = jnp.zeros_like(placed)
     factor[:, :WIDTH] = f1[:ROWS]
     contrib[...] = times_rows(f1[:ROWS], f1[ROWS:])
-    copy.wait()
     times_lower(lambda depth: r2[:, :depth], inv1, f2)
     contrib[...] = -(contrib[...] + times_rows(f2[:ROWS], f2[ROWS:]))
     factor[:, WIDTH:] = f2[:ROWS]
@@ -143,13 +170,13 @@
 def pivot_kernel(mine, theirs, p1, inv0, piv, sems):
     core = lax.rem(lax.axis_index("leaf"), 2)
     half = WIDTH // 2
-    tail = pl.ds(2 * WIDTH, half)
+    tail = pl.ds(WIDTH, half)
     copies = start_from(
         core,
         mine,
         theirs,
         [
-            (True, pl.ds(WIDTH, WIDTH), inv0, sems.at[0]),
+            (True, pl.ds(0, WIDTH), inv0, sems.at[0]),
             (True, tail, piv.at[:, :, :, pl.ds(0, half)], sems.at[1]),
             (False, tail, piv.at[:, :, :, pl.ds(half, half)], sems.at[2]),
         ],
@@ -161,7 +188,7 @@
 
 def parent_kernel(panels, own, received, p1, mine, theirs, factor, inv0, inv1, x1, f1, r2, f2, sems):
     core = lax.rem(lax.axis_index("leaf"), 2)
-    whole = pl.ds(WIDTH, WIDTH)
+    whole = pl.ds(0, WIDTH)
     copies = start_from(
         core, mine, theirs, [(True, whole, inv0, sems.at[0]), (False, whole, inv1, sems.at[1])]
     )
@@ -186,11 +213,11 @@
     return pltpu.VMEM(shape, dtype)
 
 
-def call(kernel, in_specs, outs, scratch, flops, vmem=24):
+def call(kernel, in_specs, outs, scratch, flops, vmem=24, out_spec=VMEM):
     return pl.pallas_call(
         kernel,
         in_specs=in_specs,
-        out_specs=tuple(VMEM for _ in outs),
+        out_specs=tuple(out_spec for _ in outs),
         out_shape=tuple(jax.ShapeDtypeStruct(shape, dtype) for shape, dtype in outs),
         scratch_shapes=scratch,
         compiler_params=pltpu.CompilerParams(vmem_limit_bytes=vmem << 20),
@@ -209,65 +236,80 @@
     parent_pivots,
     parent_inverse,
 ):
-    leaf = lax.axis_index("leaf")
-    core, parent = leaf % 2, leaf // 2
     half = WIDTH // 2
-    my_inverse = lax.dynamic_slice(parent_inverse, (parent, core, 0, 0), (1, 1, 16, WIDTH))[0, 0]
-    my_pivots = lax.dynamic_slice(parent_pivots, (parent, 0, core * half), (1, 16, half))[0]
-    packed = jnp.concatenate([child_inverse[0, 1], my_inverse, my_pivots], 1)
-    links = jnp.concatenate([child_links[0, :, :WIDTH], child_links[0, :, WIDTH:]], 0)
-    message = jnp.stack([child_inverse[0, 0], child_pivots[0], links], 0)
-    packed, message = lax.optimization_barrier((packed, message))
-
-    gathered = lax.all_gather(packed, "col", axis=0, tiled=False)
+    (message,) = call(
+        pack_kernel,
+        [ANY] * 5,
+        [((16, 5 * WIDTH + half), BF16)],
+        [matrix(8, 2 * WIDTH), pltpu.SemaphoreType.DMA((6,))],
+        1_000_000,
+        60,
+    )(child_links, child_pivots, child_inverse, parent_pivots, parent_inverse)
     block = lax.all_to_all(
         jnp.broadcast_to(message[None], (SIDE, *message.shape)), AXES, 0, 0, axis_index_groups=lines()
     )
     up = functools.partial(lax.ppermute, axis_name=AXES, perm=ring(1))
     down = functools.partial(lax.ppermute, axis_name=AXES, perm=ring(-1))
-    ups, downs = [block], [block]
-    for _ in range(3):
-        ups.append(up(ups[-1]))
-        downs.append(down(downs[-1]))
-    last_up, last_down = up(ups[-1][: SIDE // 2]), down(downs[-1][SIDE // 2 :])
+    first, second = block[:, :, : 3 * WIDTH], block[:, :, 3 * WIDTH :]
+    first_blocks, second_blocks = [first], [second]
+    a, b = (first, first), (second, second)
+    for step in range(3):
+        a, last = (up(a[0]), down(a[1])), b
+        b = (up(b[0]), down(b[1]))
+        if step:
+            *a, _, _ = lax.optimization_barrier((*a, *last))
+        *b, a0, a1 = lax.optimization_barrier((*b, *a))
+        first_blocks += [a0, a1]
+        second_blocks += list(b)
+    last, farthest = lax.optimization_barrier((up(a[0]), down(b[1])))
+    first_blocks.append(last)
+    first_blocks, second_blocks = (
+        [blocks[i] for i in (0, 1, 3, 5, 2, 4, 6)] + blocks[7:] for blocks in (first_blocks, second_blocks)
+    )
 
     weight = (SIDE, SIDE, 16, WIDTH)
     stack = ROWS + LINK
     f1, r2 = call(
         first_kernel,
-        [SMEM, VMEM] + [ANY] * 9,
+        [SMEM, VMEM] + [ANY] * 8,
         [((stack, WIDTH), BF16)] * 2,
-        [matrix(*weight)] * 3 + [matrix(WIDTH, WIDTH)] + [matrix(stack, WIDTH)] * 2 + [pltpu.SemaphoreType.DMA((9, 3))],
+        [matrix(*weight)] * 3 + [matrix(WIDTH, WIDTH)] + [matrix(stack, WIDTH)] * 2 + [pltpu.SemaphoreType.DMA((8, 3))],
         5_000_000_000,
-    )(block_mask, child_panels[0], *ups, *downs[1:], last_up, last_down)
-    gathered, f1, r2 = lax.optimization_barrier((gathered, f1, r2))
-    mine = gathered.reshape(SIDE, SIDE, 16, 2 * WIDTH + half)
+    )(block_mask, child_panels[0], *first_blocks)
+    inv1, mine = call(
+        order_kernel,
+        [ANY] * 8,
+        [(weight, BF16), ((SIDE, SIDE, 16, WIDTH + half), BF16)],
+        [pltpu.SemaphoreType.DMA((8, 2))],
+        1_000_000,
+        16,
+        ANY,
+    )(*second_blocks, farthest)
     theirs = swap_cores(mine)
     child_factor, own, sent = call(
         second_kernel,
-        [SMEM, VMEM, VMEM, HBM],
+        [SMEM, VMEM, VMEM, VMEM],
         [((ROWS, 2 * WIDTH), BF16), ((ROWS, LINK), F32), ((ROWS, LINK), F32)],
-        [matrix(*weight), matrix(stack, WIDTH), matrix(2 * ROWS, LINK, dtype=F32), matrix(ROWS, LINK, dtype=F32)]
-        + [pltpu.SemaphoreType.DMA(())],
+        [matrix(stack, WIDTH), matrix(2 * ROWS, LINK, dtype=F32), matrix(ROWS, LINK, dtype=F32)],
         1_500_000_000,
-        52,
-    )(row_map, f1, r2, mine)
+        24,
+    )(row_map, f1, r2, inv1)
     received = swap_cores(sent)
     (parent_p1,) = call(
         pivot_kernel,
-        [HBM, ANY],
+        [ANY, ANY],
         [((WIDTH, WIDTH), BF16)],
         [matrix(*weight)] * 2 + [pltpu.SemaphoreType.DMA((3,))],
         1_400_000_000,
-        36,
+        24,
     )(mine, theirs)
     (parent_factor,) = call(
         parent_kernel,
-        [VMEM] * 4 + [HBM, ANY],
+        [VMEM] * 4 + [ANY, ANY],
         [((ROWS, 2 * WIDTH), BF16)],
         [matrix(*weight)] * 2 + [matrix(ROWS, WIDTH)] * 4 + [pltpu.SemaphoreType.DMA((2,))],
         800_000_000,
-        36,
+        24,
     )(parent_panels[0], own, received, parent_p1, mine, theirs)
     return (child_factor[None], parent_factor[None])
 

time: 157 us -> 134 us (0.85)
  waiting for transfers between devices: 48.8 us -> 22.4 us
  starting transfers between devices: 43.3 us -> 59.1 us
  between operations: 14.3 us -> 0.9 us
  blocking collectives: 25.7 us -> 32.6 us
  local copies, waits for them, and re-layouts: 3.45 us -> 1.15 us
  Pallas kernels: 19 us -> 16.9 us
    ppermute x8 -> x14, waiting for transfers between devices: 48 us -> 22.4 us  [the longest x6 10.7 us: local(): b = (up(b[0]), down(b[1]))]
    ppermute x8 -> x14, starting transfers between devices: 28.8 us -> 47.5 us  [the longest x6 20.7 us: local(): a, last = ((up(a[0]), down(a[1])), b)]
    all_to_all x1, blocking collectives: 25.7 us -> 32.6 us  [local(): lax.all_to_all(jnp.broadcast_to(message[None], (SIDE, *message.shape)), A...]
    ppermute x2, starting transfers between devices: 14.5 us -> 11.6 us  [swap_cores(): return lax.ppermute(value, 'leaf', [(i, i ^ 1) for i in range(8)])]
    pallas_call x4 -> x6, Pallas kernels: 19 us -> 16.9 us  [the longest x1 5.22 us: local(): call(first_kernel, [SMEM, VMEM] + [ANY] * 8, [((stack, WIDTH), BF16)] * 2...]
  transfers between devices with their start and end apart: 11 -> 16, of which waited for: 7 -> 7; matrix products, arithmetic and copies ran while one was open for 0% -> 0% of each run, Pallas kernels for 9% -> 8%
where the time goes in v4:
time: 134 us; the launch traced here: 133 us
  starting transfers between devices  59.1 us (44%)
  blocking collectives  32.6 us (24%)
  waiting for transfers between devices  22.4 us (17%)
  Pallas kernels  16.9 us (13%)
    all_to_all x1, blocking collectives, local(): lax.all_to_all(jnp.broadcast_to(message[None], (SIDE, *message.shape)), A...  32.6 us
    ppermute x6, starting transfers between devices, local(): a, last = ((up(a[0]), down(a[1])), b)  20.7 us
    ppermute x6, starting transfers between devices, local(): b = (up(b[0]), down(b[1]))  19.6 us
    ppermute x2, starting transfers between devices, swap_cores(): return lax.ppermute(value, 'leaf', [(i, i ^ 1) for i in range(8)])  11.6 us
    ppermute x6, waiting for transfers between devices, local(): b = (up(b[0]), down(b[1]))  10.7 us
    ppermute x2, waiting for transfers between devices, local(): last, farthest = lax.optimization_barrier((up(a[0]), down(b[1])))  7.51 us
    ppermute x2, starting transfers between devices, local(): last, farthest = lax.optimization_barrier((up(a[0]), down(b[1])))  7.18 us
    pallas_call x1, Pallas kernels, local(): call(first_kernel, [SMEM, VMEM] + [ANY] * 8, [((stack, WIDTH), BF16)] * 2...  5.22 us
  transfers between devices with their start and end apart: 16, of which 7 were waited for; matrix products, arithmetic and copies ran while one was open for 0% of the time, Pallas kernels for 8%

profile of v4, /device:TPU:1, one launch (start us, length us, event | category | flops | bytes accessed | tf_op | source)
XLA Modules:
  0.0 133.0 jit_solution(16615650511859897410)
XLA Ops:
  0.6 1.6 %shard_map.104 = bf16[16,5632]{1,0:T(8,128)(2,1)} custom-call(bf16[1,8,2048]{2,1,0:T(8,128)(2,1)} %links.1, bf16[1,16,1024]{2,1,0:T(8,128)(2,1)} %pivots.1, bf16[1,2,16,1024]{3,2,1,0:T(8,128)(2,1)} %inverse.1, bf16[4,16,1024]{2,1,0:T(8,128)(2,1)} %upper_pivots.1, bf16[4,2,16,1024]{3,2,1,0:T(8,128)(2,1)} %upper_inverse.1), custom_call_target="tpu_custom_call" | custom-call | flops 1000000 | bytes 8388608 | tf_op jit(solution)/shard_map/pallas_call | solution.py:240
  2.2 1.0 broadcast_in_dim.12
  3.2 32.6 %all_to_all.5 = bf16[8,16,5632]{2,1,0:T(8,128)(2,1)S(1)} all-to-all(bf16[8,16,5632]{2,1,0:T(8,128)(2,1)S(1)} %broadcast_in_dim.12), channel_id=1, replica_groups={{0,1,2,3,4,5,6,7},{8,9,10,11,12,13,14,15},{16,17,18,19,20,21,22,23},{24..., dimensions={0} | all-to-all | bytes 2883584 | tf_op jit(solution)/shard_map/all_to_all | solution.py:248
  35.8 0.1 slice.8.refs_0_
  35.9 5.1 %collective-permute-start.3 = (bf16[8,16,3072]{2,1,0:T(8,128)(2,1)S(1)}, bf16[8,16,3072]{2,1,0:T(8,128)(2,1)S(1)}, u32[]{:S(2)}, u32[]{:S(2)}) collective-permute-start(bf16[8,16,3072]{2,1,0:T(8,128)(2,1)S(1)} %slice.8.refs_0_), channel_id=1, source_target_pairs={{0,56},{1,57},{2,58},{3,59},{4,60},{5,61},{6,62},{7,63},{8,0},{9,1... | collective-permute-start | bytes 2359304 | tf_op jit(solution)/shard_map/ppermute | solution.py:257
  41.0 1.9 %collective-permute-start.2 = (bf16[8,16,3072]{2,1,0:T(8,128)(2,1)S(1)}, bf16[8,16,3072]{2,1,0:T(8,128)(2,1)S(1)}, u32[]{:S(2)}, u32[]{:S(2)}) collective-permute-start(bf16[8,16,3072]{2,1,0:T(8,128)(2,1)S(1)} %slice.8.refs_0_), channel_id=1, source_target_pairs={{0,8},{1,9},{2,10},{3,11},{4,12},{5,13},{6,14},{7,15},{8,16},{9,17... | collective-permute-start | bytes 2359304 | tf_op jit(solution)/shard_map/ppermute | solution.py:257
  43.0 0.0 copy-start.1
  43.0 0.0 copy-start.2
  43.0 4.7 %collective-permute-start.1 = (bf16[8,16,2560]{2,1,0:T(8,128)(2,1)S(1)}, bf16[8,16,2560]{2,1,0:T(8,128)(2,1)S(1)}, u32[]{:S(2)}, u32[]{:S(2)}) collective-permute-start(bf16[8,16,2560]{2,1,0:T(8,128)(2,1)S(1)} %slice.9.refs_0_), channel_id=1, source_target_pairs={{0,56},{1,57},{2,58},{3,59},{4,60},{5,61},{6,62},{7,63},{8,0},{9,1... | collective-permute-start | bytes 1966088 | tf_op jit(solution)/shard_map/ppermute | solution.py:258
  47.7 1.9 %collective-permute-start = (bf16[8,16,2560]{2,1,0:T(8,128)(2,1)S(1)}, bf16[8,16,2560]{2,1,0:T(8,128)(2,1)S(1)}, u32[]{:S(2)}, u32[]{:S(2)}) collective-permute-start(bf16[8,16,2560]{2,1,0:T(8,128)(2,1)S(1)} %slice.9.refs_0_), channel_id=1, source_target_pairs={{0,8},{1,9},{2,10},{3,11},{4,12},{5,13},{6,14},{7,15},{8,16},{9,17... | collective-permute-start | bytes 1966088 | tf_op jit(solution)/shard_map/ppermute | solution.py:258
  49.7 0.3 collective-permute-done.3.refs_4_
  49.9 5.3 %collective-permute-start.7 = (bf16[8,16,3072]{2,1,0:T(8,128)(2,1)S(1)}, bf16[8,16,3072]{2,1,0:T(8,128)(2,1)S(1)}, u32[]{:S(2)}, u32[]{:S(2)}) collective-permute-start(bf16[8,16,3072]{2,1,0:T(8,128)(2,1)S(1)} %collective-permute-done.3.refs_4_), channel_id=1, source_target_pairs={{0,56},{1,57},{2,58},{3,59},{4,60},{5,61},{6,62},{7,63},{8,0},{9,1... | collective-permute-start | bytes 2359304 | tf_op jit(solution)/shard_map/ppermute | solution.py:257
  55.3 0.0 collective-permute-done.2.refs_1_
  55.3 1.9 %collective-permute-start.6 = (bf16[8,16,3072]{2,1,0:T(8,128)(2,1)S(1)}, bf16[8,16,3072]{2,1,0:T(8,128)(2,1)S(1)}, u32[]{:S(2)}, u32[]{:S(2)}) collective-permute-start(bf16[8,16,3072]{2,1,0:T(8,128)(2,1)S(1)} %collective-permute-done.2.refs_1_), channel_id=1, source_target_pairs={{0,8},{1,9},{2,10},{3,11},{4,12},{5,13},{6,14},{7,15},{8,16},{9,17... | collective-permute-start | bytes 2359304 | tf_op jit(solution)/shard_map/ppermute | solution.py:257
  57.2 0.0 collective-permute-done.1.refs_4_
  57.2 5.1 %collective-permute-done.refs_1_ = bf16[8,16,2560]{2,1,0:T(8,128)(2,1)S(1)} collective-permute-done((bf16[8,16,2560]{2,1,0:T(8,128)(2,1)S(1)}, bf16[8,16,2560]{2,1,0:T(8,128)(2,1)S(1)}, u32[]{:S(2)}, u32[]{:S(2)}) %collective-permute-start) | collective-permute-done | bytes 655392 | tf_op jit(solution)/shard_map/ppermute | solution.py:258
  62.3 1.9 %collective-permute-start.4 = (bf16[8,16,2560]{2,1,0:T(8,128)(2,1)S(1)}, bf16[8,16,2560]{2,1,0:T(8,128)(2,1)S(1)}, u32[]{:S(2)}, u32[]{:S(2)}) collective-permute-start(bf16[8,16,2560]{2,1,0:T(8,128)(2,1)S(1)} %collective-permute-done.refs_1_), channel_id=1, source_target_pairs={{0,8},{1,9},{2,10},{3,11},{4,12},{5,13},{6,14},{7,15},{8,16},{9,17... | collective-permute-start | bytes 1966088 | tf_op jit(solution)/shard_map/ppermute | solution.py:258
  64.2 4.6 %collective-permute-start.5 = (bf16[8,16,2560]{2,1,0:T(8,128)(2,1)S(1)}, bf16[8,16,2560]{2,1,0:T(8,128)(2,1)S(1)}, u32[]{:S(2)}, u32[]{:S(2)}) collective-permute-start(bf16[8,16,2560]{2,1,0:T(8,128)(2,1)S(1)} %collective-permute-done.1.refs_4_), channel_id=1, source_target_pairs={{0,56},{1,57},{2,58},{3,59},{4,60},{5,61},{6,62},{7,63},{8,0},{9,1... | collective-permute-start | bytes 1966088 | tf_op jit(solution)/shard_map/ppermute | solution.py:258
  68.8 0.0 collective-permute-done.7.refs_5_
  68.8 1.9 %collective-permute-done.6.refs_2_ = bf16[8,16,3072]{2,1,0:T(8,128)(2,1)S(1)} collective-permute-done((bf16[8,16,3072]{2,1,0:T(8,128)(2,1)S(1)}, bf16[8,16,3072]{2,1,0:T(8,128)(2,1)S(1)}, u32[]{:S(2)}, u32[]{:S(2)}) %collective-permute-start.6) | collective-permute-done | bytes 786464 | tf_op jit(solution)/shard_map/ppermute | solution.py:257
  70.7 1.9 %collective-permute-start.10 = (bf16[8,16,3072]{2,1,0:T(8,128)(2,1)S(1)}, bf16[8,16,3072]{2,1,0:T(8,128)(2,1)S(1)}, u32[]{:S(2)}, u32[]{:S(2)}) collective-permute-start(bf16[8,16,3072]{2,1,0:T(8,128)(2,1)S(1)} %collective-permute-done.6.refs_2_), channel_id=1, source_target_pairs={{0,8},{1,9},{2,10},{3,11},{4,12},{5,13},{6,14},{7,15},{8,16},{9,17... | collective-permute-start | bytes 2359304 | tf_op jit(solution)/shard_map/ppermute | solution.py:257
  72.6 4.6 %collective-permute-start.11 = (bf16[8,16,3072]{2,1,0:T(8,128)(2,1)S(1)}, bf16[8,16,3072]{2,1,0:T(8,128)(2,1)S(1)}, u32[]{:S(2)}, u32[]{:S(2)}) collective-permute-start(bf16[8,16,3072]{2,1,0:T(8,128)(2,1)S(1)} %collective-permute-done.7.refs_5_), channel_id=1, source_target_pairs={{0,56},{1,57},{2,58},{3,59},{4,60},{5,61},{6,62},{7,63},{8,0},{9,1... | collective-permute-start | bytes 2359304 | tf_op jit(solution)/shard_map/ppermute | solution.py:257
  77.2 0.5 collective-permute-done.4.refs_2_
  77.7 0.0 collective-permute-done.5.refs_5_
  77.7 1.9 %collective-permute-start.8 = (bf16[8,16,2560]{2,1,0:T(8,128)(2,1)S(1)}, bf16[8,16,2560]{2,1,0:T(8,128)(2,1)S(1)}, u32[]{:S(2)}, u32[]{:S(2)}) collective-permute-start(bf16[8,16,2560]{2,1,0:T(8,128)(2,1)S(1)} %collective-permute-done.4.refs_2_), channel_id=1, source_target_pairs={{0,8},{1,9},{2,10},{3,11},{4,12},{5,13},{6,14},{7,15},{8,16},{9,17... | collective-permute-start | bytes 1966088 | tf_op jit(solution)/shard_map/ppermute | solution.py:258
  79.7 4.6 %collective-permute-start.9 = (bf16[8,16,2560]{2,1,0:T(8,128)(2,1)S(1)}, bf16[8,16,2560]{2,1,0:T(8,128)(2,1)S(1)}, u32[]{:S(2)}, u32[]{:S(2)}) collective-permute-start(bf16[8,16,2560]{2,1,0:T(8,128)(2,1)S(1)} %collective-permute-done.5.refs_5_), channel_id=1, source_target_pairs={{0,56},{1,57},{2,58},{3,59},{4,60},{5,61},{6,62},{7,63},{8,0},{9,1... | collective-permute-start | bytes 1966088 | tf_op jit(solution)/shard_map/ppermute | solution.py:258
  84.2 1.9 %collective-permute-done.10.refs_3_ = bf16[8,16,3072]{2,1,0:T(8,128)(2,1)S(1)} collective-permute-done((bf16[8,16,3072]{2,1,0:T(8,128)(2,1)S(1)}, bf16[8,16,3072]{2,1,0:T(8,128)(2,1)S(1)}, u32[]{:S(2)}, u32[]{:S(2)}) %collective-permute-start.10) | collective-permute-done | bytes 786464 | tf_op jit(solution)/shard_map/ppermute | solution.py:257
  86.2 0.0 collective-permute-done.11.refs_6_
  86.2 1.9 %collective-permute-start.12 = (bf16[8,16,3072]{2,1,0:T(8,128)(2,1)S(1)}, bf16[8,16,3072]{2,1,0:T(8,128)(2,1)S(1)}, u32[]{:S(2)}, u32[]{:S(2)}) collective-permute-start(bf16[8,16,3072]{2,1,0:T(8,128)(2,1)S(1)} %collective-permute-done.10.refs_3_), channel_id=1, source_target_pairs={{0,8},{1,9},{2,10},{3,11},{4,12},{5,13},{6,14},{7,15},{8,16},{9,17... | collective-permute-start | bytes 2359304 | tf_op jit(solution)/shard_map/ppermute | solution.py:264
  88.1 5.1 %collective-permute-done.8.refs_3_ = bf16[8,16,2560]{2,1,0:T(8,128)(2,1)S(1)} collective-permute-done((bf16[8,16,2560]{2,1,0:T(8,128)(2,1)S(1)}, bf16[8,16,2560]{2,1,0:T(8,128)(2,1)S(1)}, u32[]{:S(2)}, u32[]{:S(2)}) %collective-permute-start.8) | collective-permute-done | bytes 655392 | tf_op jit(solution)/shard_map/ppermute | solution.py:258
  93.2 0.0 collective-permute-done.9.refs_6_
  93.2 5.3 %collective-permute-start.13 = (bf16[8,16,2560]{2,1,0:T(8,128)(2,1)S(1)}, bf16[8,16,2560]{2,1,0:T(8,128)(2,1)S(1)}, u32[]{:S(2)}, u32[]{:S(2)}) collective-permute-start(bf16[8,16,2560]{2,1,0:T(8,128)(2,1)S(1)} %collective-permute-done.9.refs_6_), channel_id=1, source_target_pairs={{0,56},{1,57},{2,58},{3,59},{4,60},{5,61},{6,62},{7,63},{8,0},{9,1... | collective-permute-start | bytes 1966088 | tf_op jit(solution)/shard_map/ppermute | solution.py:264
  98.5 7.5 %collective-permute-done.13.refs_7_ = bf16[8,16,2560]{2,1,0:T(8,128)(2,1)S(1)} collective-permute-done((bf16[8,16,2560]{2,1,0:T(8,128)(2,1)S(1)}, bf16[8,16,2560]{2,1,0:T(8,128)(2,1)S(1)}, u32[]{:S(2)}, u32[]{:S(2)}) %collective-permute-start.13) | collective-permute-done | bytes 655392 | tf_op jit(solution)/shard_map/ppermute | solution.py:264
  106.0 0.0 collective-permute-done.12.refs_7_
  106.0 0.6 shard_map.106
  106.6 9.5 %collective-permute-start.15 = (bf16[8,8,16,1536]{3,2,1,0:T(8,128)(2,1)S(1)}, bf16[8,8,16,1536]{3,2,1,0:T(8,128)(2,1)S(1)}, u32[]{:S(2)}, u32[]{:S(2)}) collective-permute-start(bf16[8,8,16,1536]{3,2,1,0:T(8,128)(2,1)S(1)} %get-tuple-element.51.mine), channel_id=1, source_target_pairs={{0,64},{64,0},{128,192},{192,128},{256,320},{320,256},{384,448},{4... | collective-permute-start | bytes 9437192 | tf_op jit(solution)/shard_map/ppermute | solution.py:40
  116.1 0.0 copy-done.1
  116.2 0.0 copy-done.2
  116.2 0.0 copy-start.3
  116.2 5.2 %shard_map.105 = (bf16[640,1024]{1,0:T(8,128)(2,1)S(1)}, bf16[640,1024]{1,0:T(8,128)(2,1)S(1)}) custom-call(s32[1,1,2]{2,1,0:T(1,128)S(1)} %copy-done.2, bf16[128,2048]{1,0:T(8,128)(2,1)S(1)} %bitcast.5, bf16[8,16,3072]{2,1,0:T(8,128)(2,1)S(1)} %slice.8.refs_0_, bf16[8,16,3072]{2,1,0:T(8,128)(2,1)S(1)} %collective-permute-done.2.refs_1_, ...), custom_call_target="tpu_custom_call" | custom-call | flops 5000000000 | bytes 8388608 | tf_op jit(solution)/shard_map/pallas_call | solution.py:272
  121.4 0.0 copy-done.3
  121.4 3.7 %shard_map.107 = (bf16[128,2048]{1,0:T(8,128)(2,1)}, f32[128,512]{1,0:T(8,128)S(1)}, f32[128,512]{1,0:T(8,128)S(1)}) custom-call(s32[1,128]{1,0:T(1,128)S(1)} %copy-done.3, bf16[640,1024]{1,0:T(8,128)(2,1)S(1)} %get-tuple-element.43.f1, bf16[640,1024]{1,0:T(8,128)(2,1)S(1)} %get-tuple-element.44.r2, bf16[8,8,16,1024]{3,2,1,0:T(8,128)(2,1)S(1)} %get-tuple-element.47.inv1), custom_call_target="tpu_custom_call" | custom-call | flops 1500000000 | bytes 8388608 | tf_op jit(solution)/shard_map/pallas_call | solution.py:289
  125.1 0.0 copy-start
  125.1 2.1 %collective-permute-start.14 = (f32[128,512]{1,0:T(8,128)S(1)}, f32[128,512]{1,0:T(8,128)S(1)}, u32[]{:S(2)}, u32[]{:S(2)}) collective-permute-start(f32[128,512]{1,0:T(8,128)S(1)} %get-tuple-element.50), channel_id=1, source_target_pairs={{0,64},{64,0},{128,192},{192,128},{256,320},{320,256},{384,448},{4... | collective-permute-start | bytes 786440 | tf_op jit(solution)/shard_map/ppermute | solution.py:40
  127.1 0.0 collective-permute-done.15.theirs
  127.2 2.3 %shard_map.108.p1 = bf16[1024,1024]{1,0:T(8,128)(2,1)S(1)} custom-call(bf16[8,8,16,1536]{3,2,1,0:T(8,128)(2,1)S(1)} %get-tuple-element.51.mine, bf16[8,8,16,1536]{3,2,1,0:T(8,128)(2,1)S(1)} %collective-permute-done.15.theirs), custom_call_target="tpu_custom_call" | custom-call | flops 1400000000 | bytes 8388608 | tf_op jit(solution)/shard_map/pallas_call | solution.py:298
  129.4 0.0 collective-permute-done.14.received
  129.4 0.0 copy-done
  129.5 3.6 %shard_map.109 = bf16[128,2048]{1,0:T(8,128)(2,1)} custom-call(bf16[128,2048]{1,0:T(8,128)(2,1)S(1)} %bitcast.4, f32[128,512]{1,0:T(8,128)S(1)} %get-tuple-element.49.own, f32[128,512]{1,0:T(8,128)S(1)} %collective-permute-done.14.received, bf16[1024,1024]{1,0:T(8,128)(2,1)S(1)} %shard_map.108.p1, bf16[8,8,16,1536]{3,2,1,0:T(8,128)(2,1)S(1)} %get-tuple-element.51.mine, ...), custom_call_target="tpu_custom_call" | custom-call | flops 800000000 | bytes 8388608 | tf_op jit(solution)/shard_map/pallas_call | solution.py:306
  (1 shorter events, 0.0 us)
Async XLA Ops:
  35.9 14.0 %collective-permute-start.3 = (bf16[8,16,3072]{2,1,0:T(8,128)(2,1)S(1)}, bf16[8,16,3072]{2,1,0:T(8,128)(2,1)S(1)}, u32[]{:S(2)}, u32[]{:S(2)}) collective-permute-start(bf16[8,16,3072]{2,1,0:T(8,128)(2,1)S(1)} %slice.8.refs_0_), channel_id=1, source_target_pairs={{0,56},{1,57},{2,58},{3,59},{4,60},{5,61},{6,62},{7,63},{8,0},{9,1... | collective-permute-start | bytes 2359304 | tf_op jit(solution)/shard_map/ppermute | solution.py:257
  41.0 14.2 %collective-permute-start.2 = (bf16[8,16,3072]{2,1,0:T(8,128)(2,1)S(1)}, bf16[8,16,3072]{2,1,0:T(8,128)(2,1)S(1)}, u32[]{:S(2)}, u32[]{:S(2)}) collective-permute-start(bf16[8,16,3072]{2,1,0:T(8,128)(2,1)S(1)} %slice.8.refs_0_), channel_id=1, source_target_pairs={{0,8},{1,9},{2,10},{3,11},{4,12},{5,13},{6,14},{7,15},{8,16},{9,17... | collective-permute-start | bytes 2359304 | tf_op jit(solution)/shard_map/ppermute | solution.py:257
  43.0 73.1 %copy-start.1 = (bf16[1,128,2048]{2,1,0:T(8,128)(2,1)S(1)}, bf16[1,128,2048]{2,1,0:T(8,128)(2,1)}, u32[]{:S(2)}) copy-start(bf16[1,128,2048]{2,1,0:T(8,128)(2,1)} %param.9) | copy-start | bytes 1572868
  43.0 73.1 %copy-start.2 = (s32[1,1,2]{2,1,0:T(1,128)S(1)}, s32[1,1,2]{2,1,0:T(1,128)}, u32[]{:S(2)}) copy-start(s32[1,1,2]{2,1,0:T(1,128)} %mask.1) | copy-start | bytes 28
  43.0 14.2 %collective-permute-start.1 = (bf16[8,16,2560]{2,1,0:T(8,128)(2,1)S(1)}, bf16[8,16,2560]{2,1,0:T(8,128)(2,1)S(1)}, u32[]{:S(2)}, u32[]{:S(2)}) collective-permute-start(bf16[8,16,2560]{2,1,0:T(8,128)(2,1)S(1)} %slice.9.refs_0_), channel_id=1, source_target_pairs={{0,56},{1,57},{2,58},{3,59},{4,60},{5,61},{6,62},{7,63},{8,0},{9,1... | collective-permute-start | bytes 1966088 | tf_op jit(solution)/shard_map/ppermute | solution.py:258
  47.7 14.5 %collective-permute-start = (bf16[8,16,2560]{2,1,0:T(8,128)(2,1)S(1)}, bf16[8,16,2560]{2,1,0:T(8,128)(2,1)S(1)}, u32[]{:S(2)}, u32[]{:S(2)}) collective-permute-start(bf16[8,16,2560]{2,1,0:T(8,128)(2,1)S(1)} %slice.9.refs_0_), channel_id=1, source_target_pairs={{0,8},{1,9},{2,10},{3,11},{4,12},{5,13},{6,14},{7,15},{8,16},{9,17... | collective-permute-start | bytes 1966088 | tf_op jit(solution)/shard_map/ppermute | solution.py:258
  49.9 18.8 %collective-permute-start.7 = (bf16[8,16,3072]{2,1,0:T(8,128)(2,1)S(1)}, bf16[8,16,3072]{2,1,0:T(8,128)(2,1)S(1)}, u32[]{:S(2)}, u32[]{:S(2)}) collective-permute-start(bf16[8,16,3072]{2,1,0:T(8,128)(2,1)S(1)} %collective-permute-done.3.refs_4_), channel_id=1, source_target_pairs={{0,56},{1,57},{2,58},{3,59},{4,60},{5,61},{6,62},{7,63},{8,0},{9,1... | collective-permute-start | bytes 2359304 | tf_op jit(solution)/shard_map/ppermute | solution.py:257
  55.3 15.4 %collective-permute-start.6 = (bf16[8,16,3072]{2,1,0:T(8,128)(2,1)S(1)}, bf16[8,16,3072]{2,1,0:T(8,128)(2,1)S(1)}, u32[]{:S(2)}, u32[]{:S(2)}) collective-permute-start(bf16[8,16,3072]{2,1,0:T(8,128)(2,1)S(1)} %collective-permute-done.2.refs_1_), channel_id=1, source_target_pairs={{0,8},{1,9},{2,10},{3,11},{4,12},{5,13},{6,14},{7,15},{8,16},{9,17... | collective-permute-start | bytes 2359304 | tf_op jit(solution)/shard_map/ppermute | solution.py:257
  62.3 15.4 %collective-permute-start.4 = (bf16[8,16,2560]{2,1,0:T(8,128)(2,1)S(1)}, bf16[8,16,2560]{2,1,0:T(8,128)(2,1)S(1)}, u32[]{:S(2)}, u32[]{:S(2)}) collective-permute-start(bf16[8,16,2560]{2,1,0:T(8,128)(2,1)S(1)} %collective-permute-done.refs_1_), channel_id=1, source_target_pairs={{0,8},{1,9},{2,10},{3,11},{4,12},{5,13},{6,14},{7,15},{8,16},{9,17... | collective-permute-start | bytes 1966088 | tf_op jit(solution)/shard_map/ppermute | solution.py:258
  64.2 13.5 %collective-permute-start.5 = (bf16[8,16,2560]{2,1,0:T(8,128)(2,1)S(1)}, bf16[8,16,2560]{2,1,0:T(8,128)(2,1)S(1)}, u32[]{:S(2)}, u32[]{:S(2)}) collective-permute-start(bf16[8,16,2560]{2,1,0:T(8,128)(2,1)S(1)} %collective-permute-done.1.refs_4_), channel_id=1, source_target_pairs={{0,56},{1,57},{2,58},{3,59},{4,60},{5,61},{6,62},{7,63},{8,0},{9,1... | collective-permute-start | bytes 1966088 | tf_op jit(solution)/shard_map/ppermute | solution.py:258
  70.7 15.4 %collective-permute-start.10 = (bf16[8,16,3072]{2,1,0:T(8,128)(2,1)S(1)}, bf16[8,16,3072]{2,1,0:T(8,128)(2,1)S(1)}, u32[]{:S(2)}, u32[]{:S(2)}) collective-permute-start(bf16[8,16,3072]{2,1,0:T(8,128)(2,1)S(1)} %collective-permute-done.6.refs_2_), channel_id=1, source_target_pairs={{0,8},{1,9},{2,10},{3,11},{4,12},{5,13},{6,14},{7,15},{8,16},{9,17... | collective-permute-start | bytes 2359304 | tf_op jit(solution)/shard_map/ppermute | solution.py:257
  72.6 13.5 %collective-permute-start.11 = (bf16[8,16,3072]{2,1,0:T(8,128)(2,1)S(1)}, bf16[8,16,3072]{2,1,0:T(8,128)(2,1)S(1)}, u32[]{:S(2)}, u32[]{:S(2)}) collective-permute-start(bf16[8,16,3072]{2,1,0:T(8,128)(2,1)S(1)} %collective-permute-done.7.refs_5_), channel_id=1, source_target_pairs={{0,56},{1,57},{2,58},{3,59},{4,60},{5,61},{6,62},{7,63},{8,0},{9,1... | collective-permute-start | bytes 2359304 | tf_op jit(solution)/shard_map/ppermute | solution.py:257
  77.7 15.4 %collective-permute-start.8 = (bf16[8,16,2560]{2,1,0:T(8,128)(2,1)S(1)}, bf16[8,16,2560]{2,1,0:T(8,128)(2,1)S(1)}, u32[]{:S(2)}, u32[]{:S(2)}) collective-permute-start(bf16[8,16,2560]{2,1,0:T(8,128)(2,1)S(1)} %collective-permute-done.4.refs_2_), channel_id=1, source_target_pairs={{0,8},{1,9},{2,10},{3,11},{4,12},{5,13},{6,14},{7,15},{8,16},{9,17... | collective-permute-start | bytes 1966088 | tf_op jit(solution)/shard_map/ppermute | solution.py:258
  79.7 13.5 %collective-permute-start.9 = (bf16[8,16,2560]{2,1,0:T(8,128)(2,1)S(1)}, bf16[8,16,2560]{2,1,0:T(8,128)(2,1)S(1)}, u32[]{:S(2)}, u32[]{:S(2)}) collective-permute-start(bf16[8,16,2560]{2,1,0:T(8,128)(2,1)S(1)} %collective-permute-done.5.refs_5_), channel_id=1, source_target_pairs={{0,56},{1,57},{2,58},{3,59},{4,60},{5,61},{6,62},{7,63},{8,0},{9,1... | collective-permute-start | bytes 1966088 | tf_op jit(solution)/shard_map/ppermute | solution.py:258
  86.2 19.8 %collective-permute-start.12 = (bf16[8,16,3072]{2,1,0:T(8,128)(2,1)S(1)}, bf16[8,16,3072]{2,1,0:T(8,128)(2,1)S(1)}, u32[]{:S(2)}, u32[]{:S(2)}) collective-permute-start(bf16[8,16,3072]{2,1,0:T(8,128)(2,1)S(1)} %collective-permute-done.10.refs_3_), channel_id=1, source_target_pairs={{0,8},{1,9},{2,10},{3,11},{4,12},{5,13},{6,14},{7,15},{8,16},{9,17... | collective-permute-start | bytes 2359304 | tf_op jit(solution)/shard_map/ppermute | solution.py:264
  93.2 12.8 %collective-permute-start.13 = (bf16[8,16,2560]{2,1,0:T(8,128)(2,1)S(1)}, bf16[8,16,2560]{2,1,0:T(8,128)(2,1)S(1)}, u32[]{:S(2)}, u32[]{:S(2)}) collective-permute-start(bf16[8,16,2560]{2,1,0:T(8,128)(2,1)S(1)} %collective-permute-done.9.refs_6_), channel_id=1, source_target_pairs={{0,56},{1,57},{2,58},{3,59},{4,60},{5,61},{6,62},{7,63},{8,0},{9,1... | collective-permute-start | bytes 1966088 | tf_op jit(solution)/shard_map/ppermute | solution.py:264
  106.6 20.5 %collective-permute-start.15 = (bf16[8,8,16,1536]{3,2,1,0:T(8,128)(2,1)S(1)}, bf16[8,8,16,1536]{3,2,1,0:T(8,128)(2,1)S(1)}, u32[]{:S(2)}, u32[]{:S(2)}) collective-permute-start(bf16[8,8,16,1536]{3,2,1,0:T(8,128)(2,1)S(1)} %get-tuple-element.51.mine), channel_id=1, source_target_pairs={{0,64},{64,0},{128,192},{192,128},{256,320},{320,256},{384,448},{4... | collective-permute-start | bytes 9437192 | tf_op jit(solution)/shard_map/ppermute | solution.py:40
  116.2 5.2 %copy-start.3 = (s32[1,128]{1,0:T(1,128)S(1)}, s32[1,128]{1,0:T(1,128)}, u32[]{:S(2)}) copy-start(s32[1,128]{1,0:T(1,128)} %row_map.1) | copy-start | bytes 1540
  125.1 4.4 %copy-start = (bf16[1,128,2048]{2,1,0:T(8,128)(2,1)S(1)}, bf16[1,128,2048]{2,1,0:T(8,128)(2,1)}, u32[]{:S(2)}) copy-start(bf16[1,128,2048]{2,1,0:T(8,128)(2,1)} %param.15) | copy-start | bytes 1572868
  125.1 4.3 %collective-permute-start.14 = (f32[128,512]{1,0:T(8,128)S(1)}, f32[128,512]{1,0:T(8,128)S(1)}, u32[]{:S(2)}, u32[]{:S(2)}) collective-permute-start(f32[128,512]{1,0:T(8,128)S(1)} %get-tuple-element.50), channel_id=1, source_target_pairs={{0,64},{64,0},{128,192},{192,128},{256,320},{320,256},{384,448},{4... | collective-permute-start | bytes 786440 | tf_op jit(solution)/shard_map/ppermute | solution.py:40

commit v5 on v4

--- a/solution.py
+++ b/solution.py
@@ -51,7 +51,7 @@
         out[:, TILE * j : depth] = times_rows(left(depth), rows).astype(BF16)
 
 
-def pack_kernel(links, pivots, inverse, upper_pivots, upper_inverse, out, low, sems):
+def pack_kernel(links, pivots, inverse, upper_pivots, upper_inverse, copied, out, low, sems):
     leaf = lax.axis_index("leaf")
     core, parent = lax.rem(leaf, 2), leaf // 2
     half = WIDTH // 2
@@ -72,6 +72,8 @@
     out[:, 2 * WIDTH : 3 * WIDTH] = jnp.concatenate([rows[:, :WIDTH], rows[:, WIDTH:]], 0).astype(BF16)
     for copy in copies[1:]:
         copy.wait()
+    for i in range(SIDE):
+        copied[i] = out[...]
 
 
 def arrivals(blocks, targets, sems):
@@ -167,7 +169,7 @@
     return copies
 
 
-def pivot_kernel(mine, theirs, p1, inv0, piv, sems):
+def pivot_kernel(mine, theirs, p1, inv0, inv1, piv, sems):
     core = lax.rem(lax.axis_index("leaf"), 2)
     half = WIDTH // 2
     tail = pl.ds(WIDTH, half)
@@ -179,31 +181,27 @@
             (True, pl.ds(0, WIDTH), inv0, sems.at[0]),
             (True, tail, piv.at[:, :, :, pl.ds(0, half)], sems.at[1]),
             (False, tail, piv.at[:, :, :, pl.ds(half, half)], sems.at[2]),
+            (False, pl.ds(0, WIDTH), inv1, sems.at[3]),
         ],
     )
-    for copy in copies:
+    for copy in copies[:3]:
         copy.wait()
     times_lower(lambda depth: piv[:, :, :, :depth].reshape(WIDTH, depth), inv0, p1)
-
-
-def parent_kernel(panels, own, received, p1, mine, theirs, factor, inv0, inv1, x1, f1, r2, f2, sems):
+    copies[3].wait()
+
+
+def parent_kernel(panels, own, received, p1, inv0, inv1, factor, x1, f1, r2, f2):
     core = lax.rem(lax.axis_index("leaf"), 2)
-    whole = pl.ds(0, WIDTH)
-    copies = start_from(
-        core, mine, theirs, [(True, whole, inv0, sems.at[0]), (False, whole, inv1, sems.at[1])]
-    )
     even = core == 0
     left = jnp.where(even, own[...], received[...])
     right = jnp.where(even, received[...], own[...])
     x1[:, :LINK] = (panels[:, :LINK].astype(F32) + left).astype(BF16)
     x1[:, LINK:] = (panels[:, LINK:WIDTH].astype(F32) + right).astype(BF16)
-    copies[0].wait()
     times_lower(lambda depth: x1[:, :depth], inv0, f1)
     for j in range(WIDTH // TILE):
         at = slice(TILE * j, TILE * j + TILE)
         source = panels[:, WIDTH + TILE * j : WIDTH + TILE * j + TILE].astype(F32)
         r2[:, at] = (source - times_rows(f1[...], p1[at, :])).astype(BF16)
-    copies[1].wait()
     times_lower(lambda depth: r2[:, :depth], inv1, f2)
     factor[:, :WIDTH] = f1[...]
     factor[:, WIDTH:] = f2[...]
@@ -221,7 +219,7 @@
         out_shape=tuple(jax.ShapeDtypeStruct(shape, dtype) for shape, dtype in outs),
         scratch_shapes=scratch,
         compiler_params=pltpu.CompilerParams(vmem_limit_bytes=vmem << 20),
-        cost_estimate=pl.CostEstimate(flops=flops, bytes_accessed=8 << 20, transcendentals=0),
+        cost_estimate=pl.CostEstimate(flops=flops, bytes_accessed=min(flops, 8 << 20), transcendentals=0),
     )
 
 
@@ -240,14 +238,12 @@
     (message,) = call(
         pack_kernel,
         [ANY] * 5,
-        [((16, 5 * WIDTH + half), BF16)],
-        [matrix(8, 2 * WIDTH), pltpu.SemaphoreType.DMA((6,))],
+        [((SIDE, 16, 5 * WIDTH + half), BF16)],
+        [matrix(16, 5 * WIDTH + half), matrix(8, 2 * WIDTH), pltpu.SemaphoreType.DMA((6,))],
         1_000_000,
         60,
     )(child_links, child_pivots, child_inverse, parent_pivots, parent_inverse)
-    block = lax.all_to_all(
-        jnp.broadcast_to(message[None], (SIDE, *message.shape)), AXES, 0, 0, axis_index_groups=lines()
-    )
+    block = lax.all_to_all(message, AXES, 0, 0, axis_index_groups=lines())
     up = functools.partial(lax.ppermute, axis_name=AXES, perm=ring(1))
     down = functools.partial(lax.ppermute, axis_name=AXES, perm=ring(-1))
     first, second = block[:, :, : 3 * WIDTH], block[:, :, 3 * WIDTH :]
@@ -261,8 +257,8 @@
         *b, a0, a1 = lax.optimization_barrier((*b, *a))
         first_blocks += [a0, a1]
         second_blocks += list(b)
-    last, farthest = lax.optimization_barrier((up(a[0]), down(b[1])))
-    first_blocks.append(last)
+    first_blocks.append(up(a[0]))
+    farthest = down(b[1])
     first_blocks, second_blocks = (
         [blocks[i] for i in (0, 1, 3, 5, 2, 4, 6)] + blocks[7:] for blocks in (first_blocks, second_blocks)
     )
@@ -274,8 +270,9 @@
         [SMEM, VMEM] + [ANY] * 8,
         [((stack, WIDTH), BF16)] * 2,
         [matrix(*weight)] * 3 + [matrix(WIDTH, WIDTH)] + [matrix(stack, WIDTH)] * 2 + [pltpu.SemaphoreType.DMA((8, 3))],
-        5_000_000_000,
+        1_000,
     )(block_mask, child_panels[0], *first_blocks)
+    farthest, f1, r2 = lax.optimization_barrier((farthest, f1, r2))
     inv1, mine = call(
         order_kernel,
         [ANY] * 8,
@@ -295,22 +292,20 @@
         24,
     )(row_map, f1, r2, inv1)
     received = swap_cores(sent)
-    (parent_p1,) = call(
+    parent_p1, upper_inv0, upper_inv1 = call(
         pivot_kernel,
         [ANY, ANY],
-        [((WIDTH, WIDTH), BF16)],
-        [matrix(*weight)] * 2 + [pltpu.SemaphoreType.DMA((3,))],
+        [((WIDTH, WIDTH), BF16), (weight, BF16), (weight, BF16)],
+        [matrix(*weight), pltpu.SemaphoreType.DMA((4,))],
         1_400_000_000,
-        24,
     )(mine, theirs)
     (parent_factor,) = call(
         parent_kernel,
-        [VMEM] * 4 + [ANY, ANY],
+        [VMEM] * 6,
         [((ROWS, 2 * WIDTH), BF16)],
-        [matrix(*weight)] * 2 + [matrix(ROWS, WIDTH)] * 4 + [pltpu.SemaphoreType.DMA((2,))],
+        [matrix(ROWS, WIDTH)] * 4,
         800_000_000,
-        24,
-    )(parent_panels[0], own, received, parent_p1, mine, theirs)
+    )(parent_panels[0], own, received, parent_p1, upper_inv0, upper_inv1)
     return (child_factor[None], parent_factor[None])
 
 

time: 134 us -> 128 us (0.955)
  waiting for transfers between devices: 22.4 us -> 18.2 us
    ppermute x2, waiting for transfers between devices: 7.51 us -> 3.15 us  [the longest x1 3.15 us: local(): first_blocks.append(up(a[0]))]
  transfers between devices with their start and end apart: 16 -> 16, of which waited for: 7 -> 7; matrix products, arithmetic and copies ran while one was open for 0% -> 0% of each run, Pallas kernels for 8% -> 9%
where the time goes in v5:
time: 128 us; the launch traced here: 127 us
  starting transfers between devices  58 us (45%)
  blocking collectives  33.1 us (26%)
  waiting for transfers between devices  18.2 us (14%)
  Pallas kernels  16.7 us (13%)
    all_to_all x1, blocking collectives, local(): block = lax.all_to_all(message, AXES, 0, 0, axis_index_groups=lines())  33.1 us
    ppermute x6, starting transfers between devices, local(): a, last = ((up(a[0]), down(a[1])), b)  20.6 us
    ppermute x6, starting transfers between devices, local(): b = (up(b[0]), down(b[1]))  19.5 us
    ppermute x2, starting transfers between devices, swap_cores(): return lax.ppermute(value, 'leaf', [(i, i ^ 1) for i in range(8)])  10.8 us
    ppermute x6, waiting for transfers between devices, local(): b = (up(b[0]), down(b[1]))  10.7 us
    ppermute x1, starting transfers between devices, local(): farthest = down(b[1])  5.27 us
    pallas_call x1, Pallas kernels, local(): call(first_kernel, [SMEM, VMEM] + [ANY] * 8, [((stack, WIDTH), BF16)] * 2...  5.22 us
    ppermute x6, waiting for transfers between devices, local(): a, last = ((up(a[0]), down(a[1])), b)  4.28 us
  transfers between devices with their start and end apart: 16, of which 7 were waited for; matrix products, arithmetic and copies ran while one was open for 0% of the time, Pallas kernels for 9%

profile of v5, /device:TPU:1, one launch (start us, length us, event | category | flops | bytes accessed | tf_op | source)
XLA Modules:
  0.0 127.0 jit_solution(2710682954416986393)
XLA Ops:
  0.6 2.1 %shard_map.104 = bf16[8,16,5632]{2,1,0:T(8,128)(2,1)} custom-call(bf16[1,8,2048]{2,1,0:T(8,128)(2,1)} %links.1, bf16[1,16,1024]{2,1,0:T(8,128)(2,1)} %pivots.1, bf16[1,2,16,1024]{3,2,1,0:T(8,128)(2,1)} %inverse.1, bf16[4,16,1024]{2,1,0:T(8,128)(2,1)} %upper_pivots.1, bf16[4,2,16,1024]{3,2,1,0:T(8,128)(2,1)} %upper_inverse.1), custom_call_target="tpu_custom_call" | custom-call | flops 1000000 | bytes 1000000 | tf_op jit(solution)/shard_map/pallas_call | solution.py:238
  2.7 33.1 %all_to_all.5 = bf16[8,16,5632]{2,1,0:T(8,128)(2,1)S(1)} all-to-all(bf16[8,16,5632]{2,1,0:T(8,128)(2,1)} %shard_map.104), channel_id=1, replica_groups={{0,1,2,3,4,5,6,7},{8,9,10,11,12,13,14,15},{16,17,18,19,20,21,22,23},{24..., dimensions={0} | all-to-all | bytes 2883584 | tf_op jit(solution)/shard_map/all_to_all | solution.py:246
  35.8 0.0 copy-start
  35.8 0.0 copy-start.2
  35.8 0.1 slice.9.refs_0_
  35.9 5.0 %collective-permute-start.3 = (bf16[8,16,3072]{2,1,0:T(8,128)(2,1)S(1)}, bf16[8,16,3072]{2,1,0:T(8,128)(2,1)S(1)}, u32[]{:S(2)}, u32[]{:S(2)}) collective-permute-start(bf16[8,16,3072]{2,1,0:T(8,128)(2,1)S(1)} %slice.9.refs_0_), channel_id=1, source_target_pairs={{0,56},{1,57},{2,58},{3,59},{4,60},{5,61},{6,62},{7,63},{8,0},{9,1... | collective-permute-start | bytes 2359304 | tf_op jit(solution)/shard_map/ppermute | solution.py:253
  40.9 1.9 %collective-permute-start.2 = (bf16[8,16,3072]{2,1,0:T(8,128)(2,1)S(1)}, bf16[8,16,3072]{2,1,0:T(8,128)(2,1)S(1)}, u32[]{:S(2)}, u32[]{:S(2)}) collective-permute-start(bf16[8,16,3072]{2,1,0:T(8,128)(2,1)S(1)} %slice.9.refs_0_), channel_id=1, source_target_pairs={{0,8},{1,9},{2,10},{3,11},{4,12},{5,13},{6,14},{7,15},{8,16},{9,17... | collective-permute-start | bytes 2359304 | tf_op jit(solution)/shard_map/ppermute | solution.py:253
  42.9 4.6 %collective-permute-start.1 = (bf16[8,16,2560]{2,1,0:T(8,128)(2,1)S(1)}, bf16[8,16,2560]{2,1,0:T(8,128)(2,1)S(1)}, u32[]{:S(2)}, u32[]{:S(2)}) collective-permute-start(bf16[8,16,2560]{2,1,0:T(8,128)(2,1)S(1)} %slice.8.refs_0_), channel_id=1, source_target_pairs={{0,56},{1,57},{2,58},{3,59},{4,60},{5,61},{6,62},{7,63},{8,0},{9,1... | collective-permute-start | bytes 1966088 | tf_op jit(solution)/shard_map/ppermute | solution.py:254
  47.5 1.9 %collective-permute-start = (bf16[8,16,2560]{2,1,0:T(8,128)(2,1)S(1)}, bf16[8,16,2560]{2,1,0:T(8,128)(2,1)S(1)}, u32[]{:S(2)}, u32[]{:S(2)}) collective-permute-start(bf16[8,16,2560]{2,1,0:T(8,128)(2,1)S(1)} %slice.8.refs_0_), channel_id=1, source_target_pairs={{0,8},{1,9},{2,10},{3,11},{4,12},{5,13},{6,14},{7,15},{8,16},{9,17... | collective-permute-start | bytes 1966088 | tf_op jit(solution)/shard_map/ppermute | solution.py:254
  49.4 0.4 collective-permute-done.3.refs_4_
  49.8 5.3 %collective-permute-start.7 = (bf16[8,16,3072]{2,1,0:T(8,128)(2,1)S(1)}, bf16[8,16,3072]{2,1,0:T(8,128)(2,1)S(1)}, u32[]{:S(2)}, u32[]{:S(2)}) collective-permute-start(bf16[8,16,3072]{2,1,0:T(8,128)(2,1)S(1)} %collective-permute-done.3.refs_4_), channel_id=1, source_target_pairs={{0,56},{1,57},{2,58},{3,59},{4,60},{5,61},{6,62},{7,63},{8,0},{9,1... | collective-permute-start | bytes 2359304 | tf_op jit(solution)/shard_map/ppermute | solution.py:253
  55.1 0.0 collective-permute-done.2.refs_1_
  55.1 1.9 %collective-permute-start.6 = (bf16[8,16,3072]{2,1,0:T(8,128)(2,1)S(1)}, bf16[8,16,3072]{2,1,0:T(8,128)(2,1)S(1)}, u32[]{:S(2)}, u32[]{:S(2)}) collective-permute-start(bf16[8,16,3072]{2,1,0:T(8,128)(2,1)S(1)} %collective-permute-done.2.refs_1_), channel_id=1, source_target_pairs={{0,8},{1,9},{2,10},{3,11},{4,12},{5,13},{6,14},{7,15},{8,16},{9,17... | collective-permute-start | bytes 2359304 | tf_op jit(solution)/shard_map/ppermute | solution.py:253
  57.1 0.0 collective-permute-done.1.refs_4_
  57.1 5.1 %collective-permute-done.refs_1_ = bf16[8,16,2560]{2,1,0:T(8,128)(2,1)S(1)} collective-permute-done((bf16[8,16,2560]{2,1,0:T(8,128)(2,1)S(1)}, bf16[8,16,2560]{2,1,0:T(8,128)(2,1)S(1)}, u32[]{:S(2)}, u32[]{:S(2)}) %collective-permute-start) | collective-permute-done | bytes 655392 | tf_op jit(solution)/shard_map/ppermute | solution.py:254
  62.2 1.9 %collective-permute-start.4 = (bf16[8,16,2560]{2,1,0:T(8,128)(2,1)S(1)}, bf16[8,16,2560]{2,1,0:T(8,128)(2,1)S(1)}, u32[]{:S(2)}, u32[]{:S(2)}) collective-permute-start(bf16[8,16,2560]{2,1,0:T(8,128)(2,1)S(1)} %collective-permute-done.refs_1_), channel_id=1, source_target_pairs={{0,8},{1,9},{2,10},{3,11},{4,12},{5,13},{6,14},{7,15},{8,16},{9,17... | collective-permute-start | bytes 1966088 | tf_op jit(solution)/shard_map/ppermute | solution.py:254
  64.1 4.6 %collective-permute-start.5 = (bf16[8,16,2560]{2,1,0:T(8,128)(2,1)S(1)}, bf16[8,16,2560]{2,1,0:T(8,128)(2,1)S(1)}, u32[]{:S(2)}, u32[]{:S(2)}) collective-permute-start(bf16[8,16,2560]{2,1,0:T(8,128)(2,1)S(1)} %collective-permute-done.1.refs_4_), channel_id=1, source_target_pairs={{0,56},{1,57},{2,58},{3,59},{4,60},{5,61},{6,62},{7,63},{8,0},{9,1... | collective-permute-start | bytes 1966088 | tf_op jit(solution)/shard_map/ppermute | solution.py:254
  68.7 0.0 collective-permute-done.7.refs_5_
  68.7 1.9 %collective-permute-done.6.refs_2_ = bf16[8,16,3072]{2,1,0:T(8,128)(2,1)S(1)} collective-permute-done((bf16[8,16,3072]{2,1,0:T(8,128)(2,1)S(1)}, bf16[8,16,3072]{2,1,0:T(8,128)(2,1)S(1)}, u32[]{:S(2)}, u32[]{:S(2)}) %collective-permute-start.6) | collective-permute-done | bytes 786464 | tf_op jit(solution)/shard_map/ppermute | solution.py:253
  70.6 1.9 %collective-permute-start.10 = (bf16[8,16,3072]{2,1,0:T(8,128)(2,1)S(1)}, bf16[8,16,3072]{2,1,0:T(8,128)(2,1)S(1)}, u32[]{:S(2)}, u32[]{:S(2)}) collective-permute-start(bf16[8,16,3072]{2,1,0:T(8,128)(2,1)S(1)} %collective-permute-done.6.refs_2_), channel_id=1, source_target_pairs={{0,8},{1,9},{2,10},{3,11},{4,12},{5,13},{6,14},{7,15},{8,16},{9,17... | collective-permute-start | bytes 2359304 | tf_op jit(solution)/shard_map/ppermute | solution.py:253
  72.5 4.6 %collective-permute-start.11 = (bf16[8,16,3072]{2,1,0:T(8,128)(2,1)S(1)}, bf16[8,16,3072]{2,1,0:T(8,128)(2,1)S(1)}, u32[]{:S(2)}, u32[]{:S(2)}) collective-permute-start(bf16[8,16,3072]{2,1,0:T(8,128)(2,1)S(1)} %collective-permute-done.7.refs_5_), channel_id=1, source_target_pairs={{0,56},{1,57},{2,58},{3,59},{4,60},{5,61},{6,62},{7,63},{8,0},{9,1... | collective-permute-start | bytes 2359304 | tf_op jit(solution)/shard_map/ppermute | solution.py:253
  77.1 0.5 collective-permute-done.4.refs_2_
  77.6 0.0 collective-permute-done.5.refs_5_
  77.6 1.9 %collective-permute-start.8 = (bf16[8,16,2560]{2,1,0:T(8,128)(2,1)S(1)}, bf16[8,16,2560]{2,1,0:T(8,128)(2,1)S(1)}, u32[]{:S(2)}, u32[]{:S(2)}) collective-permute-start(bf16[8,16,2560]{2,1,0:T(8,128)(2,1)S(1)} %collective-permute-done.4.refs_2_), channel_id=1, source_target_pairs={{0,8},{1,9},{2,10},{3,11},{4,12},{5,13},{6,14},{7,15},{8,16},{9,17... | collective-permute-start | bytes 1966088 | tf_op jit(solution)/shard_map/ppermute | solution.py:254
  79.5 4.6 %collective-permute-start.9 = (bf16[8,16,2560]{2,1,0:T(8,128)(2,1)S(1)}, bf16[8,16,2560]{2,1,0:T(8,128)(2,1)S(1)}, u32[]{:S(2)}, u32[]{:S(2)}) collective-permute-start(bf16[8,16,2560]{2,1,0:T(8,128)(2,1)S(1)} %collective-permute-done.5.refs_5_), channel_id=1, source_target_pairs={{0,56},{1,57},{2,58},{3,59},{4,60},{5,61},{6,62},{7,63},{8,0},{9,1... | collective-permute-start | bytes 1966088 | tf_op jit(solution)/shard_map/ppermute | solution.py:254
  84.1 1.9 %collective-permute-done.10.refs_3_ = bf16[8,16,3072]{2,1,0:T(8,128)(2,1)S(1)} collective-permute-done((bf16[8,16,3072]{2,1,0:T(8,128)(2,1)S(1)}, bf16[8,16,3072]{2,1,0:T(8,128)(2,1)S(1)}, u32[]{:S(2)}, u32[]{:S(2)}) %collective-permute-start.10) | collective-permute-done | bytes 786464 | tf_op jit(solution)/shard_map/ppermute | solution.py:253
  86.0 0.0 collective-permute-done.11.refs_6_
  86.0 1.9 %collective-permute-start.13 = (bf16[8,16,3072]{2,1,0:T(8,128)(2,1)S(1)}, bf16[8,16,3072]{2,1,0:T(8,128)(2,1)S(1)}, u32[]{:S(2)}, u32[]{:S(2)}) collective-permute-start(bf16[8,16,3072]{2,1,0:T(8,128)(2,1)S(1)} %collective-permute-done.10.refs_3_), channel_id=1, source_target_pairs={{0,8},{1,9},{2,10},{3,11},{4,12},{5,13},{6,14},{7,15},{8,16},{9,17... | collective-permute-start | bytes 2359304 | tf_op jit(solution)/shard_map/ppermute | solution.py:260
  88.0 5.1 %collective-permute-done.8.refs_3_ = bf16[8,16,2560]{2,1,0:T(8,128)(2,1)S(1)} collective-permute-done((bf16[8,16,2560]{2,1,0:T(8,128)(2,1)S(1)}, bf16[8,16,2560]{2,1,0:T(8,128)(2,1)S(1)}, u32[]{:S(2)}, u32[]{:S(2)}) %collective-permute-start.8) | collective-permute-done | bytes 655392 | tf_op jit(solution)/shard_map/ppermute | solution.py:254
  93.1 0.0 collective-permute-done.9.refs_6_
  93.1 5.3 %collective-permute-start.12 = (bf16[8,16,2560]{2,1,0:T(8,128)(2,1)S(1)}, bf16[8,16,2560]{2,1,0:T(8,128)(2,1)S(1)}, u32[]{:S(2)}, u32[]{:S(2)}) collective-permute-start(bf16[8,16,2560]{2,1,0:T(8,128)(2,1)S(1)} %collective-permute-done.9.refs_6_), channel_id=1, source_target_pairs={{0,56},{1,57},{2,58},{3,59},{4,60},{5,61},{6,62},{7,63},{8,0},{9,1... | collective-permute-start | bytes 1966088 | tf_op jit(solution)/shard_map/ppermute | solution.py:261
  98.3 3.1 %collective-permute-done.13.refs_7_ = bf16[8,16,3072]{2,1,0:T(8,128)(2,1)S(1)} collective-permute-done((bf16[8,16,3072]{2,1,0:T(8,128)(2,1)S(1)}, bf16[8,16,3072]{2,1,0:T(8,128)(2,1)S(1)}, u32[]{:S(2)}, u32[]{:S(2)}) %collective-permute-start.13) | collective-permute-done | bytes 786464 | tf_op jit(solution)/shard_map/ppermute | solution.py:260
  101.5 0.0 copy-done
  101.5 0.0 copy-done.2
  101.5 5.2 %shard_map.105 = (bf16[640,1024]{1,0:T(8,128)(2,1)S(1)}, bf16[640,1024]{1,0:T(8,128)(2,1)S(1)}) custom-call(s32[1,1,2]{2,1,0:T(1,128)S(1)} %copy-done.2, bf16[128,2048]{1,0:T(8,128)(2,1)S(1)} %bitcast.4, bf16[8,16,3072]{2,1,0:T(8,128)(2,1)S(1)} %slice.9.refs_0_, bf16[8,16,3072]{2,1,0:T(8,128)(2,1)S(1)} %collective-permute-done.2.refs_1_, ...), custom_call_target="tpu_custom_call" | custom-call | flops 1000 | bytes 1000 | tf_op jit(solution)/shard_map/pallas_call | solution.py:268
  106.7 0.0 collective-permute-done.12.refs_7_
  106.7 0.0 copy-start.3
  106.7 0.7 shard_map.106
  107.4 8.7 %collective-permute-start.15 = (bf16[8,8,16,1536]{3,2,1,0:T(8,128)(2,1)S(1)}, bf16[8,8,16,1536]{3,2,1,0:T(8,128)(2,1)S(1)}, u32[]{:S(2)}, u32[]{:S(2)}) collective-permute-start(bf16[8,8,16,1536]{3,2,1,0:T(8,128)(2,1)S(1)} %get-tuple-element.56.mine), channel_id=1, source_target_pairs={{0,64},{64,0},{128,192},{192,128},{256,320},{320,256},{384,448},{4... | collective-permute-start | bytes 9437192 | tf_op jit(solution)/shard_map/ppermute | solution.py:40
  116.2 0.0 copy-done.3
  116.2 3.7 %shard_map.107 = (bf16[128,2048]{1,0:T(8,128)(2,1)}, f32[128,512]{1,0:T(8,128)S(1)}, f32[128,512]{1,0:T(8,128)S(1)}) custom-call(s32[1,128]{1,0:T(1,128)S(1)} %copy-done.3, bf16[640,1024]{1,0:T(8,128)(2,1)S(1)} %get-tuple-element.48.f1, bf16[640,1024]{1,0:T(8,128)(2,1)S(1)} %get-tuple-element.49.r2, bf16[8,8,16,1024]{3,2,1,0:T(8,128)(2,1)S(1)} %get-tuple-element.52.inv1), custom_call_target="tpu_custom_call" | custom-call | flops 1500000000 | bytes 8388608 | tf_op jit(solution)/shard_map/pallas_call | solution.py:286
  119.8 0.0 copy-start.1
  119.8 2.0 %collective-permute-start.14 = (f32[128,512]{1,0:T(8,128)S(1)}, f32[128,512]{1,0:T(8,128)S(1)}, u32[]{:S(2)}, u32[]{:S(2)}) collective-permute-start(f32[128,512]{1,0:T(8,128)S(1)} %get-tuple-element.55), channel_id=1, source_target_pairs={{0,64},{64,0},{128,192},{192,128},{256,320},{320,256},{384,448},{4... | collective-permute-start | bytes 786440 | tf_op jit(solution)/shard_map/ppermute | solution.py:40
  121.9 0.0 collective-permute-done.15.theirs
  121.9 2.6 %shard_map.108 = (bf16[1024,1024]{1,0:T(8,128)(2,1)S(1)}, bf16[8,8,16,1024]{3,2,1,0:T(8,128)(2,1)S(1)}, bf16[8,8,16,1024]{3,2,1,0:T(8,128)(2,1)S(1)}) custom-call(bf16[8,8,16,1536]{3,2,1,0:T(8,128)(2,1)S(1)} %get-tuple-element.56.mine, bf16[8,8,16,1536]{3,2,1,0:T(8,128)(2,1)S(1)} %collective-permute-done.15.theirs), custom_call_target="tpu_custom_call" | custom-call | flops 1400000000 | bytes 8388608 | tf_op jit(solution)/shard_map/pallas_call | solution.py:295
  124.5 0.0 collective-permute-done.14.received
  124.5 0.0 copy-done.1
  124.5 2.4 %shard_map.109 = bf16[128,2048]{1,0:T(8,128)(2,1)} custom-call(bf16[128,2048]{1,0:T(8,128)(2,1)S(1)} %bitcast.5, f32[128,512]{1,0:T(8,128)S(1)} %get-tuple-element.54.own, f32[128,512]{1,0:T(8,128)S(1)} %collective-permute-done.14.received, bf16[1024,1024]{1,0:T(8,128)(2,1)S(1)} %get-tuple-element.57.p1, ...), custom_call_target="tpu_custom_call" | custom-call | flops 800000000 | bytes 8388608 | tf_op jit(solution)/shard_map/pallas_call | solution.py:302
  (1 shorter events, 0.0 us)
Async XLA Ops:
  35.8 65.7 %copy-start = (bf16[1,128,2048]{2,1,0:T(8,128)(2,1)S(1)}, bf16[1,128,2048]{2,1,0:T(8,128)(2,1)}, u32[]{:S(2)}) copy-start(bf16[1,128,2048]{2,1,0:T(8,128)(2,1)} %param.9) | copy-start | bytes 1572868
  35.8 65.7 %copy-start.2 = (s32[1,1,2]{2,1,0:T(1,128)S(1)}, s32[1,1,2]{2,1,0:T(1,128)}, u32[]{:S(2)}) copy-start(s32[1,1,2]{2,1,0:T(1,128)} %mask.1) | copy-start | bytes 28
  35.9 13.9 %collective-permute-start.3 = (bf16[8,16,3072]{2,1,0:T(8,128)(2,1)S(1)}, bf16[8,16,3072]{2,1,0:T(8,128)(2,1)S(1)}, u32[]{:S(2)}, u32[]{:S(2)}) collective-permute-start(bf16[8,16,3072]{2,1,0:T(8,128)(2,1)S(1)} %slice.9.refs_0_), channel_id=1, source_target_pairs={{0,56},{1,57},{2,58},{3,59},{4,60},{5,61},{6,62},{7,63},{8,0},{9,1... | collective-permute-start | bytes 2359304 | tf_op jit(solution)/shard_map/ppermute | solution.py:253
  40.9 14.2 %collective-permute-start.2 = (bf16[8,16,3072]{2,1,0:T(8,128)(2,1)S(1)}, bf16[8,16,3072]{2,1,0:T(8,128)(2,1)S(1)}, u32[]{:S(2)}, u32[]{:S(2)}) collective-permute-start(bf16[8,16,3072]{2,1,0:T(8,128)(2,1)S(1)} %slice.9.refs_0_), channel_id=1, source_target_pairs={{0,8},{1,9},{2,10},{3,11},{4,12},{5,13},{6,14},{7,15},{8,16},{9,17... | collective-permute-start | bytes 2359304 | tf_op jit(solution)/shard_map/ppermute | solution.py:253
  42.9 14.2 %collective-permute-start.1 = (bf16[8,16,2560]{2,1,0:T(8,128)(2,1)S(1)}, bf16[8,16,2560]{2,1,0:T(8,128)(2,1)S(1)}, u32[]{:S(2)}, u32[]{:S(2)}) collective-permute-start(bf16[8,16,2560]{2,1,0:T(8,128)(2,1)S(1)} %slice.8.refs_0_), channel_id=1, source_target_pairs={{0,56},{1,57},{2,58},{3,59},{4,60},{5,61},{6,62},{7,63},{8,0},{9,1... | collective-permute-start | bytes 1966088 | tf_op jit(solution)/shard_map/ppermute | solution.py:254
  47.5 14.7 %collective-permute-start = (bf16[8,16,2560]{2,1,0:T(8,128)(2,1)S(1)}, bf16[8,16,2560]{2,1,0:T(8,128)(2,1)S(1)}, u32[]{:S(2)}, u32[]{:S(2)}) collective-permute-start(bf16[8,16,2560]{2,1,0:T(8,128)(2,1)S(1)} %slice.8.refs_0_), channel_id=1, source_target_pairs={{0,8},{1,9},{2,10},{3,11},{4,12},{5,13},{6,14},{7,15},{8,16},{9,17... | collective-permute-start | bytes 1966088 | tf_op jit(solution)/shard_map/ppermute | solution.py:254
  49.8 18.8 %collective-permute-start.7 = (bf16[8,16,3072]{2,1,0:T(8,128)(2,1)S(1)}, bf16[8,16,3072]{2,1,0:T(8,128)(2,1)S(1)}, u32[]{:S(2)}, u32[]{:S(2)}) collective-permute-start(bf16[8,16,3072]{2,1,0:T(8,128)(2,1)S(1)} %collective-permute-done.3.refs_4_), channel_id=1, source_target_pairs={{0,56},{1,57},{2,58},{3,59},{4,60},{5,61},{6,62},{7,63},{8,0},{9,1... | collective-permute-start | bytes 2359304 | tf_op jit(solution)/shard_map/ppermute | solution.py:253
  55.1 15.4 %collective-permute-start.6 = (bf16[8,16,3072]{2,1,0:T(8,128)(2,1)S(1)}, bf16[8,16,3072]{2,1,0:T(8,128)(2,1)S(1)}, u32[]{:S(2)}, u32[]{:S(2)}) collective-permute-start(bf16[8,16,3072]{2,1,0:T(8,128)(2,1)S(1)} %collective-permute-done.2.refs_1_), channel_id=1, source_target_pairs={{0,8},{1,9},{2,10},{3,11},{4,12},{5,13},{6,14},{7,15},{8,16},{9,17... | collective-permute-start | bytes 2359304 | tf_op jit(solution)/shard_map/ppermute | solution.py:253
  62.2 15.4 %collective-permute-start.4 = (bf16[8,16,2560]{2,1,0:T(8,128)(2,1)S(1)}, bf16[8,16,2560]{2,1,0:T(8,128)(2,1)S(1)}, u32[]{:S(2)}, u32[]{:S(2)}) collective-permute-start(bf16[8,16,2560]{2,1,0:T(8,128)(2,1)S(1)} %collective-permute-done.refs_1_), channel_id=1, source_target_pairs={{0,8},{1,9},{2,10},{3,11},{4,12},{5,13},{6,14},{7,15},{8,16},{9,17... | collective-permute-start | bytes 1966088 | tf_op jit(solution)/shard_map/ppermute | solution.py:254
  64.1 13.5 %collective-permute-start.5 = (bf16[8,16,2560]{2,1,0:T(8,128)(2,1)S(1)}, bf16[8,16,2560]{2,1,0:T(8,128)(2,1)S(1)}, u32[]{:S(2)}, u32[]{:S(2)}) collective-permute-start(bf16[8,16,2560]{2,1,0:T(8,128)(2,1)S(1)} %collective-permute-done.1.refs_4_), channel_id=1, source_target_pairs={{0,56},{1,57},{2,58},{3,59},{4,60},{5,61},{6,62},{7,63},{8,0},{9,1... | collective-permute-start | bytes 1966088 | tf_op jit(solution)/shard_map/ppermute | solution.py:254
  70.6 15.4 %collective-permute-start.10 = (bf16[8,16,3072]{2,1,0:T(8,128)(2,1)S(1)}, bf16[8,16,3072]{2,1,0:T(8,128)(2,1)S(1)}, u32[]{:S(2)}, u32[]{:S(2)}) collective-permute-start(bf16[8,16,3072]{2,1,0:T(8,128)(2,1)S(1)} %collective-permute-done.6.refs_2_), channel_id=1, source_target_pairs={{0,8},{1,9},{2,10},{3,11},{4,12},{5,13},{6,14},{7,15},{8,16},{9,17... | collective-permute-start | bytes 2359304 | tf_op jit(solution)/shard_map/ppermute | solution.py:253
  72.5 13.5 %collective-permute-start.11 = (bf16[8,16,3072]{2,1,0:T(8,128)(2,1)S(1)}, bf16[8,16,3072]{2,1,0:T(8,128)(2,1)S(1)}, u32[]{:S(2)}, u32[]{:S(2)}) collective-permute-start(bf16[8,16,3072]{2,1,0:T(8,128)(2,1)S(1)} %collective-permute-done.7.refs_5_), channel_id=1, source_target_pairs={{0,56},{1,57},{2,58},{3,59},{4,60},{5,61},{6,62},{7,63},{8,0},{9,1... | collective-permute-start | bytes 2359304 | tf_op jit(solution)/shard_map/ppermute | solution.py:253
  77.6 15.4 %collective-permute-start.8 = (bf16[8,16,2560]{2,1,0:T(8,128)(2,1)S(1)}, bf16[8,16,2560]{2,1,0:T(8,128)(2,1)S(1)}, u32[]{:S(2)}, u32[]{:S(2)}) collective-permute-start(bf16[8,16,2560]{2,1,0:T(8,128)(2,1)S(1)} %collective-permute-done.4.refs_2_), channel_id=1, source_target_pairs={{0,8},{1,9},{2,10},{3,11},{4,12},{5,13},{6,14},{7,15},{8,16},{9,17... | collective-permute-start | bytes 1966088 | tf_op jit(solution)/shard_map/ppermute | solution.py:254
  79.5 13.5 %collective-permute-start.9 = (bf16[8,16,2560]{2,1,0:T(8,128)(2,1)S(1)}, bf16[8,16,2560]{2,1,0:T(8,128)(2,1)S(1)}, u32[]{:S(2)}, u32[]{:S(2)}) collective-permute-start(bf16[8,16,2560]{2,1,0:T(8,128)(2,1)S(1)} %collective-permute-done.5.refs_5_), channel_id=1, source_target_pairs={{0,56},{1,57},{2,58},{3,59},{4,60},{5,61},{6,62},{7,63},{8,0},{9,1... | collective-permute-start | bytes 1966088 | tf_op jit(solution)/shard_map/ppermute | solution.py:254
  86.0 15.4 %collective-permute-start.13 = (bf16[8,16,3072]{2,1,0:T(8,128)(2,1)S(1)}, bf16[8,16,3072]{2,1,0:T(8,128)(2,1)S(1)}, u32[]{:S(2)}, u32[]{:S(2)}) collective-permute-start(bf16[8,16,3072]{2,1,0:T(8,128)(2,1)S(1)} %collective-permute-done.10.refs_3_), channel_id=1, source_target_pairs={{0,8},{1,9},{2,10},{3,11},{4,12},{5,13},{6,14},{7,15},{8,16},{9,17... | collective-permute-start | bytes 2359304 | tf_op jit(solution)/shard_map/ppermute | solution.py:260
  93.1 13.7 %collective-permute-start.12 = (bf16[8,16,2560]{2,1,0:T(8,128)(2,1)S(1)}, bf16[8,16,2560]{2,1,0:T(8,128)(2,1)S(1)}, u32[]{:S(2)}, u32[]{:S(2)}) collective-permute-start(bf16[8,16,2560]{2,1,0:T(8,128)(2,1)S(1)} %collective-permute-done.9.refs_6_), channel_id=1, source_target_pairs={{0,56},{1,57},{2,58},{3,59},{4,60},{5,61},{6,62},{7,63},{8,0},{9,1... | collective-permute-start | bytes 1966088 | tf_op jit(solution)/shard_map/ppermute | solution.py:261
  106.7 9.4 %copy-start.3 = (s32[1,128]{1,0:T(1,128)S(1)}, s32[1,128]{1,0:T(1,128)}, u32[]{:S(2)}) copy-start(s32[1,128]{1,0:T(1,128)} %row_map.1) | copy-start | bytes 1540
  107.4 14.5 %collective-permute-start.15 = (bf16[8,8,16,1536]{3,2,1,0:T(8,128)(2,1)S(1)}, bf16[8,8,16,1536]{3,2,1,0:T(8,128)(2,1)S(1)}, u32[]{:S(2)}, u32[]{:S(2)}) collective-permute-start(bf16[8,8,16,1536]{3,2,1,0:T(8,128)(2,1)S(1)} %get-tuple-element.56.mine), channel_id=1, source_target_pairs={{0,64},{64,0},{128,192},{192,128},{256,320},{320,256},{384,448},{4... | collective-permute-start | bytes 9437192 | tf_op jit(solution)/shard_map/ppermute | solution.py:40
  119.8 4.7 %copy-start.1 = (bf16[1,128,2048]{2,1,0:T(8,128)(2,1)S(1)}, bf16[1,128,2048]{2,1,0:T(8,128)(2,1)}, u32[]{:S(2)}) copy-start(bf16[1,128,2048]{2,1,0:T(8,128)(2,1)} %param.15) | copy-start | bytes 1572868
  119.8 4.7 %collective-permute-start.14 = (f32[128,512]{1,0:T(8,128)S(1)}, f32[128,512]{1,0:T(8,128)S(1)}, u32[]{:S(2)}, u32[]{:S(2)}) collective-permute-start(f32[128,512]{1,0:T(8,128)S(1)} %get-tuple-element.55), channel_id=1, source_target_pairs={{0,64},{64,0},{128,192},{192,128},{256,320},{320,256},{384,448},{4... | collective-permute-start | bytes 786440 | tf_op jit(solution)/shard_map/ppermute | solution.py:40

commit v6 on v5

--- a/solution.py
+++ b/solution.py
@@ -13,6 +13,8 @@
 WIDTH = 1024
 LINK = 512
 TILE = 256
+CARRIED = 640
+FIRST = CARRIED + 2 * WIDTH
 AXES = ("leaf", "col")
 VMEM = pl.BlockSpec(memory_space=pltpu.VMEM)
 SMEM = pl.BlockSpec(memory_space=pltpu.SMEM)
@@ -51,72 +53,128 @@
         out[:, TILE * j : depth] = times_rows(left(depth), rows).astype(BF16)
 
 
-def pack_kernel(links, pivots, inverse, upper_pivots, upper_inverse, copied, out, low, sems):
+def lent_kernel(inverse, upper_inverse, out, sems):
     leaf = lax.axis_index("leaf")
+    core, parent = lax.rem(leaf, 2), leaf // 2
+    units = (inverse.at[0, 0], inverse.at[0, 1], upper_inverse.at[parent, core])
+    copies = [
+        pltpu.make_async_copy(
+            unit.at[:, pl.ds(CARRIED, WIDTH - CARRIED)],
+            out.at[:, pl.ds((WIDTH - CARRIED) * i, WIDTH - CARRIED)],
+            sems.at[i],
+        )
+        for i, unit in enumerate(units)
+    ]
+    for copy in copies:
+        copy.start()
+    for copy in copies:
+        copy.wait()
+
+
+def pack_kernel(links, pivots, inverse, upper_pivots, upper_inverse, lent, out, low, inv0, inv1, upper, sems):
+    leaf, z = lax.axis_index("leaf"), lax.axis_index("col") // SIDE
     core, parent = lax.rem(leaf, 2), leaf // 2
     half = WIDTH // 2
     part = upper_pivots.at[parent, :, pl.ds(pl.multiple_of(core * half, half), half)]
     pairs = [
         (links.at[0], low),
-        (inverse.at[0, 0], out.at[:, pl.ds(0, WIDTH)]),
-        (pivots.at[0], out.at[:, pl.ds(WIDTH, WIDTH)]),
-        (inverse.at[0, 1], out.at[:, pl.ds(3 * WIDTH, WIDTH)]),
-        (upper_inverse.at[parent, core], out.at[:, pl.ds(4 * WIDTH, WIDTH)]),
-        (part, out.at[:, pl.ds(5 * WIDTH, half)]),
+        (inverse.at[0, 0], inv0),
+        (inverse.at[0, 1], inv1),
+        (upper_inverse.at[parent, core], upper),
+        (pivots.at[0], out.at[:, pl.ds(CARRIED, WIDTH)]),
+        (part, out.at[:, pl.ds(FIRST + 2 * CARRIED, half)]),
     ]
     copies = [pltpu.make_async_copy(source, target, sems.at[i]) for i, (source, target) in enumerate(pairs)]
     for copy in copies:
         copy.start()
-    copies[0].wait()
+    for copy in copies[:4]:
+        copy.wait()
     rows = low[...].astype(F32)
-    out[:, 2 * WIDTH : 3 * WIDTH] = jnp.concatenate([rows[:, :WIDTH], rows[:, WIDTH:]], 0).astype(BF16)
-    for copy in copies[1:]:
+    rows = jnp.concatenate([rows[:, :WIDTH], rows[:, WIDTH:]], 0).astype(BF16)
+    out[:, CARRIED + WIDTH : FIRST] = rows
+    for i, (unit, at) in enumerate(((inv0, 0), (inv1, FIRST), (upper, FIRST + CARRIED))):
+        more = lent[:, (WIDTH - CARRIED) * i : (WIDTH - CARRIED) * (i + 1)]
+        out[:, at : at + 256] = unit[:, :256]
+        out[:, at + 256 : at + 512] = jnp.where(z < 2, more[:, :256], unit[:, 256:512])
+        last = jnp.where(z < 4, more[:, :128], unit[:, 512:CARRIED])
+        out[:, at + 512 : at + CARRIED] = jnp.where(z < 2, more[:, 256:], last)
+    for copy in copies[4:]:
         copy.wait()
-    for i in range(SIDE):
-        copied[i] = out[...]
 
 
 def arrivals(blocks, targets, sems):
     leaf, col = lax.axis_index("leaf"), lax.axis_index("col")
     core = lax.rem(leaf, 2)
     place = jnp.where(core == 0, col // SIDE, lax.rem(col, SIDE))
-    copies = [[] for _ in targets]
+    by_z, by_y = [[] for _ in targets], [[] for _ in targets]
     for i, (block, offset) in enumerate(zip(blocks, (0, -1, -2, -3, 1, 2, 3, 4), strict=True)):
         at = lax.rem(place + offset + SIDE, SIDE)
-        for m, (target, lane) in enumerate(targets):
-            source, sem = block.at[:, :, pl.ds(lane, target.shape[3])], sems.at[i, m]
-            by_z = pltpu.make_async_copy(source, target.at[at], sem)
-            by_y = pltpu.make_async_copy(source, target.at[:, at], sem)
-
-            @pl.when(core == 0)
-            def _():
-                by_z.start()
-
-            @pl.when(core != 0)
-            def _():
-                by_y.start()
-
-            copies[m].append(by_z)
-    return copies
+        mirror = SIDE - 1 - at
+        for m, (target, lane, lanes, triangle) in enumerate(targets):
+            if not triangle:
+                source = block.at[:, :, pl.ds(lane, lanes)]
+                by_z[m].append(pltpu.make_async_copy(source, target.at[at], sems.at[i, m, 0]))
+                by_y[m].append(pltpu.make_async_copy(source, target.at[:, at], sems.at[i, m, 0]))
+                continue
+            second = jnp.where(at < 2, mirror, at), pl.multiple_of(jnp.where(at < 2, 640, 256), 128)
+            third = jnp.where(at < 4, mirror, at), pl.multiple_of(jnp.where(at < 2, 896, jnp.where(at < 4, 640, 512)), 128)
+            for k, (start, count, (row, to)) in enumerate(
+                ((0, 256, (at, 0)), (256, 256, second), (512, 128, third))
+            ):
+                source = block.at[:, :, pl.ds(lane + start, count)]
+                by_z[m].append(
+                    pltpu.make_async_copy(source, target.at[row, :, :, pl.ds(to, count)], sems.at[i, m, k])
+                )
+            pieces = [(0, 8, 0, 0, 256, 0), (2, 6, 2, 256, 256, 256), (4, 4, 4, 512, 128, 512)]
+            pieces += [(0, 1, 7, 256, 256, 640), (1, 1, 6, 256, 256, 640), (0, 1, 7, 512, 128, 896)]
+            pieces += [(1, 1, 6, 512, 128, 896), (2, 1, 5, 512, 128, 640), (3, 1, 4, 512, 128, 640)]
+            for k, (first, rows, row, start, count, to) in enumerate(pieces):
+                source = block.at[pl.ds(first, rows), :, pl.ds(lane + start, count)]
+                by_y[m].append(
+                    pltpu.make_async_copy(
+                        source, target.at[pl.ds(row, rows), at, :, pl.ds(to, count)], sems.at[i, m, k]
+                    )
+                )
+
+    def each(copies, act):
+        for copy in copies:
+            act(copy)
+
+    def both(lists, act):
+        @pl.when(core == 0)
+        def _():
+            for copies in lists[0]:
+                each(copies, act)
+
+        @pl.when(core != 0)
+        def _():
+            for copies in lists[1]:
+                each(copies, act)
+
+    both((by_z, by_y), lambda copy: copy.start())
+    return [
+        (lambda m=m: both((by_z[m : m + 1], by_y[m : m + 1]), lambda copy: copy.wait())) for m in range(len(targets))
+    ]
 
 
 def order_kernel(*refs):
     blocks, (inv1, mine, sems) = refs[:8], refs[8:]
-    for copies in arrivals(blocks, [(inv1, 0), (mine, WIDTH)], sems):
-        for copy in copies:
-            copy.wait()
+    tail = mine.at[:, :, :, pl.ds(WIDTH, WIDTH // 2)]
+    targets = [(inv1, 0, CARRIED, True), (mine, CARRIED, CARRIED, True), (tail, 2 * CARRIED, WIDTH // 2, False)]
+    for wait in arrivals(blocks, targets, sems):
+        wait()
 
 
 def first_kernel(mask, panels, *refs):
     blocks, refs = refs[:8], refs[8:]
     f1, r2, inv0, piv, lnk, p1, x1, x2, sems = refs
-    copies = arrivals(blocks, [(inv0, 0), (piv, WIDTH), (lnk, 2 * WIDTH)], sems)
+    targets = [(inv0, 0, CARRIED, True), (piv, CARRIED, WIDTH, False), (lnk, CARRIED + WIDTH, WIDTH, False)]
+    waits = arrivals(blocks, targets, sems)
     zero = jnp.zeros((), BF16)
     x1[:ROWS] = jnp.where(mask[0, 0, 0] != 0, panels[:, :WIDTH], zero)
     x2[:ROWS] = jnp.where(mask[0, 0, 1] != 0, panels[:, WIDTH:], zero)
-    for m in (2, 0, 1):
-        for copy in copies[m]:
-            copy.wait()
+    for wait in waits:
+        wait()
     for j in range(LINK // 16):
         one = lnk[j // 4, 2 * j % 8].astype(F32)
         two = lnk[j // 4, 2 * j % 8 + 1].astype(F32)
@@ -235,30 +293,42 @@
     parent_inverse,
 ):
     half = WIDTH // 2
+    (lent,) = call(
+        lent_kernel,
+        [ANY] * 2,
+        [((16, 3 * (WIDTH - CARRIED)), BF16)],
+        [pltpu.SemaphoreType.DMA((3,))],
+        1_000,
+        60,
+    )(child_inverse, parent_inverse)
+    mirrored = [(z * SIDE + y, (SIDE - 1 - z) * SIDE + y) for z in range(SIDE // 2, SIDE) for y in range(SIDE)]
+    lent = lax.ppermute(lent, "col", mirrored)
     (message,) = call(
         pack_kernel,
-        [ANY] * 5,
-        [((SIDE, 16, 5 * WIDTH + half), BF16)],
-        [matrix(16, 5 * WIDTH + half), matrix(8, 2 * WIDTH), pltpu.SemaphoreType.DMA((6,))],
-        1_000_000,
+        [ANY] * 5 + [VMEM],
+        [((16, FIRST + 2 * CARRIED + half), BF16)],
+        [matrix(8, 2 * WIDTH)] + [matrix(16, WIDTH)] * 3 + [pltpu.SemaphoreType.DMA((6,))],
+        1_000,
         60,
-    )(child_links, child_pivots, child_inverse, parent_pivots, parent_inverse)
+    )(child_links, child_pivots, child_inverse, parent_pivots, parent_inverse, lent)
+    message = jnp.broadcast_to(message[None], (SIDE, *message.shape))
     block = lax.all_to_all(message, AXES, 0, 0, axis_index_groups=lines())
     up = functools.partial(lax.ppermute, axis_name=AXES, perm=ring(1))
     down = functools.partial(lax.ppermute, axis_name=AXES, perm=ring(-1))
-    first, second = block[:, :, : 3 * WIDTH], block[:, :, 3 * WIDTH :]
+    first, second = block[:, :, :FIRST], block[:, :, FIRST:]
     first_blocks, second_blocks = [first], [second]
     a, b = (first, first), (second, second)
     for step in range(3):
-        a, last = (up(a[0]), down(a[1])), b
-        b = (up(b[0]), down(b[1]))
+        b, last = (up(b[0]), down(b[1])), a
+        a = (up(a[0]), down(a[1]))
         if step:
-            *a, _, _ = lax.optimization_barrier((*a, *last))
-        *b, a0, a1 = lax.optimization_barrier((*b, *a))
-        first_blocks += [a0, a1]
-        second_blocks += list(b)
-    first_blocks.append(up(a[0]))
-    farthest = down(b[1])
+            *b, _, _ = lax.optimization_barrier((*b, *last))
+        *a, b0, b1 = lax.optimization_barrier((*a, *b))
+        second_blocks += [b0, b1]
+        first_blocks += list(a)
+    upper_far, lower_far = lax.optimization_barrier((up(b[0]), down(a[1])))
+    second_blocks.append(upper_far)
+    first_blocks.append(lower_far)
     first_blocks, second_blocks = (
         [blocks[i] for i in (0, 1, 3, 5, 2, 4, 6)] + blocks[7:] for blocks in (first_blocks, second_blocks)
     )
@@ -269,19 +339,18 @@
         first_kernel,
         [SMEM, VMEM] + [ANY] * 8,
         [((stack, WIDTH), BF16)] * 2,
-        [matrix(*weight)] * 3 + [matrix(WIDTH, WIDTH)] + [matrix(stack, WIDTH)] * 2 + [pltpu.SemaphoreType.DMA((8, 3))],
+        [matrix(*weight)] * 3 + [matrix(WIDTH, WIDTH)] + [matrix(stack, WIDTH)] * 2 + [pltpu.SemaphoreType.DMA((8, 3, 9))],
         1_000,
     )(block_mask, child_panels[0], *first_blocks)
-    farthest, f1, r2 = lax.optimization_barrier((farthest, f1, r2))
     inv1, mine = call(
         order_kernel,
         [ANY] * 8,
         [(weight, BF16), ((SIDE, SIDE, 16, WIDTH + half), BF16)],
-        [pltpu.SemaphoreType.DMA((8, 2))],
+        [pltpu.SemaphoreType.DMA((8, 3, 9))],
         1_000_000,
         16,
         ANY,
-    )(*second_blocks, farthest)
+    )(*second_blocks)
     theirs = swap_cores(mine)
     child_factor, own, sent = call(
         second_kernel,

time: 128 us -> 150 us (1.17)
  waiting for transfers between devices: 18.2 us -> 43.4 us
  blocking collectives: 33.1 us -> 21.2 us
  Pallas kernels: 16.7 us -> 22.5 us
  starting transfers between devices: 58 us -> 59.7 us
  local copies, waits for them, and re-layouts: 0.13 us -> 1.71 us
    ppermute x14 -> x15, waiting for transfers between devices: 18.2 us -> 43.4 us  [the longest x6 23.4 us: local(): b, last = ((up(b[0]), down(b[1])), a)]
    all_to_all x1, blocking collectives: 33.1 us -> 21.2 us  [local(): block = lax.all_to_all(message, AXES, 0, 0, axis_index_groups=lines())]
    pallas_call x1, Pallas kernels: 0.67 us -> 2.96 us  [local(): call(order_kernel, [ANY] * 8, [(weight, BF16), ((SIDE, SIDE, 16, WIDTH +...]
    pallas_call x1, Pallas kernels: 5.22 us -> 7.16 us  [local(): call(first_kernel, [SMEM, VMEM] + [ANY] * 8, [((stack, WIDTH), BF16)] * 2...]
    pallas_call x1 -> x2, Pallas kernels: 2.1 us -> 3.69 us  [the longest x1 2.3 us: local(): call(pack_kernel, [ANY] * 5 + [VMEM], [((16, FIRST + 2 * CARRIED + half),...]
    ppermute x14 -> x15, starting transfers between devices: 47.2 us -> 48 us  [the longest x6 21.2 us: local(): a = (up(a[0]), down(a[1]))]
  transfers between devices with their start and end apart: 16 -> 17, of which waited for: 7 -> 7; matrix products, arithmetic and copies ran while one was open for 0% -> 0% of each run, Pallas kernels for 9% -> 9%
where the time goes in v6:
time: 150 us; the launch traced here: 149 us
  starting transfers between devices  59.7 us (40%)
  waiting for transfers between devices  43.4 us (29%)
  Pallas kernels  22.5 us (15%)
  blocking collectives  21.2 us (14%)
  local copies, waits for them, and re-layouts  1.71 us (1%)
    ppermute x6, waiting for transfers between devices, local(): b, last = ((up(b[0]), down(b[1])), a)  23.4 us
    all_to_all x1, blocking collectives, local(): block = lax.all_to_all(message, AXES, 0, 0, axis_index_groups=lines())  21.2 us
    ppermute x6, starting transfers between devices, local(): a = (up(a[0]), down(a[1]))  21.2 us
    ppermute x6, starting transfers between devices, local(): b, last = ((up(b[0]), down(b[1])), a)  18.3 us
    ppermute x2, starting transfers between devices, swap_cores(): return lax.ppermute(value, 'leaf', [(i, i ^ 1) for i in range(8)])  11.7 us
    ppermute x1, waiting for transfers between devices, local(): lent = lax.ppermute(lent, 'col', mirrored)  11.5 us
    ppermute x2, waiting for transfers between devices, local(): upper_far, lower_far = lax.optimization_barrier((up(b[0]), down(a[1])))  8.51 us
    ppermute x2, starting transfers between devices, local(): upper_far, lower_far = lax.optimization_barrier((up(b[0]), down(a[1])))  7.23 us
  transfers between devices with their start and end apart: 17, of which 7 were waited for; matrix products, arithmetic and copies ran while one was open for 0% of the time, Pallas kernels for 9%

profile of v6, /device:TPU:1, one launch (start us, length us, event | category | flops | bytes accessed | tf_op | source)
XLA Modules:
  0.0 149.4 jit_solution(2621619778230817010)
XLA Ops:
  0.6 1.4 shard_map.104
  2.0 1.3 collective-permute-start
  3.3 11.5 %collective-permute-done.lent = bf16[16,1152]{1,0:T(8,128)(2,1)S(1)} collective-permute-done((bf16[16,1152]{1,0:T(8,128)(2,1)}, bf16[16,1152]{1,0:T(8,128)(2,1)S(1)}, u32[]{:S(2)}, u32[]{:S(2)}) %collective-permute-start) | collective-permute-done | bytes 36896 | tf_op jit(solution)/shard_map/ppermute | solution.py:305
  14.8 0.0 copy-start.4
  14.8 0.6 copy-done.4
  15.4 2.3 %shard_map.105 = bf16[16,4480]{1,0:T(8,128)(2,1)} custom-call(bf16[1,8,2048]{2,1,0:T(8,128)(2,1)} %links.1, bf16[1,16,1024]{2,1,0:T(8,128)(2,1)} %pivots.1, bf16[1,2,16,1024]{3,2,1,0:T(8,128)(2,1)} %inverse.3, bf16[4,16,1024]{2,1,0:T(8,128)(2,1)} %upper_pivots.1, bf16[4,2,16,1024]{3,2,1,0:T(8,128)(2,1)} %upper_inverse.3, bf16[16,1152]{1,0:T(8,128)(2,1)} %copy-done.4), custom_call_target="tpu_custom_call" | custom-call | flops 1000 | bytes 1000 | tf_op jit(solution)/shard_map/pallas_call | solution.py:306
  17.8 1.0 broadcast_in_dim.12
  18.7 21.2 %all_to_all.5 = bf16[8,16,4480]{2,1,0:T(8,128)(2,1)S(1)} all-to-all(bf16[8,16,4480]{2,1,0:T(8,128)(2,1)S(1)} %broadcast_in_dim.12), channel_id=1, replica_groups={{0,1,2,3,4,5,6,7},{8,9,10,11,12,13,14,15},{16,17,18,19,20,21,22,23},{24..., dimensions={0} | all-to-all | bytes 2293760 | tf_op jit(solution)/shard_map/all_to_all | solution.py:315
  40.0 0.0 copy-start
  40.0 0.0 copy-start.2
  40.0 5.5 %collective-permute-start.2 = (bf16[8,16,2688]{2,1,0:T(8,128)(2,1)S(1)}, bf16[8,16,2688]{2,1,0:T(8,128)(2,1)S(1)}, u32[]{:S(2)}, u32[]{:S(2)}) collective-permute-start(bf16[8,16,2688]{2,1,0:T(8,128)(2,1)S(1)} %slice.8.refs_0_), channel_id=1, source_target_pairs={{0,56},{1,57},{2,58},{3,59},{4,60},{5,61},{6,62},{7,63},{8,0},{9,1... | collective-permute-start | bytes 2064392 | tf_op jit(solution)/shard_map/ppermute | solution.py:323
  45.6 1.9 %collective-permute-start.1 = (bf16[8,16,2688]{2,1,0:T(8,128)(2,1)S(1)}, bf16[8,16,2688]{2,1,0:T(8,128)(2,1)S(1)}, u32[]{:S(2)}, u32[]{:S(2)}) collective-permute-start(bf16[8,16,2688]{2,1,0:T(8,128)(2,1)S(1)} %slice.8.refs_0_), channel_id=1, source_target_pairs={{0,8},{1,9},{2,10},{3,11},{4,12},{5,13},{6,14},{7,15},{8,16},{9,17... | collective-permute-start | bytes 2064392 | tf_op jit(solution)/shard_map/ppermute | solution.py:323
  47.5 4.6 %collective-permute-start.4 = (bf16[8,16,1792]{2,1,0:T(8,128)(2,1)S(1)}, bf16[8,16,1792]{2,1,0:T(8,128)(2,1)S(1)}, u32[]{:S(2)}, u32[]{:S(2)}) collective-permute-start(bf16[8,16,1792]{2,1,0:T(8,128)(2,1)S(1)} %slice.9.refs_0_), channel_id=1, source_target_pairs={{0,56},{1,57},{2,58},{3,59},{4,60},{5,61},{6,62},{7,63},{8,0},{9,1... | collective-permute-start | bytes 1376264 | tf_op jit(solution)/shard_map/ppermute | solution.py:322
  52.1 1.9 %collective-permute-start.3 = (bf16[8,16,1792]{2,1,0:T(8,128)(2,1)S(1)}, bf16[8,16,1792]{2,1,0:T(8,128)(2,1)S(1)}, u32[]{:S(2)}, u32[]{:S(2)}) collective-permute-start(bf16[8,16,1792]{2,1,0:T(8,128)(2,1)S(1)} %slice.9.refs_0_), channel_id=1, source_target_pairs={{0,8},{1,9},{2,10},{3,11},{4,12},{5,13},{6,14},{7,15},{8,16},{9,17... | collective-permute-start | bytes 1376264 | tf_op jit(solution)/shard_map/ppermute | solution.py:322
  54.0 4.3 %collective-permute-done.4.refs_4_ = bf16[8,16,1792]{2,1,0:T(8,128)(2,1)S(1)} collective-permute-done((bf16[8,16,1792]{2,1,0:T(8,128)(2,1)S(1)}, bf16[8,16,1792]{2,1,0:T(8,128)(2,1)S(1)}, u32[]{:S(2)}, u32[]{:S(2)}) %collective-permute-start.4) | collective-permute-done | bytes 458784 | tf_op jit(solution)/shard_map/ppermute | solution.py:322
  58.3 5.3 %collective-permute-done.3.refs_1_ = bf16[8,16,1792]{2,1,0:T(8,128)(2,1)S(1)} collective-permute-done((bf16[8,16,1792]{2,1,0:T(8,128)(2,1)S(1)}, bf16[8,16,1792]{2,1,0:T(8,128)(2,1)S(1)}, u32[]{:S(2)}, u32[]{:S(2)}) %collective-permute-start.3) | collective-permute-done | bytes 458784 | tf_op jit(solution)/shard_map/ppermute | solution.py:322
  63.7 0.0 collective-permute-done.2.refs_4_
  63.7 0.0 collective-permute-done.1.refs_1_
  63.7 1.9 %collective-permute-start.5 = (bf16[8,16,2688]{2,1,0:T(8,128)(2,1)S(1)}, bf16[8,16,2688]{2,1,0:T(8,128)(2,1)S(1)}, u32[]{:S(2)}, u32[]{:S(2)}) collective-permute-start(bf16[8,16,2688]{2,1,0:T(8,128)(2,1)S(1)} %collective-permute-done.1.refs_1_), channel_id=1, source_target_pairs={{0,8},{1,9},{2,10},{3,11},{4,12},{5,13},{6,14},{7,15},{8,16},{9,17... | collective-permute-start | bytes 2064392 | tf_op jit(solution)/shard_map/ppermute | solution.py:323
  65.6 4.6 %collective-permute-start.6 = (bf16[8,16,2688]{2,1,0:T(8,128)(2,1)S(1)}, bf16[8,16,2688]{2,1,0:T(8,128)(2,1)S(1)}, u32[]{:S(2)}, u32[]{:S(2)}) collective-permute-start(bf16[8,16,2688]{2,1,0:T(8,128)(2,1)S(1)} %collective-permute-done.2.refs_4_), channel_id=1, source_target_pairs={{0,56},{1,57},{2,58},{3,59},{4,60},{5,61},{6,62},{7,63},{8,0},{9,1... | collective-permute-start | bytes 2064392 | tf_op jit(solution)/shard_map/ppermute | solution.py:323
  70.2 1.9 %collective-permute-start.8 = (bf16[8,16,1792]{2,1,0:T(8,128)(2,1)S(1)}, bf16[8,16,1792]{2,1,0:T(8,128)(2,1)S(1)}, u32[]{:S(2)}, u32[]{:S(2)}) collective-permute-start(bf16[8,16,1792]{2,1,0:T(8,128)(2,1)S(1)} %collective-permute-done.4.refs_4_), channel_id=1, source_target_pairs={{0,56},{1,57},{2,58},{3,59},{4,60},{5,61},{6,62},{7,63},{8,0},{9,1... | collective-permute-start | bytes 1376264 | tf_op jit(solution)/shard_map/ppermute | solution.py:322
  72.1 3.4 %collective-permute-start.7 = (bf16[8,16,1792]{2,1,0:T(8,128)(2,1)S(1)}, bf16[8,16,1792]{2,1,0:T(8,128)(2,1)S(1)}, u32[]{:S(2)}, u32[]{:S(2)}) collective-permute-start(bf16[8,16,1792]{2,1,0:T(8,128)(2,1)S(1)} %collective-permute-done.3.refs_1_), channel_id=1, source_target_pairs={{0,8},{1,9},{2,10},{3,11},{4,12},{5,13},{6,14},{7,15},{8,16},{9,17... | collective-permute-start | bytes 1376264 | tf_op jit(solution)/shard_map/ppermute | solution.py:322
  75.5 7.5 %collective-permute-done.8.refs_5_ = bf16[8,16,1792]{2,1,0:T(8,128)(2,1)S(1)} collective-permute-done((bf16[8,16,1792]{2,1,0:T(8,128)(2,1)S(1)}, bf16[8,16,1792]{2,1,0:T(8,128)(2,1)S(1)}, u32[]{:S(2)}, u32[]{:S(2)}) %collective-permute-start.8) | collective-permute-done | bytes 458784 | tf_op jit(solution)/shard_map/ppermute | solution.py:322
  82.9 0.0 collective-permute-done.7.refs_2_
  82.9 0.0 collective-permute-done.5.refs_2_
  83.0 0.0 collective-permute-done.6.refs_5_
  83.0 2.0 %collective-permute-start.9 = (bf16[8,16,2688]{2,1,0:T(8,128)(2,1)S(1)}, bf16[8,16,2688]{2,1,0:T(8,128)(2,1)S(1)}, u32[]{:S(2)}, u32[]{:S(2)}) collective-permute-start(bf16[8,16,2688]{2,1,0:T(8,128)(2,1)S(1)} %collective-permute-done.5.refs_2_), channel_id=1, source_target_pairs={{0,8},{1,9},{2,10},{3,11},{4,12},{5,13},{6,14},{7,15},{8,16},{9,17... | collective-permute-start | bytes 2064392 | tf_op jit(solution)/shard_map/ppermute | solution.py:323
  85.0 5.2 %collective-permute-start.10 = (bf16[8,16,2688]{2,1,0:T(8,128)(2,1)S(1)}, bf16[8,16,2688]{2,1,0:T(8,128)(2,1)S(1)}, u32[]{:S(2)}, u32[]{:S(2)}) collective-permute-start(bf16[8,16,2688]{2,1,0:T(8,128)(2,1)S(1)} %collective-permute-done.6.refs_5_), channel_id=1, source_target_pairs={{0,56},{1,57},{2,58},{3,59},{4,60},{5,61},{6,62},{7,63},{8,0},{9,1... | collective-permute-start | bytes 2064392 | tf_op jit(solution)/shard_map/ppermute | solution.py:323
  90.2 1.9 %collective-permute-start.11 = (bf16[8,16,1792]{2,1,0:T(8,128)(2,1)S(1)}, bf16[8,16,1792]{2,1,0:T(8,128)(2,1)S(1)}, u32[]{:S(2)}, u32[]{:S(2)}) collective-permute-start(bf16[8,16,1792]{2,1,0:T(8,128)(2,1)S(1)} %collective-permute-done.7.refs_2_), channel_id=1, source_target_pairs={{0,8},{1,9},{2,10},{3,11},{4,12},{5,13},{6,14},{7,15},{8,16},{9,17... | collective-permute-start | bytes 1376264 | tf_op jit(solution)/shard_map/ppermute | solution.py:322
  92.1 4.6 %collective-permute-start.12 = (bf16[8,16,1792]{2,1,0:T(8,128)(2,1)S(1)}, bf16[8,16,1792]{2,1,0:T(8,128)(2,1)S(1)}, u32[]{:S(2)}, u32[]{:S(2)}) collective-permute-start(bf16[8,16,1792]{2,1,0:T(8,128)(2,1)S(1)} %collective-permute-done.8.refs_5_), channel_id=1, source_target_pairs={{0,56},{1,57},{2,58},{3,59},{4,60},{5,61},{6,62},{7,63},{8,0},{9,1... | collective-permute-start | bytes 1376264 | tf_op jit(solution)/shard_map/ppermute | solution.py:322
  96.7 5.1 %collective-permute-done.11.refs_3_ = bf16[8,16,1792]{2,1,0:T(8,128)(2,1)S(1)} collective-permute-done((bf16[8,16,1792]{2,1,0:T(8,128)(2,1)S(1)}, bf16[8,16,1792]{2,1,0:T(8,128)(2,1)S(1)}, u32[]{:S(2)}, u32[]{:S(2)}) %collective-permute-start.11) | collective-permute-done | bytes 458784 | tf_op jit(solution)/shard_map/ppermute | solution.py:322
  101.8 1.2 collective-permute-done.12.refs_6_
  103.0 0.0 collective-permute-done.9.refs_3_
  103.0 0.0 collective-permute-done.10.refs_6_
  103.0 5.3 %collective-permute-start.14 = (bf16[8,16,2688]{2,1,0:T(8,128)(2,1)S(1)}, bf16[8,16,2688]{2,1,0:T(8,128)(2,1)S(1)}, u32[]{:S(2)}, u32[]{:S(2)}) collective-permute-start(bf16[8,16,2688]{2,1,0:T(8,128)(2,1)S(1)} %collective-permute-done.10.refs_6_), channel_id=1, source_target_pairs={{0,56},{1,57},{2,58},{3,59},{4,60},{5,61},{6,62},{7,63},{8,0},{9,1... | collective-permute-start | bytes 2064392 | tf_op jit(solution)/shard_map/ppermute | solution.py:329
  108.3 1.9 %collective-permute-start.13 = (bf16[8,16,1792]{2,1,0:T(8,128)(2,1)S(1)}, bf16[8,16,1792]{2,1,0:T(8,128)(2,1)S(1)}, u32[]{:S(2)}, u32[]{:S(2)}) collective-permute-start(bf16[8,16,1792]{2,1,0:T(8,128)(2,1)S(1)} %collective-permute-done.11.refs_3_), channel_id=1, source_target_pairs={{0,8},{1,9},{2,10},{3,11},{4,12},{5,13},{6,14},{7,15},{8,16},{9,17... | collective-permute-start | bytes 1376264 | tf_op jit(solution)/shard_map/ppermute | solution.py:329
  110.2 8.5 %collective-permute-done.13.refs_7_ = bf16[8,16,1792]{2,1,0:T(8,128)(2,1)S(1)} collective-permute-done((bf16[8,16,1792]{2,1,0:T(8,128)(2,1)S(1)}, bf16[8,16,1792]{2,1,0:T(8,128)(2,1)S(1)}, u32[]{:S(2)}, u32[]{:S(2)}) %collective-permute-start.13) | collective-permute-done | bytes 458784 | tf_op jit(solution)/shard_map/ppermute | solution.py:329
  118.7 0.0 collective-permute-done.14.refs_7_
  118.7 3.0 %shard_map.107 = (bf16[8,8,16,1024]{3,2,1,0:T(8,128)(2,1)S(1)}, bf16[8,8,16,1536]{3,2,1,0:T(8,128)(2,1)S(1)}) custom-call(bf16[8,16,1792]{2,1,0:T(8,128)(2,1)S(1)} %slice.9.refs_0_, bf16[8,16,1792]{2,1,0:T(8,128)(2,1)S(1)} %collective-permute-done.3.refs_1_, bf16[8,16,1792]{2,1,0:T(8,128)(2,1)S(1)} %collective-permute-done.7.refs_2_, ...), custom_call_target="tpu_custom_call" | custom-call | flops 1000000 | bytes 1000000 | tf_op jit(solution)/shard_map/pallas_call | solution.py:345
  121.7 9.7 %collective-permute-start.16 = (bf16[8,8,16,1536]{3,2,1,0:T(8,128)(2,1)S(1)}, bf16[8,8,16,1536]{3,2,1,0:T(8,128)(2,1)S(1)}, u32[]{:S(2)}, u32[]{:S(2)}) collective-permute-start(bf16[8,8,16,1536]{3,2,1,0:T(8,128)(2,1)S(1)} %get-tuple-element.54.mine), channel_id=1, source_target_pairs={{0,64},{64,0},{128,192},{192,128},{256,320},{320,256},{384,448},{4... | collective-permute-start | bytes 9437192 | tf_op jit(solution)/shard_map/ppermute | solution.py:42
  131.4 0.0 copy-done
  131.4 0.0 copy-done.2
  131.4 0.0 copy-start.3
  131.5 7.2 %shard_map.106 = (bf16[640,1024]{1,0:T(8,128)(2,1)S(1)}, bf16[640,1024]{1,0:T(8,128)(2,1)S(1)}) custom-call(s32[1,1,2]{2,1,0:T(1,128)S(1)} %copy-done.2, bf16[128,2048]{1,0:T(8,128)(2,1)S(1)} %bitcast.4, bf16[8,16,2688]{2,1,0:T(8,128)(2,1)S(1)} %slice.8.refs_0_, bf16[8,16,2688]{2,1,0:T(8,128)(2,1)S(1)} %collective-permute-done.1.refs_1_, ...), custom_call_target="tpu_custom_call" | custom-call | flops 1000 | bytes 1000 | tf_op jit(solution)/shard_map/pallas_call | solution.py:338
  138.6 0.0 copy-done.3
  138.6 3.7 %shard_map.108 = (bf16[128,2048]{1,0:T(8,128)(2,1)}, f32[128,512]{1,0:T(8,128)S(1)}, f32[128,512]{1,0:T(8,128)S(1)}) custom-call(s32[1,128]{1,0:T(1,128)S(1)} %copy-done.3, bf16[640,1024]{1,0:T(8,128)(2,1)S(1)} %get-tuple-element.41.f1, bf16[640,1024]{1,0:T(8,128)(2,1)S(1)} %get-tuple-element.42.r2, bf16[8,8,16,1024]{3,2,1,0:T(8,128)(2,1)S(1)} %get-tuple-element.50.inv1), custom_call_target="tpu_custom_call" | custom-call | flops 1500000000 | bytes 8388608 | tf_op jit(solution)/shard_map/pallas_call | solution.py:355
  142.3 0.0 copy-start.1
  142.3 2.0 %collective-permute-start.15 = (f32[128,512]{1,0:T(8,128)S(1)}, f32[128,512]{1,0:T(8,128)S(1)}, u32[]{:S(2)}, u32[]{:S(2)}) collective-permute-start(f32[128,512]{1,0:T(8,128)S(1)} %get-tuple-element.53), channel_id=1, source_target_pairs={{0,64},{64,0},{128,192},{192,128},{256,320},{320,256},{384,448},{4... | collective-permute-start | bytes 786440 | tf_op jit(solution)/shard_map/ppermute | solution.py:42
  144.3 0.0 collective-permute-done.16.theirs
  144.4 2.6 %shard_map.109 = (bf16[1024,1024]{1,0:T(8,128)(2,1)S(1)}, bf16[8,8,16,1024]{3,2,1,0:T(8,128)(2,1)S(1)}, bf16[8,8,16,1024]{3,2,1,0:T(8,128)(2,1)S(1)}) custom-call(bf16[8,8,16,1536]{3,2,1,0:T(8,128)(2,1)S(1)} %get-tuple-element.54.mine, bf16[8,8,16,1536]{3,2,1,0:T(8,128)(2,1)S(1)} %collective-permute-done.16.theirs), custom_call_target="tpu_custom_call" | custom-call | flops 1400000000 | bytes 8388608 | tf_op jit(solution)/shard_map/pallas_call | solution.py:364
  147.0 0.0 collective-permute-done.15.received
  147.0 0.0 copy-done.1
  147.0 2.4 %shard_map.110 = bf16[128,2048]{1,0:T(8,128)(2,1)} custom-call(bf16[128,2048]{1,0:T(8,128)(2,1)S(1)} %bitcast.5, f32[128,512]{1,0:T(8,128)S(1)} %get-tuple-element.52.own, f32[128,512]{1,0:T(8,128)S(1)} %collective-permute-done.15.received, bf16[1024,1024]{1,0:T(8,128)(2,1)S(1)} %get-tuple-element.55.p1, ...), custom_call_target="tpu_custom_call" | custom-call | flops 800000000 | bytes 8388608 | tf_op jit(solution)/shard_map/pallas_call | solution.py:371
  (2 shorter events, 0.1 us)
Async XLA Ops:
  2.0 12.8 %collective-permute-start = (bf16[16,1152]{1,0:T(8,128)(2,1)}, bf16[16,1152]{1,0:T(8,128)(2,1)S(1)}, u32[]{:S(2)}, u32[]{:S(2)}) collective-permute-start(bf16[16,1152]{1,0:T(8,128)(2,1)} %shard_map.104), channel_id=1, source_target_pairs={{32,24},{33,25},{34,26},{35,27},{36,28},{37,29},{38,30},{39,31},{4... | collective-permute-start | bytes 110600 | tf_op jit(solution)/shard_map/ppermute | solution.py:305
  14.8 0.6 copy-start.4
  40.0 91.4 %copy-start = (bf16[1,128,2048]{2,1,0:T(8,128)(2,1)S(1)}, bf16[1,128,2048]{2,1,0:T(8,128)(2,1)}, u32[]{:S(2)}) copy-start(bf16[1,128,2048]{2,1,0:T(8,128)(2,1)} %param.9) | copy-start | bytes 1572868
  40.0 91.4 %copy-start.2 = (s32[1,1,2]{2,1,0:T(1,128)S(1)}, s32[1,1,2]{2,1,0:T(1,128)}, u32[]{:S(2)}) copy-start(s32[1,1,2]{2,1,0:T(1,128)} %mask.1) | copy-start | bytes 28
  40.0 23.6 %collective-permute-start.2 = (bf16[8,16,2688]{2,1,0:T(8,128)(2,1)S(1)}, bf16[8,16,2688]{2,1,0:T(8,128)(2,1)S(1)}, u32[]{:S(2)}, u32[]{:S(2)}) collective-permute-start(bf16[8,16,2688]{2,1,0:T(8,128)(2,1)S(1)} %slice.8.refs_0_), channel_id=1, source_target_pairs={{0,56},{1,57},{2,58},{3,59},{4,60},{5,61},{6,62},{7,63},{8,0},{9,1... | collective-permute-start | bytes 2064392 | tf_op jit(solution)/shard_map/ppermute | solution.py:323
  45.6 18.1 %collective-permute-start.1 = (bf16[8,16,2688]{2,1,0:T(8,128)(2,1)S(1)}, bf16[8,16,2688]{2,1,0:T(8,128)(2,1)S(1)}, u32[]{:S(2)}, u32[]{:S(2)}) collective-permute-start(bf16[8,16,2688]{2,1,0:T(8,128)(2,1)S(1)} %slice.8.refs_0_), channel_id=1, source_target_pairs={{0,8},{1,9},{2,10},{3,11},{4,12},{5,13},{6,14},{7,15},{8,16},{9,17... | collective-permute-start | bytes 2064392 | tf_op jit(solution)/shard_map/ppermute | solution.py:323
  47.5 10.8 %collective-permute-start.4 = (bf16[8,16,1792]{2,1,0:T(8,128)(2,1)S(1)}, bf16[8,16,1792]{2,1,0:T(8,128)(2,1)S(1)}, u32[]{:S(2)}, u32[]{:S(2)}) collective-permute-start(bf16[8,16,1792]{2,1,0:T(8,128)(2,1)S(1)} %slice.9.refs_0_), channel_id=1, source_target_pairs={{0,56},{1,57},{2,58},{3,59},{4,60},{5,61},{6,62},{7,63},{8,0},{9,1... | collective-permute-start | bytes 1376264 | tf_op jit(solution)/shard_map/ppermute | solution.py:322
  52.1 11.6 %collective-permute-start.3 = (bf16[8,16,1792]{2,1,0:T(8,128)(2,1)S(1)}, bf16[8,16,1792]{2,1,0:T(8,128)(2,1)S(1)}, u32[]{:S(2)}, u32[]{:S(2)}) collective-permute-start(bf16[8,16,1792]{2,1,0:T(8,128)(2,1)S(1)} %slice.9.refs_0_), channel_id=1, source_target_pairs={{0,8},{1,9},{2,10},{3,11},{4,12},{5,13},{6,14},{7,15},{8,16},{9,17... | collective-permute-start | bytes 1376264 | tf_op jit(solution)/shard_map/ppermute | solution.py:322
  63.7 19.3 %collective-permute-start.5 = (bf16[8,16,2688]{2,1,0:T(8,128)(2,1)S(1)}, bf16[8,16,2688]{2,1,0:T(8,128)(2,1)S(1)}, u32[]{:S(2)}, u32[]{:S(2)}) collective-permute-start(bf16[8,16,2688]{2,1,0:T(8,128)(2,1)S(1)} %collective-permute-done.1.refs_1_), channel_id=1, source_target_pairs={{0,8},{1,9},{2,10},{3,11},{4,12},{5,13},{6,14},{7,15},{8,16},{9,17... | collective-permute-start | bytes 2064392 | tf_op jit(solution)/shard_map/ppermute | solution.py:323
  65.6 17.4 %collective-permute-start.6 = (bf16[8,16,2688]{2,1,0:T(8,128)(2,1)S(1)}, bf16[8,16,2688]{2,1,0:T(8,128)(2,1)S(1)}, u32[]{:S(2)}, u32[]{:S(2)}) collective-permute-start(bf16[8,16,2688]{2,1,0:T(8,128)(2,1)S(1)} %collective-permute-done.2.refs_4_), channel_id=1, source_target_pairs={{0,56},{1,57},{2,58},{3,59},{4,60},{5,61},{6,62},{7,63},{8,0},{9,1... | collective-permute-start | bytes 2064392 | tf_op jit(solution)/shard_map/ppermute | solution.py:323
  70.2 12.8 %collective-permute-start.8 = (bf16[8,16,1792]{2,1,0:T(8,128)(2,1)S(1)}, bf16[8,16,1792]{2,1,0:T(8,128)(2,1)S(1)}, u32[]{:S(2)}, u32[]{:S(2)}) collective-permute-start(bf16[8,16,1792]{2,1,0:T(8,128)(2,1)S(1)} %collective-permute-done.4.refs_4_), channel_id=1, source_target_pairs={{0,56},{1,57},{2,58},{3,59},{4,60},{5,61},{6,62},{7,63},{8,0},{9,1... | collective-permute-start | bytes 1376264 | tf_op jit(solution)/shard_map/ppermute | solution.py:322
  72.1 10.8 %collective-permute-start.7 = (bf16[8,16,1792]{2,1,0:T(8,128)(2,1)S(1)}, bf16[8,16,1792]{2,1,0:T(8,128)(2,1)S(1)}, u32[]{:S(2)}, u32[]{:S(2)}) collective-permute-start(bf16[8,16,1792]{2,1,0:T(8,128)(2,1)S(1)} %collective-permute-done.3.refs_1_), channel_id=1, source_target_pairs={{0,8},{1,9},{2,10},{3,11},{4,12},{5,13},{6,14},{7,15},{8,16},{9,17... | collective-permute-start | bytes 1376264 | tf_op jit(solution)/shard_map/ppermute | solution.py:322
  83.0 20.0 %collective-permute-start.9 = (bf16[8,16,2688]{2,1,0:T(8,128)(2,1)S(1)}, bf16[8,16,2688]{2,1,0:T(8,128)(2,1)S(1)}, u32[]{:S(2)}, u32[]{:S(2)}) collective-permute-start(bf16[8,16,2688]{2,1,0:T(8,128)(2,1)S(1)} %collective-permute-done.5.refs_2_), channel_id=1, source_target_pairs={{0,8},{1,9},{2,10},{3,11},{4,12},{5,13},{6,14},{7,15},{8,16},{9,17... | collective-permute-start | bytes 2064392 | tf_op jit(solution)/shard_map/ppermute | solution.py:323
  85.0 18.0 %collective-permute-start.10 = (bf16[8,16,2688]{2,1,0:T(8,128)(2,1)S(1)}, bf16[8,16,2688]{2,1,0:T(8,128)(2,1)S(1)}, u32[]{:S(2)}, u32[]{:S(2)}) collective-permute-start(bf16[8,16,2688]{2,1,0:T(8,128)(2,1)S(1)} %collective-permute-done.6.refs_5_), channel_id=1, source_target_pairs={{0,56},{1,57},{2,58},{3,59},{4,60},{5,61},{6,62},{7,63},{8,0},{9,1... | collective-permute-start | bytes 2064392 | tf_op jit(solution)/shard_map/ppermute | solution.py:323
  90.2 11.6 %collective-permute-start.11 = (bf16[8,16,1792]{2,1,0:T(8,128)(2,1)S(1)}, bf16[8,16,1792]{2,1,0:T(8,128)(2,1)S(1)}, u32[]{:S(2)}, u32[]{:S(2)}) collective-permute-start(bf16[8,16,1792]{2,1,0:T(8,128)(2,1)S(1)} %collective-permute-done.7.refs_2_), channel_id=1, source_target_pairs={{0,8},{1,9},{2,10},{3,11},{4,12},{5,13},{6,14},{7,15},{8,16},{9,17... | collective-permute-start | bytes 1376264 | tf_op jit(solution)/shard_map/ppermute | solution.py:322
  92.1 10.8 %collective-permute-start.12 = (bf16[8,16,1792]{2,1,0:T(8,128)(2,1)S(1)}, bf16[8,16,1792]{2,1,0:T(8,128)(2,1)S(1)}, u32[]{:S(2)}, u32[]{:S(2)}) collective-permute-start(bf16[8,16,1792]{2,1,0:T(8,128)(2,1)S(1)} %collective-permute-done.8.refs_5_), channel_id=1, source_target_pairs={{0,56},{1,57},{2,58},{3,59},{4,60},{5,61},{6,62},{7,63},{8,0},{9,1... | collective-permute-start | bytes 1376264 | tf_op jit(solution)/shard_map/ppermute | solution.py:322
  103.0 15.8 %collective-permute-start.14 = (bf16[8,16,2688]{2,1,0:T(8,128)(2,1)S(1)}, bf16[8,16,2688]{2,1,0:T(8,128)(2,1)S(1)}, u32[]{:S(2)}, u32[]{:S(2)}) collective-permute-start(bf16[8,16,2688]{2,1,0:T(8,128)(2,1)S(1)} %collective-permute-done.10.refs_6_), channel_id=1, source_target_pairs={{0,56},{1,57},{2,58},{3,59},{4,60},{5,61},{6,62},{7,63},{8,0},{9,1... | collective-permute-start | bytes 2064392 | tf_op jit(solution)/shard_map/ppermute | solution.py:329
  108.3 10.4 %collective-permute-start.13 = (bf16[8,16,1792]{2,1,0:T(8,128)(2,1)S(1)}, bf16[8,16,1792]{2,1,0:T(8,128)(2,1)S(1)}, u32[]{:S(2)}, u32[]{:S(2)}) collective-permute-start(bf16[8,16,1792]{2,1,0:T(8,128)(2,1)S(1)} %collective-permute-done.11.refs_3_), channel_id=1, source_target_pairs={{0,8},{1,9},{2,10},{3,11},{4,12},{5,13},{6,14},{7,15},{8,16},{9,17... | collective-permute-start | bytes 1376264 | tf_op jit(solution)/shard_map/ppermute | solution.py:329
  121.7 22.6 %collective-permute-start.16 = (bf16[8,8,16,1536]{3,2,1,0:T(8,128)(2,1)S(1)}, bf16[8,8,16,1536]{3,2,1,0:T(8,128)(2,1)S(1)}, u32[]{:S(2)}, u32[]{:S(2)}) collective-permute-start(bf16[8,8,16,1536]{3,2,1,0:T(8,128)(2,1)S(1)} %get-tuple-element.54.mine), channel_id=1, source_target_pairs={{0,64},{64,0},{128,192},{192,128},{256,320},{320,256},{384,448},{4... | collective-permute-start | bytes 9437192 | tf_op jit(solution)/shard_map/ppermute | solution.py:42
  131.4 7.2 %copy-start.3 = (s32[1,128]{1,0:T(1,128)S(1)}, s32[1,128]{1,0:T(1,128)}, u32[]{:S(2)}) copy-start(s32[1,128]{1,0:T(1,128)} %row_map.1) | copy-start | bytes 1540
  142.3 4.7 %copy-start.1 = (bf16[1,128,2048]{2,1,0:T(8,128)(2,1)S(1)}, bf16[1,128,2048]{2,1,0:T(8,128)(2,1)}, u32[]{:S(2)}) copy-start(bf16[1,128,2048]{2,1,0:T(8,128)(2,1)} %param.15) | copy-start | bytes 1572868
  142.3 4.7 %collective-permute-start.15 = (f32[128,512]{1,0:T(8,128)S(1)}, f32[128,512]{1,0:T(8,128)S(1)}, u32[]{:S(2)}, u32[]{:S(2)}) collective-permute-start(f32[128,512]{1,0:T(8,128)S(1)} %get-tuple-element.53), channel_id=1, source_target_pairs={{0,64},{64,0},{128,192},{192,128},{256,320},{320,256},{384,448},{4... | collective-permute-start | bytes 786440 | tf_op jit(solution)/shard_map/ppermute | solution.py:42

commit v7 on v5

--- a/solution.py
+++ b/solution.py
@@ -139,13 +139,9 @@
     factor[:, WIDTH:] = f2[:ROWS]
     flip = core * ROWS
 
-    def put(r, carry):
+    for r in range(ROWS):
         t = row_map[0, r]
-        t = jnp.where(t >= ROWS, t - flip, t + flip)
-        placed[pl.ds(t, 1), :] = contrib[pl.ds(r, 1), :]
-        return carry
-
-    lax.fori_loop(0, ROWS, put, 0, unroll=8)
+        placed[pl.ds(jnp.where(t >= ROWS, t - flip, t + flip), 1), :] = contrib[r : r + 1, :]
     own[...] = placed[:ROWS]
     sent[...] = placed[ROWS:]
 

time: 128 us -> 127 us (level)
  no operation moved by 1% of the time
where the time goes in v7:
time: 127 us
  starting transfers between devices  58 us (46%)
  blocking collectives  33.1 us (26%)
  waiting for transfers between devices  18.2 us (14%)
  Pallas kernels  16.3 us (13%)
    all_to_all x1, blocking collectives, local(): block = lax.all_to_all(message, AXES, 0, 0, axis_index_groups=lines())  33.1 us
    ppermute x6, starting transfers between devices, local(): a, last = ((up(a[0]), down(a[1])), b)  20.6 us
    ppermute x6, starting transfers between devices, local(): b = (up(b[0]), down(b[1]))  19.5 us
    ppermute x2, starting transfers between devices, swap_cores(): return lax.ppermute(value, 'leaf', [(i, i ^ 1) for i in range(8)])  10.8 us
    ppermute x6, waiting for transfers between devices, local(): b = (up(b[0]), down(b[1]))  10.7 us
    ppermute x1, starting transfers between devices, local(): farthest = down(b[1])  5.27 us
    pallas_call x1, Pallas kernels, local(): call(first_kernel, [SMEM, VMEM] + [ANY] * 8, [((stack, WIDTH), BF16)] * 2...  5.22 us
    ppermute x6, waiting for transfers between devices, local(): a, last = ((up(a[0]), down(a[1])), b)  4.28 us
  transfers between devices with their start and end apart: 16, of which 7 were waited for; matrix products, arithmetic and copies ran while one was open for 0% of the time, Pallas kernels for 9%

profile of v7, /device:TPU:1, one launch (start us, length us, event | category | flops | bytes accessed | tf_op | source)
XLA Modules:
  0.0 126.6 jit_solution(15416694558720713134)
XLA Ops:
  0.6 2.1 %shard_map.104 = bf16[8,16,5632]{2,1,0:T(8,128)(2,1)} custom-call(bf16[1,8,2048]{2,1,0:T(8,128)(2,1)} %links.1, bf16[1,16,1024]{2,1,0:T(8,128)(2,1)} %pivots.1, bf16[1,2,16,1024]{3,2,1,0:T(8,128)(2,1)} %inverse.1, bf16[4,16,1024]{2,1,0:T(8,128)(2,1)} %upper_pivots.1, bf16[4,2,16,1024]{3,2,1,0:T(8,128)(2,1)} %upper_inverse.1), custom_call_target="tpu_custom_call" | custom-call | flops 1000000 | bytes 1000000 | tf_op jit(solution)/shard_map/pallas_call | solution.py:234
  2.7 33.1 %all_to_all.5 = bf16[8,16,5632]{2,1,0:T(8,128)(2,1)S(1)} all-to-all(bf16[8,16,5632]{2,1,0:T(8,128)(2,1)} %shard_map.104), channel_id=1, replica_groups={{0,1,2,3,4,5,6,7},{8,9,10,11,12,13,14,15},{16,17,18,19,20,21,22,23},{24..., dimensions={0} | all-to-all | bytes 2883584 | tf_op jit(solution)/shard_map/all_to_all | solution.py:242
  35.8 0.0 copy-start
  35.8 0.0 copy-start.2
  35.8 0.1 slice.9.refs_0_
  35.9 5.0 %collective-permute-start.3 = (bf16[8,16,3072]{2,1,0:T(8,128)(2,1)S(1)}, bf16[8,16,3072]{2,1,0:T(8,128)(2,1)S(1)}, u32[]{:S(2)}, u32[]{:S(2)}) collective-permute-start(bf16[8,16,3072]{2,1,0:T(8,128)(2,1)S(1)} %slice.9.refs_0_), channel_id=1, source_target_pairs={{0,56},{1,57},{2,58},{3,59},{4,60},{5,61},{6,62},{7,63},{8,0},{9,1... | collective-permute-start | bytes 2359304 | tf_op jit(solution)/shard_map/ppermute | solution.py:249
  40.9 1.9 %collective-permute-start.2 = (bf16[8,16,3072]{2,1,0:T(8,128)(2,1)S(1)}, bf16[8,16,3072]{2,1,0:T(8,128)(2,1)S(1)}, u32[]{:S(2)}, u32[]{:S(2)}) collective-permute-start(bf16[8,16,3072]{2,1,0:T(8,128)(2,1)S(1)} %slice.9.refs_0_), channel_id=1, source_target_pairs={{0,8},{1,9},{2,10},{3,11},{4,12},{5,13},{6,14},{7,15},{8,16},{9,17... | collective-permute-start | bytes 2359304 | tf_op jit(solution)/shard_map/ppermute | solution.py:249
  42.9 4.6 %collective-permute-start.1 = (bf16[8,16,2560]{2,1,0:T(8,128)(2,1)S(1)}, bf16[8,16,2560]{2,1,0:T(8,128)(2,1)S(1)}, u32[]{:S(2)}, u32[]{:S(2)}) collective-permute-start(bf16[8,16,2560]{2,1,0:T(8,128)(2,1)S(1)} %slice.8.refs_0_), channel_id=1, source_target_pairs={{0,56},{1,57},{2,58},{3,59},{4,60},{5,61},{6,62},{7,63},{8,0},{9,1... | collective-permute-start | bytes 1966088 | tf_op jit(solution)/shard_map/ppermute | solution.py:250
  47.5 1.9 %collective-permute-start = (bf16[8,16,2560]{2,1,0:T(8,128)(2,1)S(1)}, bf16[8,16,2560]{2,1,0:T(8,128)(2,1)S(1)}, u32[]{:S(2)}, u32[]{:S(2)}) collective-permute-start(bf16[8,16,2560]{2,1,0:T(8,128)(2,1)S(1)} %slice.8.refs_0_), channel_id=1, source_target_pairs={{0,8},{1,9},{2,10},{3,11},{4,12},{5,13},{6,14},{7,15},{8,16},{9,17... | collective-permute-start | bytes 1966088 | tf_op jit(solution)/shard_map/ppermute | solution.py:250
  49.4 0.4 collective-permute-done.3.refs_4_
  49.8 5.3 %collective-permute-start.7 = (bf16[8,16,3072]{2,1,0:T(8,128)(2,1)S(1)}, bf16[8,16,3072]{2,1,0:T(8,128)(2,1)S(1)}, u32[]{:S(2)}, u32[]{:S(2)}) collective-permute-start(bf16[8,16,3072]{2,1,0:T(8,128)(2,1)S(1)} %collective-permute-done.3.refs_4_), channel_id=1, source_target_pairs={{0,56},{1,57},{2,58},{3,59},{4,60},{5,61},{6,62},{7,63},{8,0},{9,1... | collective-permute-start | bytes 2359304 | tf_op jit(solution)/shard_map/ppermute | solution.py:249
  55.1 0.0 collective-permute-done.2.refs_1_
  55.1 1.9 %collective-permute-start.6 = (bf16[8,16,3072]{2,1,0:T(8,128)(2,1)S(1)}, bf16[8,16,3072]{2,1,0:T(8,128)(2,1)S(1)}, u32[]{:S(2)}, u32[]{:S(2)}) collective-permute-start(bf16[8,16,3072]{2,1,0:T(8,128)(2,1)S(1)} %collective-permute-done.2.refs_1_), channel_id=1, source_target_pairs={{0,8},{1,9},{2,10},{3,11},{4,12},{5,13},{6,14},{7,15},{8,16},{9,17... | collective-permute-start | bytes 2359304 | tf_op jit(solution)/shard_map/ppermute | solution.py:249
  57.1 0.0 collective-permute-done.1.refs_4_
  57.1 5.1 %collective-permute-done.refs_1_ = bf16[8,16,2560]{2,1,0:T(8,128)(2,1)S(1)} collective-permute-done((bf16[8,16,2560]{2,1,0:T(8,128)(2,1)S(1)}, bf16[8,16,2560]{2,1,0:T(8,128)(2,1)S(1)}, u32[]{:S(2)}, u32[]{:S(2)}) %collective-permute-start) | collective-permute-done | bytes 655392 | tf_op jit(solution)/shard_map/ppermute | solution.py:250
  62.2 1.9 %collective-permute-start.4 = (bf16[8,16,2560]{2,1,0:T(8,128)(2,1)S(1)}, bf16[8,16,2560]{2,1,0:T(8,128)(2,1)S(1)}, u32[]{:S(2)}, u32[]{:S(2)}) collective-permute-start(bf16[8,16,2560]{2,1,0:T(8,128)(2,1)S(1)} %collective-permute-done.refs_1_), channel_id=1, source_target_pairs={{0,8},{1,9},{2,10},{3,11},{4,12},{5,13},{6,14},{7,15},{8,16},{9,17... | collective-permute-start | bytes 1966088 | tf_op jit(solution)/shard_map/ppermute | solution.py:250
  64.1 4.6 %collective-permute-start.5 = (bf16[8,16,2560]{2,1,0:T(8,128)(2,1)S(1)}, bf16[8,16,2560]{2,1,0:T(8,128)(2,1)S(1)}, u32[]{:S(2)}, u32[]{:S(2)}) collective-permute-start(bf16[8,16,2560]{2,1,0:T(8,128)(2,1)S(1)} %collective-permute-done.1.refs_4_), channel_id=1, source_target_pairs={{0,56},{1,57},{2,58},{3,59},{4,60},{5,61},{6,62},{7,63},{8,0},{9,1... | collective-permute-start | bytes 1966088 | tf_op jit(solution)/shard_map/ppermute | solution.py:250
  68.7 0.0 collective-permute-done.7.refs_5_
  68.7 1.9 %collective-permute-done.6.refs_2_ = bf16[8,16,3072]{2,1,0:T(8,128)(2,1)S(1)} collective-permute-done((bf16[8,16,3072]{2,1,0:T(8,128)(2,1)S(1)}, bf16[8,16,3072]{2,1,0:T(8,128)(2,1)S(1)}, u32[]{:S(2)}, u32[]{:S(2)}) %collective-permute-start.6) | collective-permute-done | bytes 786464 | tf_op jit(solution)/shard_map/ppermute | solution.py:249
  70.6 1.9 %collective-permute-start.10 = (bf16[8,16,3072]{2,1,0:T(8,128)(2,1)S(1)}, bf16[8,16,3072]{2,1,0:T(8,128)(2,1)S(1)}, u32[]{:S(2)}, u32[]{:S(2)}) collective-permute-start(bf16[8,16,3072]{2,1,0:T(8,128)(2,1)S(1)} %collective-permute-done.6.refs_2_), channel_id=1, source_target_pairs={{0,8},{1,9},{2,10},{3,11},{4,12},{5,13},{6,14},{7,15},{8,16},{9,17... | collective-permute-start | bytes 2359304 | tf_op jit(solution)/shard_map/ppermute | solution.py:249
  72.5 4.6 %collective-permute-start.11 = (bf16[8,16,3072]{2,1,0:T(8,128)(2,1)S(1)}, bf16[8,16,3072]{2,1,0:T(8,128)(2,1)S(1)}, u32[]{:S(2)}, u32[]{:S(2)}) collective-permute-start(bf16[8,16,3072]{2,1,0:T(8,128)(2,1)S(1)} %collective-permute-done.7.refs_5_), channel_id=1, source_target_pairs={{0,56},{1,57},{2,58},{3,59},{4,60},{5,61},{6,62},{7,63},{8,0},{9,1... | collective-permute-start | bytes 2359304 | tf_op jit(solution)/shard_map/ppermute | solution.py:249
  77.1 0.5 collective-permute-done.4.refs_2_
  77.6 0.0 collective-permute-done.5.refs_5_
  77.6 1.9 %collective-permute-start.8 = (bf16[8,16,2560]{2,1,0:T(8,128)(2,1)S(1)}, bf16[8,16,2560]{2,1,0:T(8,128)(2,1)S(1)}, u32[]{:S(2)}, u32[]{:S(2)}) collective-permute-start(bf16[8,16,2560]{2,1,0:T(8,128)(2,1)S(1)} %collective-permute-done.4.refs_2_), channel_id=1, source_target_pairs={{0,8},{1,9},{2,10},{3,11},{4,12},{5,13},{6,14},{7,15},{8,16},{9,17... | collective-permute-start | bytes 1966088 | tf_op jit(solution)/shard_map/ppermute | solution.py:250
  79.5 4.6 %collective-permute-start.9 = (bf16[8,16,2560]{2,1,0:T(8,128)(2,1)S(1)}, bf16[8,16,2560]{2,1,0:T(8,128)(2,1)S(1)}, u32[]{:S(2)}, u32[]{:S(2)}) collective-permute-start(bf16[8,16,2560]{2,1,0:T(8,128)(2,1)S(1)} %collective-permute-done.5.refs_5_), channel_id=1, source_target_pairs={{0,56},{1,57},{2,58},{3,59},{4,60},{5,61},{6,62},{7,63},{8,0},{9,1... | collective-permute-start | bytes 1966088 | tf_op jit(solution)/shard_map/ppermute | solution.py:250
  84.1 1.9 %collective-permute-done.10.refs_3_ = bf16[8,16,3072]{2,1,0:T(8,128)(2,1)S(1)} collective-permute-done((bf16[8,16,3072]{2,1,0:T(8,128)(2,1)S(1)}, bf16[8,16,3072]{2,1,0:T(8,128)(2,1)S(1)}, u32[]{:S(2)}, u32[]{:S(2)}) %collective-permute-start.10) | collective-permute-done | bytes 786464 | tf_op jit(solution)/shard_map/ppermute | solution.py:249
  86.0 0.0 collective-permute-done.11.refs_6_
  86.0 1.9 %collective-permute-start.13 = (bf16[8,16,3072]{2,1,0:T(8,128)(2,1)S(1)}, bf16[8,16,3072]{2,1,0:T(8,128)(2,1)S(1)}, u32[]{:S(2)}, u32[]{:S(2)}) collective-permute-start(bf16[8,16,3072]{2,1,0:T(8,128)(2,1)S(1)} %collective-permute-done.10.refs_3_), channel_id=1, source_target_pairs={{0,8},{1,9},{2,10},{3,11},{4,12},{5,13},{6,14},{7,15},{8,16},{9,17... | collective-permute-start | bytes 2359304 | tf_op jit(solution)/shard_map/ppermute | solution.py:256
  88.0 5.1 %collective-permute-done.8.refs_3_ = bf16[8,16,2560]{2,1,0:T(8,128)(2,1)S(1)} collective-permute-done((bf16[8,16,2560]{2,1,0:T(8,128)(2,1)S(1)}, bf16[8,16,2560]{2,1,0:T(8,128)(2,1)S(1)}, u32[]{:S(2)}, u32[]{:S(2)}) %collective-permute-start.8) | collective-permute-done | bytes 655392 | tf_op jit(solution)/shard_map/ppermute | solution.py:250
  93.1 0.0 collective-permute-done.9.refs_6_
  93.1 5.3 %collective-permute-start.12 = (bf16[8,16,2560]{2,1,0:T(8,128)(2,1)S(1)}, bf16[8,16,2560]{2,1,0:T(8,128)(2,1)S(1)}, u32[]{:S(2)}, u32[]{:S(2)}) collective-permute-start(bf16[8,16,2560]{2,1,0:T(8,128)(2,1)S(1)} %collective-permute-done.9.refs_6_), channel_id=1, source_target_pairs={{0,56},{1,57},{2,58},{3,59},{4,60},{5,61},{6,62},{7,63},{8,0},{9,1... | collective-permute-start | bytes 1966088 | tf_op jit(solution)/shard_map/ppermute | solution.py:257
  98.3 3.1 %collective-permute-done.13.refs_7_ = bf16[8,16,3072]{2,1,0:T(8,128)(2,1)S(1)} collective-permute-done((bf16[8,16,3072]{2,1,0:T(8,128)(2,1)S(1)}, bf16[8,16,3072]{2,1,0:T(8,128)(2,1)S(1)}, u32[]{:S(2)}, u32[]{:S(2)}) %collective-permute-start.13) | collective-permute-done | bytes 786464 | tf_op jit(solution)/shard_map/ppermute | solution.py:256
  101.5 0.0 copy-done
  101.5 0.0 copy-done.2
  101.5 5.2 %shard_map.105 = (bf16[640,1024]{1,0:T(8,128)(2,1)S(1)}, bf16[640,1024]{1,0:T(8,128)(2,1)S(1)}) custom-call(s32[1,1,2]{2,1,0:T(1,128)S(1)} %copy-done.2, bf16[128,2048]{1,0:T(8,128)(2,1)S(1)} %bitcast.4, bf16[8,16,3072]{2,1,0:T(8,128)(2,1)S(1)} %slice.9.refs_0_, bf16[8,16,3072]{2,1,0:T(8,128)(2,1)S(1)} %collective-permute-done.2.refs_1_, ...), custom_call_target="tpu_custom_call" | custom-call | flops 1000 | bytes 1000 | tf_op jit(solution)/shard_map/pallas_call | solution.py:264
  106.7 0.0 collective-permute-done.12.refs_7_
  106.7 0.0 copy-start.3
  106.7 0.7 shard_map.106
  107.4 8.7 %collective-permute-start.15 = (bf16[8,8,16,1536]{3,2,1,0:T(8,128)(2,1)S(1)}, bf16[8,8,16,1536]{3,2,1,0:T(8,128)(2,1)S(1)}, u32[]{:S(2)}, u32[]{:S(2)}) collective-permute-start(bf16[8,8,16,1536]{3,2,1,0:T(8,128)(2,1)S(1)} %get-tuple-element.56.mine), channel_id=1, source_target_pairs={{0,64},{64,0},{128,192},{192,128},{256,320},{320,256},{384,448},{4... | collective-permute-start | bytes 9437192 | tf_op jit(solution)/shard_map/ppermute | solution.py:40
  116.2 0.0 copy-done.3
  116.2 3.3 %shard_map.107 = (bf16[128,2048]{1,0:T(8,128)(2,1)}, f32[128,512]{1,0:T(8,128)S(1)}, f32[128,512]{1,0:T(8,128)S(1)}) custom-call(s32[1,128]{1,0:T(1,128)S(1)} %copy-done.3, bf16[640,1024]{1,0:T(8,128)(2,1)S(1)} %get-tuple-element.48.f1, bf16[640,1024]{1,0:T(8,128)(2,1)S(1)} %get-tuple-element.49.r2, bf16[8,8,16,1024]{3,2,1,0:T(8,128)(2,1)S(1)} %get-tuple-element.52.inv1), custom_call_target="tpu_custom_call" | custom-call | flops 1500000000 | bytes 8388608 | tf_op jit(solution)/shard_map/pallas_call | solution.py:282
  119.5 0.0 copy-start.1
  119.5 2.0 %collective-permute-start.14 = (f32[128,512]{1,0:T(8,128)S(1)}, f32[128,512]{1,0:T(8,128)S(1)}, u32[]{:S(2)}, u32[]{:S(2)}) collective-permute-start(f32[128,512]{1,0:T(8,128)S(1)} %get-tuple-element.55), channel_id=1, source_target_pairs={{0,64},{64,0},{128,192},{192,128},{256,320},{320,256},{384,448},{4... | collective-permute-start | bytes 786440 | tf_op jit(solution)/shard_map/ppermute | solution.py:40
  121.5 0.0 collective-permute-done.15.theirs
  121.5 2.6 %shard_map.108 = (bf16[1024,1024]{1,0:T(8,128)(2,1)S(1)}, bf16[8,8,16,1024]{3,2,1,0:T(8,128)(2,1)S(1)}, bf16[8,8,16,1024]{3,2,1,0:T(8,128)(2,1)S(1)}) custom-call(bf16[8,8,16,1536]{3,2,1,0:T(8,128)(2,1)S(1)} %get-tuple-element.56.mine, bf16[8,8,16,1536]{3,2,1,0:T(8,128)(2,1)S(1)} %collective-permute-done.15.theirs), custom_call_target="tpu_custom_call" | custom-call | flops 1400000000 | bytes 8388608 | tf_op jit(solution)/shard_map/pallas_call | solution.py:291
  124.1 0.0 collective-permute-done.14.received
  124.1 0.0 copy-done.1
  124.2 2.4 %shard_map.109 = bf16[128,2048]{1,0:T(8,128)(2,1)} custom-call(bf16[128,2048]{1,0:T(8,128)(2,1)S(1)} %bitcast.5, f32[128,512]{1,0:T(8,128)S(1)} %get-tuple-element.54.own, f32[128,512]{1,0:T(8,128)S(1)} %collective-permute-done.14.received, bf16[1024,1024]{1,0:T(8,128)(2,1)S(1)} %get-tuple-element.57.p1, ...), custom_call_target="tpu_custom_call" | custom-call | flops 800000000 | bytes 8388608 | tf_op jit(solution)/shard_map/pallas_call | solution.py:298
  (1 shorter events, 0.0 us)
Async XLA Ops:
  35.8 65.7 %copy-start = (bf16[1,128,2048]{2,1,0:T(8,128)(2,1)S(1)}, bf16[1,128,2048]{2,1,0:T(8,128)(2,1)}, u32[]{:S(2)}) copy-start(bf16[1,128,2048]{2,1,0:T(8,128)(2,1)} %param.9) | copy-start | bytes 1572868
  35.8 65.7 %copy-start.2 = (s32[1,1,2]{2,1,0:T(1,128)S(1)}, s32[1,1,2]{2,1,0:T(1,128)}, u32[]{:S(2)}) copy-start(s32[1,1,2]{2,1,0:T(1,128)} %mask.1) | copy-start | bytes 28
  35.9 13.9 %collective-permute-start.3 = (bf16[8,16,3072]{2,1,0:T(8,128)(2,1)S(1)}, bf16[8,16,3072]{2,1,0:T(8,128)(2,1)S(1)}, u32[]{:S(2)}, u32[]{:S(2)}) collective-permute-start(bf16[8,16,3072]{2,1,0:T(8,128)(2,1)S(1)} %slice.9.refs_0_), channel_id=1, source_target_pairs={{0,56},{1,57},{2,58},{3,59},{4,60},{5,61},{6,62},{7,63},{8,0},{9,1... | collective-permute-start | bytes 2359304 | tf_op jit(solution)/shard_map/ppermute | solution.py:249
  40.9 14.2 %collective-permute-start.2 = (bf16[8,16,3072]{2,1,0:T(8,128)(2,1)S(1)}, bf16[8,16,3072]{2,1,0:T(8,128)(2,1)S(1)}, u32[]{:S(2)}, u32[]{:S(2)}) collective-permute-start(bf16[8,16,3072]{2,1,0:T(8,128)(2,1)S(1)} %slice.9.refs_0_), channel_id=1, source_target_pairs={{0,8},{1,9},{2,10},{3,11},{4,12},{5,13},{6,14},{7,15},{8,16},{9,17... | collective-permute-start | bytes 2359304 | tf_op jit(solution)/shard_map/ppermute | solution.py:249
  42.9 14.2 %collective-permute-start.1 = (bf16[8,16,2560]{2,1,0:T(8,128)(2,1)S(1)}, bf16[8,16,2560]{2,1,0:T(8,128)(2,1)S(1)}, u32[]{:S(2)}, u32[]{:S(2)}) collective-permute-start(bf16[8,16,2560]{2,1,0:T(8,128)(2,1)S(1)} %slice.8.refs_0_), channel_id=1, source_target_pairs={{0,56},{1,57},{2,58},{3,59},{4,60},{5,61},{6,62},{7,63},{8,0},{9,1... | collective-permute-start | bytes 1966088 | tf_op jit(solution)/shard_map/ppermute | solution.py:250
  47.5 14.7 %collective-permute-start = (bf16[8,16,2560]{2,1,0:T(8,128)(2,1)S(1)}, bf16[8,16,2560]{2,1,0:T(8,128)(2,1)S(1)}, u32[]{:S(2)}, u32[]{:S(2)}) collective-permute-start(bf16[8,16,2560]{2,1,0:T(8,128)(2,1)S(1)} %slice.8.refs_0_), channel_id=1, source_target_pairs={{0,8},{1,9},{2,10},{3,11},{4,12},{5,13},{6,14},{7,15},{8,16},{9,17... | collective-permute-start | bytes 1966088 | tf_op jit(solution)/shard_map/ppermute | solution.py:250
  49.8 18.8 %collective-permute-start.7 = (bf16[8,16,3072]{2,1,0:T(8,128)(2,1)S(1)}, bf16[8,16,3072]{2,1,0:T(8,128)(2,1)S(1)}, u32[]{:S(2)}, u32[]{:S(2)}) collective-permute-start(bf16[8,16,3072]{2,1,0:T(8,128)(2,1)S(1)} %collective-permute-done.3.refs_4_), channel_id=1, source_target_pairs={{0,56},{1,57},{2,58},{3,59},{4,60},{5,61},{6,62},{7,63},{8,0},{9,1... | collective-permute-start | bytes 2359304 | tf_op jit(solution)/shard_map/ppermute | solution.py:249
  55.1 15.4 %collective-permute-start.6 = (bf16[8,16,3072]{2,1,0:T(8,128)(2,1)S(1)}, bf16[8,16,3072]{2,1,0:T(8,128)(2,1)S(1)}, u32[]{:S(2)}, u32[]{:S(2)}) collective-permute-start(bf16[8,16,3072]{2,1,0:T(8,128)(2,1)S(1)} %collective-permute-done.2.refs_1_), channel_id=1, source_target_pairs={{0,8},{1,9},{2,10},{3,11},{4,12},{5,13},{6,14},{7,15},{8,16},{9,17... | collective-permute-start | bytes 2359304 | tf_op jit(solution)/shard_map/ppermute | solution.py:249
  62.2 15.4 %collective-permute-start.4 = (bf16[8,16,2560]{2,1,0:T(8,128)(2,1)S(1)}, bf16[8,16,2560]{2,1,0:T(8,128)(2,1)S(1)}, u32[]{:S(2)}, u32[]{:S(2)}) collective-permute-start(bf16[8,16,2560]{2,1,0:T(8,128)(2,1)S(1)} %collective-permute-done.refs_1_), channel_id=1, source_target_pairs={{0,8},{1,9},{2,10},{3,11},{4,12},{5,13},{6,14},{7,15},{8,16},{9,17... | collective-permute-start | bytes 1966088 | tf_op jit(solution)/shard_map/ppermute | solution.py:250
  64.1 13.5 %collective-permute-start.5 = (bf16[8,16,2560]{2,1,0:T(8,128)(2,1)S(1)}, bf16[8,16,2560]{2,1,0:T(8,128)(2,1)S(1)}, u32[]{:S(2)}, u32[]{:S(2)}) collective-permute-start(bf16[8,16,2560]{2,1,0:T(8,128)(2,1)S(1)} %collective-permute-done.1.refs_4_), channel_id=1, source_target_pairs={{0,56},{1,57},{2,58},{3,59},{4,60},{5,61},{6,62},{7,63},{8,0},{9,1... | collective-permute-start | bytes 1966088 | tf_op jit(solution)/shard_map/ppermute | solution.py:250
  70.6 15.4 %collective-permute-start.10 = (bf16[8,16,3072]{2,1,0:T(8,128)(2,1)S(1)}, bf16[8,16,3072]{2,1,0:T(8,128)(2,1)S(1)}, u32[]{:S(2)}, u32[]{:S(2)}) collective-permute-start(bf16[8,16,3072]{2,1,0:T(8,128)(2,1)S(1)} %collective-permute-done.6.refs_2_), channel_id=1, source_target_pairs={{0,8},{1,9},{2,10},{3,11},{4,12},{5,13},{6,14},{7,15},{8,16},{9,17... | collective-permute-start | bytes 2359304 | tf_op jit(solution)/shard_map/ppermute | solution.py:249
  72.5 13.5 %collective-permute-start.11 = (bf16[8,16,3072]{2,1,0:T(8,128)(2,1)S(1)}, bf16[8,16,3072]{2,1,0:T(8,128)(2,1)S(1)}, u32[]{:S(2)}, u32[]{:S(2)}) collective-permute-start(bf16[8,16,3072]{2,1,0:T(8,128)(2,1)S(1)} %collective-permute-done.7.refs_5_), channel_id=1, source_target_pairs={{0,56},{1,57},{2,58},{3,59},{4,60},{5,61},{6,62},{7,63},{8,0},{9,1... | collective-permute-start | bytes 2359304 | tf_op jit(solution)/shard_map/ppermute | solution.py:249
  77.6 15.4 %collective-permute-start.8 = (bf16[8,16,2560]{2,1,0:T(8,128)(2,1)S(1)}, bf16[8,16,2560]{2,1,0:T(8,128)(2,1)S(1)}, u32[]{:S(2)}, u32[]{:S(2)}) collective-permute-start(bf16[8,16,2560]{2,1,0:T(8,128)(2,1)S(1)} %collective-permute-done.4.refs_2_), channel_id=1, source_target_pairs={{0,8},{1,9},{2,10},{3,11},{4,12},{5,13},{6,14},{7,15},{8,16},{9,17... | collective-permute-start | bytes 1966088 | tf_op jit(solution)/shard_map/ppermute | solution.py:250
  79.5 13.5 %collective-permute-start.9 = (bf16[8,16,2560]{2,1,0:T(8,128)(2,1)S(1)}, bf16[8,16,2560]{2,1,0:T(8,128)(2,1)S(1)}, u32[]{:S(2)}, u32[]{:S(2)}) collective-permute-start(bf16[8,16,2560]{2,1,0:T(8,128)(2,1)S(1)} %collective-permute-done.5.refs_5_), channel_id=1, source_target_pairs={{0,56},{1,57},{2,58},{3,59},{4,60},{5,61},{6,62},{7,63},{8,0},{9,1... | collective-permute-start | bytes 1966088 | tf_op jit(solution)/shard_map/ppermute | solution.py:250
  86.0 15.4 %collective-permute-start.13 = (bf16[8,16,3072]{2,1,0:T(8,128)(2,1)S(1)}, bf16[8,16,3072]{2,1,0:T(8,128)(2,1)S(1)}, u32[]{:S(2)}, u32[]{:S(2)}) collective-permute-start(bf16[8,16,3072]{2,1,0:T(8,128)(2,1)S(1)} %collective-permute-done.10.refs_3_), channel_id=1, source_target_pairs={{0,8},{1,9},{2,10},{3,11},{4,12},{5,13},{6,14},{7,15},{8,16},{9,17... | collective-permute-start | bytes 2359304 | tf_op jit(solution)/shard_map/ppermute | solution.py:256
  93.1 13.7 %collective-permute-start.12 = (bf16[8,16,2560]{2,1,0:T(8,128)(2,1)S(1)}, bf16[8,16,2560]{2,1,0:T(8,128)(2,1)S(1)}, u32[]{:S(2)}, u32[]{:S(2)}) collective-permute-start(bf16[8,16,2560]{2,1,0:T(8,128)(2,1)S(1)} %collective-permute-done.9.refs_6_), channel_id=1, source_target_pairs={{0,56},{1,57},{2,58},{3,59},{4,60},{5,61},{6,62},{7,63},{8,0},{9,1... | collective-permute-start | bytes 1966088 | tf_op jit(solution)/shard_map/ppermute | solution.py:257
  106.7 9.4 %copy-start.3 = (s32[1,128]{1,0:T(1,128)S(1)}, s32[1,128]{1,0:T(1,128)}, u32[]{:S(2)}) copy-start(s32[1,128]{1,0:T(1,128)} %row_map.1) | copy-start | bytes 1540
  107.4 14.1 %collective-permute-start.15 = (bf16[8,8,16,1536]{3,2,1,0:T(8,128)(2,1)S(1)}, bf16[8,8,16,1536]{3,2,1,0:T(8,128)(2,1)S(1)}, u32[]{:S(2)}, u32[]{:S(2)}) collective-permute-start(bf16[8,8,16,1536]{3,2,1,0:T(8,128)(2,1)S(1)} %get-tuple-element.56.mine), channel_id=1, source_target_pairs={{0,64},{64,0},{128,192},{192,128},{256,320},{320,256},{384,448},{4... | collective-permute-start | bytes 9437192 | tf_op jit(solution)/shard_map/ppermute | solution.py:40
  119.5 4.7 %copy-start.1 = (bf16[1,128,2048]{2,1,0:T(8,128)(2,1)S(1)}, bf16[1,128,2048]{2,1,0:T(8,128)(2,1)}, u32[]{:S(2)}) copy-start(bf16[1,128,2048]{2,1,0:T(8,128)(2,1)} %param.15) | copy-start | bytes 1572868
  119.5 4.7 %collective-permute-start.14 = (f32[128,512]{1,0:T(8,128)S(1)}, f32[128,512]{1,0:T(8,128)S(1)}, u32[]{:S(2)}, u32[]{:S(2)}) collective-permute-start(f32[128,512]{1,0:T(8,128)S(1)} %get-tuple-element.55), channel_id=1, source_target_pairs={{0,64},{64,0},{128,192},{192,128},{256,320},{320,256},{384,448},{4... | collective-permute-start | bytes 786440 | tf_op jit(solution)/shard_map/ppermute | solution.py:40
